TPU v7x, 32 devices: a whole 2x2x4 slice. The times are simulated.
32 devices in a mesh: dp: 8 (over z, y), tensor: 4 (over x, core).
Axes of the slice: x: 2, y: 2, z: 4, core: 2. Of those that a mesh axis runs over, the one named last changes fastest.
Arguments:
- tokens: bfloat16 [8192, 2048], P(('dp', 'tensor')), may hold values from -6 to 6
- segment_ids: int32 [8, 1024], P('dp'), may hold values from 0 to 34, as said below
- mixer_in: bfloat16 [2048, 4, 2048], P('dp', None, 'tensor'), may hold values from -0.125 to 0.125
- mixer_out: bfloat16 [2048, 2048], P('tensor', 'dp'), may hold values from -0.25 to 0.25
- gate_up: bfloat16 [2048, 2, 5632], P('dp', None, 'tensor'), may hold values from -0.125 to 0.125
- down: bfloat16 [5632, 2048], P('tensor', 'dp'), may hold values from -0.15625 to 0.15625
- norm_gain: bfloat16 [2048], P('dp'), may hold values from 0.25 to 1.75
- group_gain: bfloat16 [128], P('dp'), may hold values from 0.25 to 1.75
- ffn_gain: bfloat16 [2048], P('dp'), may hold values from 0.25 to 1.75
- cotangent: bfloat16 [8192, 2048], P(('dp', 'tensor')), may hold values from -6 to 6
Outputs:
- output: bfloat16 [8192, 2048], P(('dp', 'tensor'))
- d_tokens: bfloat16 [8192, 2048], P(('dp', 'tensor'))
- d_mixer_in: float32 [2048, 4, 2048], P('dp', None, 'tensor')
- d_mixer_out: float32 [2048, 2048], P('tensor', 'dp')
- d_gate_up: float32 [2048, 2, 5632], P('dp', None, 'tensor')
- d_down: float32 [5632, 2048], P('tensor', 'dp')
- d_norm_gain: float32 [2048], P('dp')
- d_group_gain: float32 [128], P('dp')
- d_ffn_gain: float32 [2048], P('dp')
Inputs may be any that keep to these rules, and one draw needn't show every extreme that they name: `segment_ids`: each row counts documents from 0 upward and never falls, and holds exactly 35 documents; one of them begins before position 128 and ends at position 896 or later, and the rest are short.
All inputs are finite; a program needn't handle non-finite values.
Results may differ from a plain program's by a relative error of at most 0.023.
The roundings to bfloat16 on the way count: a program that leaves them out, or rounds other values in their place, can miss the bound.
Values may be sent and summed in bfloat16 or wider, within the bound.
No kernel may reach another device: no remote copies, remote signals or barrier semaphores. Data moves between devices by JAX's collectives and lax.ppermute only.
A program may use at most 256 MiB of HBM per device.

v0:
```python
import jax
import jax.numpy as jnp
from jax import lax
from jax.sharding import PartitionSpec as P

HD = 128
SPAN = 64


EPSILON = 1e-06
GROUP_EPSILON = 0.01
FORGET_FLOOR = 0.8
HIGHEST = lax.Precision.HIGHEST
CONTRACT_LAST = (((1,), (1,)), ((), ()))
CONTRACT_FIRST = (((0,), (0,)), ((), ()))


def rms_norm(values, gain, offset=EPSILON):
    return values * lax.rsqrt(jnp.mean(values * values, axis=-1, keepdims=True) + offset) * gain


def mixer_core(query, forget_raw, inputs, out_gate, group_weight, doc_ids):
    length = query.shape[0]
    width = query.shape[1]
    heads = width // HD
    blocks = length // SPAN
    forget = FORGET_FLOOR + (1.0 - FORGET_FLOOR) * jax.nn.sigmoid(forget_raw)
    decay_logs = jnp.log(forget)
    key_rows = 1.0 - forget

    def split_blocks(array):
        return array.reshape(blocks, SPAN, heads, HD)

    cumulative = jnp.cumsum(split_blocks(decay_logs), axis=1)
    doc_blocks = doc_ids.reshape(blocks, SPAN)
    causal = jnp.arange(SPAN)[:, None] >= jnp.arange(SPAN)[None, :]

    def block_step(carry, item):
        memory, last_doc = carry
        query_block, key_block, input_block, cum_block, doc_block = item
        query_decay = query_block * jnp.exp(cum_block)
        key_decay = key_block * jnp.exp(-cum_block)
        scores = jnp.einsum("thc,shc->hts", query_decay, key_decay, precision=HIGHEST)
        same_doc = jnp.logical_and(causal, doc_block[:, None] == doc_block[None, :])
        scores = jnp.where(same_doc[None], scores, 0.0)
        within = jnp.einsum("hts,she->the", scores, input_block, precision=HIGHEST)
        continued = (doc_block == last_doc).astype(jnp.float32)
        earlier = (
            jnp.einsum("thc,hce->the", query_decay, memory, precision=HIGHEST)
            * continued[:, None, None]
        )
        total_decay = cum_block[-1]
        end_doc = doc_block[-1]
        tail_rows = (doc_block == end_doc).astype(jnp.float32)
        key_tail = key_block * jnp.exp(total_decay[None] - cum_block) * tail_rows[:, None, None]
        kept_memory = (
            memory * jnp.exp(total_decay)[:, :, None] * (end_doc == last_doc).astype(jnp.float32)
        )
        memory = kept_memory + jnp.einsum("shc,she->hce", key_tail, input_block, precision=HIGHEST)
        return ((memory, end_doc), within + earlier)

    initial = (jnp.zeros((heads, HD, HD), jnp.float32), jnp.array(-1, jnp.int32))
    _, mixed = lax.scan(
        jax.checkpoint(block_step),
        initial,
        (split_blocks(query), split_blocks(key_rows), split_blocks(inputs), cumulative, doc_blocks),
    )
    mixed = mixed.reshape(length, heads, HD)
    normed = rms_norm(mixed, group_weight, GROUP_EPSILON)
    gate_heads = out_gate.reshape(length, heads, HD)
    return (normed * jax.nn.silu(gate_heads)).reshape(length, width)


def body(
    tokens,
    segment_ids,
    mixer_in,
    mixer_out,
    gate_up,
    down,
    norm_gain,
    group_gain,
    ffn_gain,
    cotangent,
):
    doc_ids = segment_ids[0]
    inputs_wide = tokens.astype(jnp.float32)
    w_in, w_out, gain_in, gain_group = (
        lax.all_gather(mixer_in, "dp", axis=0, tiled=True),
        lax.all_gather(mixer_out, "dp", axis=1, tiled=True),
        lax.all_gather(norm_gain, "dp", axis=0, tiled=True),
        lax.all_gather(group_gain, "dp", axis=0, tiled=True),
    )
    width = w_out.shape[0]
    model_width = w_out.shape[1]
    w_in_flat = w_in.reshape(model_width, 4 * width)
    normed_in, norm_in_back = jax.vjp(rms_norm, inputs_wide, gain_in.astype(jnp.float32))
    seq_normed = lax.all_gather(normed_in.astype(jnp.bfloat16), "tensor", axis=0, tiled=True)
    projected = jnp.dot(seq_normed, w_in_flat, preferred_element_type=jnp.float32).astype(
        jnp.bfloat16
    )
    proj_parts = [
        projected[:, column_group * width : (column_group + 1) * width].astype(jnp.float32)
        for column_group in range(4)
    ]

    def core_apply(query, forget_raw, inputs, out_gate, group_weight):
        return mixer_core(query, forget_raw, inputs, out_gate, group_weight, doc_ids)

    mixed, core_back = jax.vjp(
        core_apply,
        proj_parts[0],
        proj_parts[1],
        proj_parts[2],
        proj_parts[3],
        gain_group.astype(jnp.float32),
    )
    mixed_low = mixed.astype(jnp.bfloat16)
    rows_block = mixed_low
    attention = lax.psum_scatter(
        jnp.dot(rows_block, w_out, preferred_element_type=jnp.float32).astype(jnp.bfloat16),
        "tensor",
        scatter_dimension=0,
        tiled=True,
    ).astype(jnp.float32)
    resid = inputs_wide + attention
    w_gu, w_down, gain_ffn = (
        lax.all_gather(gate_up, "dp", axis=0, tiled=True),
        lax.all_gather(down, "dp", axis=1, tiled=True),
        lax.all_gather(ffn_gain, "dp", axis=0, tiled=True),
    )
    hidden_width = w_down.shape[0]
    w_gu_flat = w_gu.reshape(model_width, 2 * hidden_width)
    normed_ffn, norm_ffn_back = jax.vjp(rms_norm, resid, gain_ffn.astype(jnp.float32))
    seq_ffn = lax.all_gather(normed_ffn.astype(jnp.bfloat16), "tensor", axis=0, tiled=True)
    gate_up_vals = jnp.dot(seq_ffn, w_gu_flat, preferred_element_type=jnp.float32)
    gate_vals = gate_up_vals[:, :hidden_width]
    up_vals = gate_up_vals[:, hidden_width:]
    sigma = jax.nn.sigmoid(gate_vals)
    swish = gate_vals * sigma
    hidden = (swish * up_vals).astype(jnp.bfloat16)
    rows_block = hidden
    ffn_out = lax.psum_scatter(
        jnp.dot(rows_block, w_down, preferred_element_type=jnp.float32).astype(jnp.bfloat16),
        "tensor",
        scatter_dimension=0,
        tiled=True,
    ).astype(jnp.float32)
    output = (resid + ffn_out).astype(jnp.bfloat16)
    w_gu, w_down = (
        lax.all_gather(gate_up, "dp", axis=0, tiled=True),
        lax.all_gather(down, "dp", axis=1, tiled=True),
    )
    w_gu_flat = w_gu.reshape(model_width, 2 * hidden_width)
    seq_cot = lax.all_gather(cotangent, "tensor", axis=0, tiled=True)
    d_hidden = lax.dot_general(seq_cot, w_down, CONTRACT_LAST, preferred_element_type=jnp.float32)
    d_gate = (d_hidden * up_vals * sigma * (1.0 + gate_vals * (1.0 - sigma))).astype(jnp.bfloat16)
    d_up = (d_hidden * swish).astype(jnp.bfloat16)
    d_gate_rows = jnp.concatenate([d_gate, d_up], axis=1)
    grad_gate_up = lax.dot_general(
        seq_ffn, d_gate_rows, CONTRACT_FIRST, preferred_element_type=jnp.float32
    ).reshape(model_width, 2, hidden_width)
    rows_block = d_gate_rows
    d_normed_ffn = lax.psum_scatter(
        lax.dot_general(
            rows_block, w_gu_flat, CONTRACT_LAST, preferred_element_type=jnp.float32
        ).astype(jnp.bfloat16),
        "tensor",
        scatter_dimension=0,
        tiled=True,
    ).astype(jnp.float32)
    d_resid_norm, grad_gain_ffn = norm_ffn_back(d_normed_ffn)
    d_resid = cotangent.astype(jnp.float32) + d_resid_norm
    w_in, w_out = (
        lax.all_gather(mixer_in, "dp", axis=0, tiled=True),
        lax.all_gather(mixer_out, "dp", axis=1, tiled=True),
    )
    w_in_flat = w_in.reshape(model_width, 4 * width)
    seq_d_attn = lax.all_gather(d_resid.astype(jnp.bfloat16), "tensor", axis=0, tiled=True)
    d_mixed = lax.dot_general(seq_d_attn, w_out, CONTRACT_LAST, preferred_element_type=jnp.float32)
    grad_out = lax.dot_general(
        mixed_low, seq_d_attn, CONTRACT_FIRST, preferred_element_type=jnp.float32
    )
    core_grads = core_back(d_mixed)
    d_projected = jnp.concatenate(
        [core_grads[0], core_grads[1], core_grads[2], core_grads[3]], axis=1
    ).astype(jnp.bfloat16)
    grad_group = core_grads[4]
    grad_in = lax.dot_general(
        seq_normed, d_projected, CONTRACT_FIRST, preferred_element_type=jnp.float32
    ).reshape(model_width, 4, width)
    rows_block = d_projected
    d_normed_in = lax.psum_scatter(
        lax.dot_general(
            rows_block, w_in_flat, CONTRACT_LAST, preferred_element_type=jnp.float32
        ).astype(jnp.bfloat16),
        "tensor",
        scatter_dimension=0,
        tiled=True,
    ).astype(jnp.float32)
    d_inputs_norm, grad_gain_in = norm_in_back(d_normed_in)
    d_tokens = (d_resid + d_inputs_norm).astype(jnp.bfloat16)
    grad_down = lax.dot_general(hidden, seq_cot, CONTRACT_FIRST, preferred_element_type=jnp.float32)
    share_in, share_out, share_gate_up, share_down, share_gain_in, share_group, share_gain_ffn = (
        lax.psum_scatter(
            grad_in.astype(jnp.bfloat16), "dp", scatter_dimension=0, tiled=True
        ).astype(jnp.float32),
        lax.psum_scatter(
            grad_out.astype(jnp.bfloat16), "dp", scatter_dimension=1, tiled=True
        ).astype(jnp.float32),
        lax.psum_scatter(
            grad_gate_up.astype(jnp.bfloat16), "dp", scatter_dimension=0, tiled=True
        ).astype(jnp.float32),
        lax.psum_scatter(
            grad_down.astype(jnp.bfloat16), "dp", scatter_dimension=1, tiled=True
        ).astype(jnp.float32),
        lax.psum_scatter(
            grad_gain_in.astype(jnp.bfloat16), "dp", scatter_dimension=0, tiled=True
        ).astype(jnp.float32),
        lax.psum_scatter(
            grad_group.astype(jnp.bfloat16), "dp", scatter_dimension=0, tiled=True
        ).astype(jnp.float32),
        lax.psum_scatter(
            grad_gain_ffn.astype(jnp.bfloat16), "dp", scatter_dimension=0, tiled=True
        ).astype(jnp.float32),
    )
    total_gain_in, total_group, total_gain_ffn = lax.psum(
        (share_gain_in, share_group, share_gain_ffn), "tensor"
    )
    return (
        output,
        d_tokens,
        share_in,
        share_out,
        share_gate_up,
        share_down,
        total_gain_in,
        total_group,
        total_gain_ffn,
    )


def solution(mesh):
    placed = (
        P(("dp", "tensor"), None),
        P("dp", None),
        P("dp", None, "tensor"),
        P("tensor", "dp"),
        P("dp", None, "tensor"),
        P("tensor", "dp"),
        P("dp"),
        P("dp"),
        P("dp"),
        P(("dp", "tensor"), None),
    )
    return jax.shard_map(
        body,
        mesh=mesh,
        in_specs=placed,
        out_specs=(
            P(("dp", "tensor"), None),
            P(("dp", "tensor"), None),
            P("dp", None, "tensor"),
            P("tensor", "dp"),
            P("dp", None, "tensor"),
            P("tensor", "dp"),
            P("dp"),
            P("dp"),
            P("dp"),
        ),
        check_vma=False,
    )
```

profile of v0, /device:TPU:0, one launch (start us, length us, event | category | flops | bytes accessed | tf_op | source)
XLA Modules:
  0.0 2021.5 jit_solution(6900306967754589369)
XLA Ops:
  8.6 22.4 %all-gather = bf16[8,1,256]{2,1,0:T(2,128)(2,1)S(1)} all-gather(bf16[1,1,256]{2,1,0:T(2,128)(2,1)S(1)} %reshape.285), channel_id=1, replica_groups=mesh['dp'=8,'tensor'=4] {'dp'}, dimensions={0}, use_global_device_ids=true | all-gather | bytes 4608 | tf_op jit(solution)/shard_map/all_gather | solution.py:91
  39.3 17.6 all-reduce.1
  56.9 81.2 %all-gather.13.cloned.1.call-done = bf16[2048,4,512]{2,1,0:T(4,128)(2,1)} async-done(((bf16[256,4,512]{2,1,0:T(4,128)(2,1)}), bf16[2048,4,512]{2,1,0:T(4,128)(2,1)}) %all-gather.13.cloned.1.call-update) | async-done | bytes 8388624 | tf_op jit(solution)/shard_map/all_gather | solution.py:89
  138.1 10.8 copy.144
  148.9 24.1 %all-gather.11.cloned.1.call-done = bf16[1024,2048]{1,0:T(8,128)(2,1)} async-done(((bf16[256,2048]{1,0:T(8,128)(2,1)}), bf16[1024,2048]{1,0:T(8,128)(2,1)}) %all-gather.11.cloned.1.call-update) | async-done | bytes 4194320 | tf_op jit(solution)/shard_map/all_gather | solution.py:98
  172.9 12.5 convolution_convert_fusion.7
  215.6 191.4 %while.43 = (s32[]{:T(128)}, f32[4,128,128]{2,1,0:T(8,128)S(1)}, s32[]{:T(128)}, f32[16,64,4,128]{3,1,2,0:T(8,128)S(1)}, f32[16,4,128,128]{3,2,1,0:T(8,128)}, /*...) while((s32[]{:T(128)}, f32[4,128,128]{2,1,0:T(8,128)S(1)}, ...), condition=%wide.region_3.4_spmd.clone, body=%wide.region_2.3_spmd.clone.sunk | while | flops 151712000 | bytes 3172831 | solution.py:63
  425.1 20.6 %all-gather.1 = bf16[8,1,256]{2,1,0:T(2,128)(2,1)S(1)} all-gather(bf16[1,1,256]{2,1,0:T(2,128)(2,1)S(1)} %reshape.287), channel_id=1, replica_groups=mesh['dp'=8,'tensor'=4] {'dp'}, dimensions={0}, use_global_device_ids=true | all-gather | bytes 4608 | tf_op jit(solution)/shard_map/all_gather | solution.py:130
  445.7 23.5 %reduce-scatter.7.cloned.1.call-done = bf16[256,2048]{1,0:T(8,128)(2,1)} async-done(((bf16[1024,2048]{1,0:T(8,128)(2,1)}), bf16[256,2048]{1,0:T(8,128)(2,1)}) %reduce-scatter.7.cloned.1.call-update) | async-done | bytes 1048592 | tf_op jit(solution)/shard_map/reduce_scatter | solution.py:120
  474.0 161.1 %all-gather.19.cloned.1.call-done = bf16[2048,2,1408]{2,1,0:T(2,128)(2,1)} async-done(((bf16[256,2,1408]{2,1,0:T(2,128)(2,1)}), bf16[2048,2,1408]{2,1,0:T(2,128)(2,1)}) %all-gather.19.cloned.1.call-update) | async-done | bytes 11534352 | tf_op jit(solution)/shard_map/all_gather | solution.py:128
  635.1 12.0 copy.147
  647.2 22.7 %all-gather.17.cloned.1.call-done = bf16[1024,2048]{1,0:T(8,128)(2,1)} async-done(((bf16[256,2048]{1,0:T(8,128)(2,1)}), bf16[1024,2048]{1,0:T(8,128)(2,1)}) %all-gather.17.cloned.1.call-update) | async-done | bytes 4194320 | tf_op jit(solution)/shard_map/all_gather | solution.py:135
  669.9 18.7 fusion.99
  688.6 17.5 all-gather.23.cloned.1.call-done
  706.0 95.9 %all-gather.21.cloned.1.call-done = bf16[1408,2048]{1,0:T(8,128)(2,1)} async-done(((bf16[1408,256]{1,0:T(8,128)(2,1)}), bf16[1408,2048]{1,0:T(8,128)(2,1)}) %all-gather.21.cloned.1.call-update) | async-done | bytes 5767184 | tf_op jit(solution)/shard_map/all_gather | solution.py:129
  801.9 16.3 multiply_convert_fusion.1
  820.7 16.3 convolution_convert_fusion.3
  837.2 42.6 %reduce-scatter.11.cloned.1.call-done = bf16[256,2048]{1,0:T(8,128)(2,1)} async-done(((bf16[1024,2048]{1,0:T(8,128)(2,1)}), bf16[256,2048]{1,0:T(8,128)(2,1)}) %reduce-scatter.11.cloned.1.call-update) | async-done | bytes 1048592 | tf_op jit(solution)/shard_map/reduce_scatter | solution.py:164
  885.2 10.5 convolution_convert_fusion.1
  900.9 18.9 all-gather.25.cloned.1.call-done
  929.2 6.6 multiply_reduce_fusion.1
  953.2 309.9 %while.44 = (s32[]{:T(128)}, f32[4,128,128]{2,1,0:T(8,128)S(1)}, bf16[16,64,4,128]{3,1,2,0:T(8,128)(2,1)S(1)}, f32[16,64,4,128]{3,1,2,0:T(8,128)}, bf16[16,64,4,...) while((s32[]{:T(128)}, f32[4,128,128]{2,1,0:T(8,128)S(1)}, ...), condition=%wide.region_14.15_spmd.clone, body=%wide.region_11.14_spmd.clone.sunk | while | flops 328904960 | bytes 10279685 | solution.py:63
  1266.9 25.9 %fusion.98 = f32[16,64,4,128]{3,0,1,2:T(8,128)S(1)} fusion(f32[16,64,4,128]{3,0,1,2:T(8,128)S(1)} %copy-done.16), kind=kOutput, calls=%fused_computation.193 | output fusion | flops 33030144 | bytes 4194304 | tf_op jit(solution)/shard_map/transpose(jvp(jit(cumsum)))/reduce_window_sum | solution.py:34
  1300.4 12.4 convolution_convert_fusion.4
  1312.8 10.9 convolution_convert_fusion.5
  1323.9 18.3 convolution_convert_fusion
  1342.2 22.7 %convert_element_type.207 = bf16[2048,2,1408]{2,1,0:T(2,128)(2,1)} reshape(bf16[2048,2816]{1,0:T(8,128)(2,1)} %convolution_convert_fusion) | data formatting | bytes 23068672 | tf_op jit(solution)/shard_map/convert_element_type | solution.py:212
  1364.9 13.8 convolution_convert_fusion.2
  1378.7 14.8 copy.124
  1401.6 22.7 %all-reduce.8 = (bf16[2048]{0:T(1024)(128)(2,1)S(1)}, bf16[128]{0:T(256)(128)(2,1)S(1)}, bf16[2048]{0:T(1024)(128)(2,1)S(1)}) all-reduce(bf16[2048]{0:T(1024)(128)(2,1)S(1)} %get-tuple-element.626, bf16[128]{0:T(256)(128)(2,1)S(1)} %copy-done.37, bf16[2048]{0:T(1024)(128)(2,1)S(1)} %copy-done.27), channel_id=10, replica_groups=mesh['dp'=8,'tensor'=4] {'dp'}, use_global_device_ids=true, to_apply=%region_23.24.clone | all-reduce | flops 4224 | bytes 16896
  1424.5 6.6 all-reduce.7
  1436.0 572.0 %all-reduce.12.cloned.1.call-done = (bf16[2048,4,512]{2,1,0:T(4,128)(2,1)}, bf16[2048,2,1408]{2,1,0:T(2,128)(2,1)}) async-done(((bf16[2048,4,512]{2,1,0:T(4,128)(2,1)}, bf16[2048,2,1408]{2,1,0:T(2,128)(2,1)}), (bf16[2048,4,512]{2,1,0:T(4,128)(2,1)}, bf16[2048,2,1408]{2,1,0:T(2,128)(2,1)})) %all-reduce.12.cloned.1.call-update) | async-done | bytes 19922960
  (823 shorter events, 588.0 us)
Async XLA Ops:
  7.2 26.5 %copy-start = (bf16[256,2048]{1,0:T(8,128)(2,1)S(1)}, bf16[256,2048]{1,0:T(8,128)(2,1)}, u32[]{:S(2)}) copy-start(bf16[256,2048]{1,0:T(8,128)(2,1)} %param.14) | copy-start | bytes 3145732
  7.2 130.9 %all-gather.13.cloned.1.call-start = ((), (), s32[]{:S(2)}) async-start(), calls=%async_computation.7 | async-start | bytes 9437184 | tf_op jit(solution)/shard_map/all_gather | solution.py:89
  7.9 165.0 %all-gather.11.cloned.1.call-start = ((), (), s32[]{:S(2)}) async-start(), calls=%async_computation.6 | async-start | bytes 5242880 | tf_op jit(solution)/shard_map/all_gather | solution.py:98
  31.0 6.7 copy-start.38
  31.0 8.0 copy-start.39
  35.0 383.2 %all-gather.15.cloned.1.call-start = ((), (), s32[]{:S(2)}) async-start(), calls=%async_computation.8 | async-start | bytes 2359296 | tf_op jit(solution)/shard_map/all_gather | solution.py:90
  35.8 433.4 %reduce-scatter.7.cloned.1.call-start = ((), (), s32[]{:S(2)}) async-start(), calls=%async_computation.9 | async-start | bytes 5242880 | tf_op jit(solution)/shard_map/reduce_scatter | solution.py:120
  56.9 92.0 %copy-start.34 = (f32[128]{0:T(128)}, f32[128]{0:T(128)S(1)}, u32[]{:S(2)}) copy-start(f32[128]{0:T(128)S(1)} %convert_element_type.181) | copy-start | bytes 1540
  56.9 357.0 %copy-start.25 = (f32[512]{0:T(512)}, f32[512]{0:T(512)S(1)}, u32[]{:S(2)}) copy-start(f32[512]{0:T(512)S(1)} %broadcast_bitcast_fusion) | copy-start | bytes 6148
  424.4 210.7 %all-gather.19.cloned.1.call-start = ((), (), s32[]{:S(2)}) async-start(), calls=%async_computation.11 | async-start | bytes 12976128 | tf_op jit(solution)/shard_map/all_gather | solution.py:128
  425.0 244.8 %all-gather.17.cloned.1.call-start = ((), (), s32[]{:S(2)}) async-start(), calls=%async_computation.10 | async-start | bytes 5242880 | tf_op jit(solution)/shard_map/all_gather | solution.py:135
  470.9 412.2 %copy-start.23 = (f32[256]{0:T(256)}, f32[256]{0:T(256)S(1)}, u32[]{:S(2)}) copy-start(f32[256]{0:T(256)S(1)} %fusion.89) | copy-start | bytes 3076
  472.4 233.6 %all-gather.23.cloned.1.call-start = ((), (), s32[]{:S(2)}) async-start(), calls=%async_computation.14 | async-start | bytes 5242880 | tf_op jit(solution)/shard_map/all_gather | solution.py:155
  473.2 328.7 %all-gather.21.cloned.1.call-start = ((), (), s32[]{:S(2)}) async-start(), calls=%async_computation.12 | async-start | bytes 6488064 | tf_op jit(solution)/shard_map/all_gather | solution.py:129
  473.9 405.9 %reduce-scatter.11.cloned.1.call-start = ((), (), s32[]{:S(2)}) async-start(), calls=%async_computation.15 | async-start | bytes 5242880 | tf_op jit(solution)/shard_map/reduce_scatter | solution.py:164
  837.0 82.8 %all-gather.25.cloned.1.call-start = ((), (), s32[]{:S(2)}) async-start(), calls=%async_computation.16 | async-start | bytes 5242880 | tf_op jit(solution)/shard_map/all_gather | solution.py:179
  885.2 509.9 %reduce-scatter.17.cloned.1.call-start = ((), (), s32[]{:S(2)}) async-start(), calls=%async_computation.19 | async-start | bytes 6488064 | tf_op jit(solution)/shard_map/reduce_scatter | solution.py:214
  895.7 501.8 %reduce-scatter.15.cloned.1.call-start = ((), (), s32[]{:S(2)}) async-start(), calls=%async_computation.18 | async-start | bytes 2359296 | tf_op jit(solution)/shard_map/reduce_scatter | solution.py:208
  949.6 449.6 %reduce-scatter.13.cloned.1.call-start = ((), (), s32[]{:S(2)}) async-start(), calls=%async_computation.17 | async-start | bytes 5242880 | tf_op jit(solution)/shard_map/reduce_scatter | solution.py:193
  1265.5 34.9 %slice-start = ((s8[8388608]{0:T(1024)(128)(4,1)}), s8[4194304]{0:T(1024)(128)(4,1)S(1)}, s32[]{:S(2)}) async-start(s8[8388608]{0:T(1024)(128)(4,1)} %bitcast.297), calls=%async_computation.21 | async-start | bytes 8388608
  1266.9 29.0 %copy-start.17 = (f32[1024,512]{1,0:T(8,128)S(1)}, f32[1024,512]{1,0:T(8,128)}, u32[]{:S(2)}) copy-start(f32[1024,512]{1,0:T(8,128)} %fusion.100) | copy-start | bytes 6291460
  1266.9 29.0 %copy-start.26 = (f32[512]{0:T(512)S(1)}, f32[512]{0:T(512)}, u32[]{:S(2)}) copy-start(f32[512]{0:T(512)} %copy-done.25) | copy-start | bytes 6148
  1312.8 118.3 %reduce-scatter.9.cloned.1.call-start = ((), (), s32[]{:S(2)}) async-start(), calls=%async_computation.13 | async-start | bytes 5242880 | tf_op jit(solution)/shard_map/reduce_scatter | solution.py:143
  1323.8 684.2 %all-reduce.12.cloned.1.call-start = ((), (), s32[]{:S(2)}) async-start(), calls=%async_computation.20 | async-start | bytes 39845888
  1342.2 22.7 %copy-start.19 = (bf16[1024,512]{1,0:T(8,128)(2,1)S(1)}, bf16[1024,512]{1,0:T(8,128)(2,1)}, u32[]{:S(2)}) copy-start(bf16[1024,512]{1,0:T(8,128)(2,1)} %get-tuple-element.716) | copy-start | bytes 3145732
  1342.2 22.7 %copy-start.20 = (bf16[1024,512]{1,0:T(8,128)(2,1)S(1)}, bf16[1024,512]{1,0:T(8,128)(2,1)}, u32[]{:S(2)}) copy-start(bf16[1024,512]{1,0:T(8,128)(2,1)} %get-tuple-element.717) | copy-start | bytes 3145732
  1394.9 6.6 copy-start.27
  1395.0 36.1 %copy-start.31 = (f32[256]{0:T(256)S(1)}, f32[256]{0:T(256)}, u32[]{:S(2)}) copy-start(f32[256]{0:T(256)} %copy-done.30) | copy-start | bytes 3076
  1395.0 36.2 %copy-start.3 = (bf16[256,2048]{1,0:T(8,128)(2,1)S(1)}, bf16[256,2048]{1,0:T(8,128)(2,1)}, u32[]{:S(2)}) copy-start(bf16[256,2048]{1,0:T(8,128)(2,1)} %reduce-scatter.7.cloned.1.call-done) | copy-start | bytes 3145732
  1395.0 36.2 %copy-start.13 = (bf16[256,2048]{1,0:T(8,128)(2,1)S(1)}, bf16[256,2048]{1,0:T(8,128)(2,1)}, u32[]{:S(2)}) copy-start(bf16[256,2048]{1,0:T(8,128)(2,1)} %param.23) | copy-start | bytes 3145732
  1395.0 36.2 %copy-start.24 = (f32[256]{0:T(256)S(1)}, f32[256]{0:T(256)}, u32[]{:S(2)}) copy-start(f32[256]{0:T(256)} %copy-done.23) | copy-start | bytes 3076
  1395.0 36.2 %copy-start.33 = (f32[256]{0:T(256)S(1)}, f32[256]{0:T(256)}, u32[]{:S(2)}) copy-start(f32[256]{0:T(256)} %copy-done.32) | copy-start | bytes 3076
  (28 other events, 80.6 us)
Sparse Core Ops, SparseCore 0:
  10.1 127.9 all-gather.12
  140.3 32.6 all-gather.10
  175.0 51.0 all-gather.14
  424.6 44.5 reduce-scatter.6
  471.4 163.6 all-gather.18
  637.2 32.6 all-gather.16
  671.5 34.4 all-gather.22
  708.3 93.5 all-gather.20
  837.1 42.6 reduce-scatter.10
  885.3 34.4 all-gather.24
  923.5 110.3 reduce-scatter.16
  1037.3 68.2 reduce-scatter.14
  1312.9 44.6 reduce-scatter.12
  1360.1 44.5 reduce-scatter.8
  1408.9 599.0 all-reduce.11
where the time goes:
time: 2040 us; the launch traced here: 2020 us
  waiting for transfers between devices  1060 us (52%)
  local copies, waits for them, and re-layouts  336 us (16%)
  matrix products  326 us (16%)
  other arithmetic  143 us (7%)
  blocking collectives  89.9 us (4%)
  loops' own time  45 us (2%)
    unnamed x16, waiting for transfers between devices  575 us
    all_gather x1, waiting for transfers between devices, body(): lax.all_gather(gate_up, 'dp', axis=0, tiled=True)  161 us
    all_gather x1, waiting for transfers between devices, body(): lax.all_gather(down, 'dp', axis=1, tiled=True)  95.9 us
    dynamic_update_slice x32, local copies, waits for them, and re-layouts, mixer_core(): lax.scan(jax.checkpoint(block_step), initial, (split_blocks(query), split...  93.7 us
    all_gather x1, waiting for transfers between devices, body(): lax.all_gather(mixer_in, 'dp', axis=0, tiled=True)  81.2 us
    squeeze x64, local copies, waits for them, and re-layouts, mixer_core(): lax.scan(jax.checkpoint(block_step), initial, (split_blocks(query), split...  58.3 us
    dot_general x48, matrix products, block_step(): jnp.einsum('shc,she->hce', key_tail, input_block, precision=HIGHEST)  55 us
    dot_general x64, matrix products, block_step(): jnp.einsum('thc,shc->hts', query_decay, key_decay, precision=HIGHEST)  50 us
  transfers between devices with their start and end apart: 15, of which 10 were waited for; matrix products, arithmetic and copies ran while one was open for 37% of the time, Pallas kernels for 0%

commit v1 on v0

v1 whole, which is shorter than its diff:
```python
import functools
import jax
import jax.numpy as jnp
from jax import lax
from jax.experimental import pallas as pl
from jax.experimental.pallas import tpu as pltpu
from jax.sharding import PartitionSpec as P

HD = 128
CHUNK = 128
GROUP_EPSILON = 0.01
F32 = jnp.float32
BF16 = jnp.bfloat16
NN = (((1,), (0,)), ((), ()))
NT = (((1,), (1,)), ((), ()))
TN = (((0,), (0,)), ((), ()))


def mm(a, b, dims):
    return lax.dot_general(a, b, dims, preferred_element_type=F32)


def halves(x):
    high = x.astype(BF16)
    return high, (x - high.astype(F32)).astype(BF16)


def tri_sum(tri, x):
    high, rest = halves(x)
    return mm(tri, high, NN) + mm(tri, rest, NN)


def decays(a_raw, lower):
    sig = jax.nn.sigmoid(a_raw)
    forget = 0.8 + 0.2 * sig
    key = 1.0 - forget
    cum = tri_sum(lower, jnp.log(forget))
    return sig, forget, key, cum


def masks(seg, doc_col, doc_row, block):
    rows = lax.broadcasted_iota(jnp.int32, (CHUNK, CHUNK), 0)
    cols = lax.broadcasted_iota(jnp.int32, (CHUNK, CHUNK), 1)
    causal = rows >= cols
    same = jnp.logical_and(causal, doc_col == doc_row)
    start = block * CHUNK
    end_doc = seg[start + CHUNK - 1]
    last_doc = jnp.where(block > 0, seg[jnp.maximum(start - 1, 0)], -1)
    cont = (doc_col == last_doc).astype(F32)
    tail = (doc_col == end_doc).astype(F32)
    keep = jnp.where(end_doc == last_doc, 1.0, 0.0).astype(F32)
    return causal, same, cont, tail, keep


def forward_kernel(seg, q_ref, a_ref, v_ref, z_ref, col_ref, row_ref, gain_ref,
                   y_ref, o_ref, s_ref, state):
    block = pl.program_id(0)

    @pl.when(block == 0)
    def _():
        state[...] = jnp.zeros_like(state)

    width = q_ref.shape[1]
    causal, same, cont, tail, keep = masks(seg, col_ref[...], row_ref[...], block)
    lower = jnp.where(causal, 1.0, 0.0).astype(BF16)
    _, _, key, cum = decays(a_ref[...].astype(F32), lower)
    total = cum[CHUNK - 1 : CHUNK, :]
    qd, qd_rest = halves(q_ref[...].astype(F32) * jnp.exp(cum))
    kd, kd_rest = halves(key * jnp.exp(-cum))
    kt, kt_rest = halves(key * jnp.exp(total - cum) * tail)
    fade = jnp.exp(total) * keep
    gain = gain_ref[...]
    s_ref[0] = state[...]
    for head in range(width // HD):
        at = slice(head * HD, (head + 1) * HD)
        v = v_ref[:, at]
        st = state[:, at]
        st_high, st_rest = halves(st)
        qh, ql = qd[:, at], qd_rest[:, at]
        scores = mm(qh, kd[:, at], NT) + (mm(qh, kd_rest[:, at], NT) + mm(ql, kd[:, at], NT))
        scores = jnp.where(same, scores, 0.0).astype(BF16)
        earlier = mm(qh, st_high, NT) + (mm(qh, st_rest, NT) + mm(ql, st_high, NT))
        o = mm(scores, v, NN) + cont * earlier
        state[:, at] = st * fade[:, at] + (mm(v, kt[:, at], TN) + mm(v, kt_rest[:, at], TN))
        o_ref[:, at] = o
        z = z_ref[:, at].astype(F32)
        r = lax.rsqrt(jnp.mean(o * o, axis=-1, keepdims=True) + GROUP_EPSILON)
        y_ref[:, at] = (o * r * gain * (z * jax.nn.sigmoid(z))).astype(BF16)


def backward_kernel(seg, q_ref, a_ref, v_ref, z_ref, col_ref, row_ref, gain_ref, o_ref, s_ref, dy_ref,
                    d_ref, dgain_ref, dstate):
    step = pl.program_id(0)
    block = pl.num_programs(0) - 1 - step

    @pl.when(step == 0)
    def _():
        dstate[...] = jnp.zeros_like(dstate)
        dgain_ref[...] = jnp.zeros_like(dgain_ref)

    width = q_ref.shape[1]
    causal, same, cont, tail, keep = masks(seg, col_ref[...], row_ref[...], block)
    lower = jnp.where(causal, 1.0, 0.0).astype(BF16)
    sig, forget, key, cum = decays(a_ref[...].astype(F32), lower)
    total = cum[CHUNK - 1 : CHUNK, :]
    up = jnp.exp(cum)
    down = jnp.exp(-cum)
    late = jnp.exp(total - cum) * tail
    qd = (q_ref[...].astype(F32) * up).astype(BF16)
    kd = (key * down).astype(BF16)
    kt = (key * late).astype(BF16)
    fade = jnp.exp(total) * keep
    gain = gain_ref[...]
    gain_sum = jnp.zeros((1, HD), F32)
    dcums = []
    dkeys = []
    for head in range(width // HD):
        at = slice(head * HD, (head + 1) * HD)
        v = v_ref[:, at]
        o = o_ref[:, at]
        z = z_ref[:, at].astype(F32)
        dy = dy_ref[:, at]
        r = lax.rsqrt(jnp.mean(o * o, axis=-1, keepdims=True) + GROUP_EPSILON)
        n = o * r
        sz = jax.nn.sigmoid(z)
        dng = dy * (z * sz)
        gain_sum += jnp.sum(dng * n, axis=0, keepdims=True)
        dn = dng * gain
        do = (r * (dn - n * jnp.mean(dn * n, axis=-1, keepdims=True))).astype(BF16)
        d_ref[:, 3 * width + head * HD : 3 * width + (head + 1) * HD] = (
            dy * n * gain * (sz * (1.0 + z * (1.0 - sz)))
        ).astype(BF16)
        qh, kh, th = qd[:, at], kd[:, at], kt[:, at]
        scores = jnp.where(same, mm(qh, kh, NT), 0.0).astype(BF16)
        dscores = jnp.where(same, mm(do, v, NT), 0.0).astype(BF16)
        st = s_ref[0, :, at]
        dst = dstate[:, at]
        dst_low = dst.astype(BF16)
        dv = mm(scores, do, TN) + mm(th, dst_low, NT)
        dqd = mm(dscores, kh, NN) + cont * mm(do, st.astype(BF16), NN)
        dkd = mm(dscores, qh, TN)
        dkt = mm(v, dst_low, NN)
        carried = dkt * th.astype(F32)
        dtotal = jnp.sum(carried, axis=0, keepdims=True) + fade[:, at] * jnp.sum(
            dst * st, axis=0, keepdims=True
        )
        dstate[:, at] = dst * fade[:, at] + mm((do.astype(F32) * cont).astype(BF16), qh, TN)
        d_ref[:, head * HD : (head + 1) * HD] = (dqd * up[:, at]).astype(BF16)
        d_ref[:, 2 * width + head * HD : 2 * width + (head + 1) * HD] = dv.astype(BF16)
        dkeys.append(dkd * down[:, at] + dkt * late[:, at])
        dcum = dqd * qh.astype(F32) - dkd * kh.astype(F32) - carried
        high, rest = halves(dcum)
        dlog = mm(lower, high, TN) + mm(lower, rest, TN) + dtotal
        slope = 0.2 * sig[:, at] * (1.0 - sig[:, at])
        d_ref[:, width + head * HD : width + (head + 1) * HD] = (
            (dlog / forget[:, at] - dkeys[-1]) * slope
        ).astype(BF16)
    dgain_ref[...] += gain_sum


def rec_forward(proj, seg, gain):
    length, width = proj.shape[0], proj.shape[1] // 4
    blocks = length // CHUNK
    part = lambda k: pl.BlockSpec((CHUNK, width), lambda i, s, k=k: (i, k))
    return pl.pallas_call(
        forward_kernel,
        grid_spec=pltpu.PrefetchScalarGridSpec(
            num_scalar_prefetch=1,
            grid=(blocks,),
            in_specs=[part(0), part(1), part(2), part(3),
                      pl.BlockSpec((CHUNK, 1), lambda i, s: (i, 0)),
                      pl.BlockSpec((1, CHUNK), lambda i, s: (0, i)),
                      pl.BlockSpec((1, HD), lambda i, s: (0, 0))],
            out_specs=[pl.BlockSpec((CHUNK, width), lambda i, s: (i, 0)),
                       pl.BlockSpec((CHUNK, width), lambda i, s: (i, 0)),
                       pl.BlockSpec((1, HD, width), lambda i, s: (i, 0, 0))],
            scratch_shapes=[pltpu.VMEM((HD, width), F32)],
        ),
        out_shape=[jax.ShapeDtypeStruct((length, width), BF16),
                   jax.ShapeDtypeStruct((length, width), F32),
                   jax.ShapeDtypeStruct((blocks, HD, width), F32)],
        cost_estimate=pl.CostEstimate(flops=30_000_000_000, bytes_accessed=10_000_000, transcendentals=0),
        name="mixer_forward",
    )(seg, proj, proj, proj, proj, seg.reshape(length, 1), seg.reshape(1, length), gain.reshape(1, HD))


def rec_backward(proj, seg, gain, o, states, dy):
    length, width = proj.shape[0], proj.shape[1] // 4
    blocks = length // CHUNK
    last = blocks - 1
    part = lambda k: pl.BlockSpec((CHUNK, width), lambda i, s, k=k: (last - i, k))
    return pl.pallas_call(
        backward_kernel,
        grid_spec=pltpu.PrefetchScalarGridSpec(
            num_scalar_prefetch=1,
            grid=(blocks,),
            in_specs=[part(0), part(1), part(2), part(3),
                      pl.BlockSpec((CHUNK, 1), lambda i, s: (last - i, 0)),
                      pl.BlockSpec((1, CHUNK), lambda i, s: (0, last - i)),
                      pl.BlockSpec((1, HD), lambda i, s: (0, 0)),
                      part(0),
                      pl.BlockSpec((1, HD, width), lambda i, s: (last - i, 0, 0)),
                      part(0)],
            out_specs=[pl.BlockSpec((CHUNK, 4 * width), lambda i, s: (last - i, 0)),
                       pl.BlockSpec((1, HD), lambda i, s: (0, 0))],
            scratch_shapes=[pltpu.VMEM((HD, width), F32)],
        ),
        out_shape=[jax.ShapeDtypeStruct((length, 4 * width), BF16),
                   jax.ShapeDtypeStruct((1, HD), F32)],
        cost_estimate=pl.CostEstimate(flops=60_000_000_000, bytes_accessed=14_000_000, transcendentals=0),
        name="mixer_backward",
    )(seg, proj, proj, proj, proj, seg.reshape(length, 1), seg.reshape(1, length), gain.reshape(1, HD), o, states, dy)


EPSILON = 1e-06
SPEC_ROWS = P(("dp", "tensor"), None)


def ring_order(count):
    return list(range(0, count, 2)) + list(range(count - 1 - count % 2, 0, -2))


class Ring:
    def __init__(self, axis, count):
        order = ring_order(count)
        self.axis, self.count = axis, count
        self.order = jnp.array(order, jnp.int32)
        self.ahead = [(order[i], order[(i + 1) % count]) for i in range(count)]
        self.behind = [(b, a) for a, b in self.ahead]
        place = [order.index(i) for i in range(count)]
        self.me = lax.axis_index(axis)
        self.place = jnp.array(place, jnp.int32)[self.me]

    def owner(self, shift):
        return self.order[(self.place + shift + 2 * self.count) % self.count]

    def send_ahead(self, x):
        return lax.ppermute(x, self.axis, self.ahead)

    def send_behind(self, x):
        return lax.ppermute(x, self.axis, self.behind)

    def gather(self, x, dim):
        size = x.shape[dim]
        half = x.shape[0] // 2
        shape = list(x.shape)
        shape[dim] *= self.count

        def put(whole, block, owner, row=0):
            at = [row, 0]
            at[dim] = at[dim] + owner * size
            return lax.dynamic_update_slice(whole, block, at)

        whole = put(jnp.zeros(shape, x.dtype), x, self.me)
        left = right = x
        steps = self.count // 2
        for step in range(1, steps):
            left, right = self.send_ahead(left), self.send_behind(right)
            whole = put(whole, left, self.owner(-step))
            whole = put(whole, right, self.owner(step))
        left, right = self.send_ahead(left[:half]), self.send_behind(right[half:])
        whole = put(whole, left, self.owner(-steps))
        return put(whole, right, self.owner(steps), half)

    def scatter_sum(self, x, dim):
        shape = list(x.shape)
        shape[dim] //= self.count
        size, half = shape[dim], shape[0] // 2
        shape[0] = half

        def part(shift, row):
            at = [row, 0]
            at[dim] = at[dim] + self.owner(shift) * size
            return lax.dynamic_slice(x, at, shape)

        left, right = part(-1, 0), part(1, half)
        for step in range(1, self.count):
            left, right = self.send_ahead(left), self.send_behind(right)
            own_left, own_right = part(-1 - step, 0), part(1 + step, half)
            if step == self.count - 1:
                left, right = left.astype(F32), right.astype(F32)
                own_left, own_right = own_left.astype(F32), own_right.astype(F32)
            left, right = left + own_left, right + own_right
        return jnp.concatenate([left, right], axis=0)


def gather_small(row, axis, count):
    me = lax.axis_index(axis)
    whole = lax.dynamic_update_slice(jnp.zeros((count, row.shape[1]), row.dtype), row, (me, 0))
    for turn in range(1, count):
        got = lax.ppermute(row, axis, [(i, (i + turn) % count) for i in range(count)])
        whole = lax.dynamic_update_slice(whole, got, ((me - turn + count) % count, 0))
    return whole


def scatter_sum_small(rows, axis, count):
    me = lax.axis_index(axis)
    total = lax.dynamic_slice_in_dim(rows, me, 1, 0)
    for turn in range(1, count):
        mine = lax.dynamic_slice_in_dim(rows, (me + turn) % count, 1, 0)
        total = total + lax.ppermute(mine, axis, [(i, (i + turn) % count) for i in range(count)])
    return total


def norm_forward(values, gain):
    r = lax.rsqrt(jnp.mean(values * values, axis=-1, keepdims=True) + EPSILON)
    return (values * r * gain).astype(BF16), r


def norm_backward(values, r, gain, grad):
    n = values * r
    scaled = grad * gain
    back = r * (scaled - n * jnp.mean(scaled * n, axis=-1, keepdims=True))
    return back, jnp.sum(grad * n, axis=0)


def tensor_gather(x):
    return lax.all_gather(x, "tensor", axis=0, tiled=True)


def tensor_scatter_sum(x):
    return lax.psum_scatter(x, "tensor", scatter_dimension=0, tiled=True).astype(F32)


def body(n_dp, n_tensor, tokens, segment_ids, mixer_in, mixer_out, gate_up, down,
         norm_gain, group_gain, ffn_gain, cotangent):
    ring = Ring("dp", n_dp)
    seg = segment_ids[0]
    x = tokens.astype(F32)
    part, small = norm_gain.shape[0], group_gain.shape[0]
    model = part * n_dp
    width = mixer_out.shape[0]
    hidden_width = down.shape[0]

    gains = gather_small(jnp.concatenate([norm_gain, ffn_gain, group_gain]).astype(F32)[None], "dp", n_dp)
    gain_in = gains[:, :part].reshape(1, model)
    gain_ffn = gains[:, part : 2 * part].reshape(1, model)
    gain_group = gains[:, 2 * part :].reshape(1, HD)

    w_in = ring.gather(mixer_in.reshape(part, 4 * width), 0)
    w_out = ring.gather(mixer_out, 1)
    w_gu = ring.gather(gate_up.reshape(part, 2 * hidden_width), 0)
    w_down = ring.gather(down, 1)

    h1_own, r1 = norm_forward(x, gain_in)
    h1 = tensor_gather(h1_own)
    cot = tensor_gather(cotangent)
    proj = mm(h1, w_in, NN).astype(BF16)
    y, o, states = rec_forward(proj, seg, gain_group)
    attn = tensor_scatter_sum(mm(y, w_out, NN).astype(BF16))
    x2 = x + attn
    h2_own, r2 = norm_forward(x2, gain_ffn)
    h2 = tensor_gather(h2_own)
    gu = mm(h2, w_gu, NN)
    gate, up = gu[:, :hidden_width], gu[:, hidden_width:]
    sg = jax.nn.sigmoid(gate)
    swish = gate * sg
    hidden = (swish * up).astype(BF16)
    d_down = ring.scatter_sum(mm(hidden, cot, TN).astype(BF16), 1)
    dh = mm(cot, w_down, NT)
    dgate = (dh * up * sg * (1.0 + gate * (1.0 - sg))).astype(BF16)
    dup = (dh * swish).astype(BF16)
    dgu = jnp.concatenate([dgate, dup], axis=1)
    d_gu = ring.scatter_sum(mm(h2, dgu, TN).astype(BF16), 0)
    dh2 = tensor_scatter_sum(mm(dgu, w_gu, NT).astype(BF16))
    back2, d_gain_ffn = norm_backward(x2, r2, gain_ffn, dh2)
    dx2 = cotangent.astype(F32) + back2
    dattn = tensor_gather(dx2.astype(BF16))
    d_out = ring.scatter_sum(mm(y, dattn, TN).astype(BF16), 1)
    dy = mm(dattn, w_out, NT)
    dproj, d_group = rec_backward(proj, seg, gain_group, o, states, dy)
    d_in = ring.scatter_sum(mm(h1, dproj, TN).astype(BF16), 0)
    dh1 = tensor_scatter_sum(mm(dproj, w_in, NT).astype(BF16))
    back1, d_gain_in = norm_backward(x, r1, gain_in, dh1)
    d_tokens = (dx2 + back1).astype(BF16)
    output = (x2 + tensor_scatter_sum(mm(hidden, w_down, NN).astype(BF16))).astype(BF16)

    d_gains = jnp.concatenate(
        [d_gain_in.reshape(n_dp, part), d_gain_ffn.reshape(n_dp, part), d_group.reshape(n_dp, small)], axis=1
    )
    d_gains = scatter_sum_small(lax.psum(d_gains, "tensor"), "dp", n_dp)[0]
    return (
        output,
        d_tokens,
        d_in.reshape(part, 4, width),
        d_out,
        d_gu.reshape(part, 2, hidden_width),
        d_down,
        d_gains[:part],
        d_gains[2 * part :],
        d_gains[part : 2 * part],
    )


def solution(mesh):
    split = P("dp", None, "tensor")
    cross = P("tensor", "dp")
    return jax.shard_map(
        functools.partial(body, mesh.shape["dp"], mesh.shape["tensor"]),
        mesh=mesh,
        in_specs=(SPEC_ROWS, P("dp", None), split, cross, split, cross, P("dp"), P("dp"), P("dp"), SPEC_ROWS),
        out_specs=(SPEC_ROWS, SPEC_ROWS, split, cross, split, cross, P("dp"), P("dp"), P("dp")),
        check_vma=False,
    )
```

time: 2040 us -> 923 us (0.45)
  waiting for transfers between devices: 1060 us -> 455 us
  local copies, waits for them, and re-layouts: 336 us -> 69.1 us
  matrix products: 326 us -> 138 us
  starting transfers between devices: 1.19 us -> 120 us
  other arithmetic: 143 us -> 55 us
  blocking collectives: 89.9 us -> 10.3 us
  loops' own time: 45 us -> 0 us
  Pallas kernels: 0 us -> 32.9 us
    unnamed x16 -> x8, waiting for transfers between devices: 575 us -> 0.13 us
    all_gather x8 -> x4, waiting for transfers between devices: 421 us -> 24 us  [tensor_gather(): return lax.all_gather(x, 'tensor', axis=0, tiled=True)]
    ppermute x0 -> x102, waiting for transfers between devices: none -> 342 us  [the longest x44 244 us: send_ahead(): return lax.ppermute(x, self.axis, self.ahead)]
    dot_general x220 -> x12, matrix products: 326 us -> 138 us  [mm(): return lax.dot_general(a, b, dims, preferred_element_type=F32)]
    ppermute x0 -> x102, starting transfers between devices: none -> 119 us  [the longest x44 61.7 us: send_ahead(): return lax.ppermute(x, self.axis, self.ahead)]
    dynamic_update_slice x32 -> x44, local copies, waits for them, and re-layouts: 93.7 us -> 34.4 us  [the longest x36 33.9 us: put(): return lax.dynamic_update_slice(whole, block, at)]
    squeeze x64 -> x0, local copies, waits for them, and re-layouts: 58.3 us -> none  [mixer_core(): lax.scan(jax.checkpoint(block_step), initial, (split_blocks(query), split...]
    convert_element_type x64 -> x5, other arithmetic: 69.2 us -> 13.8 us  [the longest x2 5.09 us: norm_forward(): return ((values * r * gain).astype(BF16), r)]
  transfers between devices with their start and end apart: 15 -> 110, of which waited for: 10 -> 53; matrix products, arithmetic and copies ran while one was open for 37% -> 18% of each run, Pallas kernels for 0% -> 0%
where the time goes in v1:
time: 923 us; the launch traced here: 916 us
  waiting for transfers between devices  455 us (49%)
  matrix products  138 us (15%)
  starting transfers between devices  120 us (13%)
  local copies, waits for them, and re-layouts  69.1 us (7%)
  other arithmetic  55 us (6%)
  between operations  36.7 us (4%)
  Pallas kernels  32.9 us (4%)
  blocking collectives  10.3 us (1%)
    ppermute x44, waiting for transfers between devices, send_ahead(): return lax.ppermute(x, self.axis, self.ahead)  244 us
    dot_general x12, matrix products, mm(): return lax.dot_general(a, b, dims, preferred_element_type=F32)  138 us
    ppermute x44, waiting for transfers between devices, send_behind(): return lax.ppermute(x, self.axis, self.behind)  95.5 us
    reduce_scatter x4, waiting for transfers between devices, tensor_scatter_sum(): lax.psum_scatter(x, 'tensor', scatter_dimension=0, tiled=True).astype(F32)  88.7 us
    ppermute x44, starting transfers between devices, send_ahead(): return lax.ppermute(x, self.axis, self.ahead)  61.7 us
    ppermute x44, starting transfers between devices, send_behind(): return lax.ppermute(x, self.axis, self.behind)  35.8 us
    dynamic_update_slice x36, local copies, waits for them, and re-layouts, put(): return lax.dynamic_update_slice(whole, block, at)  33.9 us
    add x28, other arithmetic, scatter_sum(): left, right = (left + own_left, right + own_right)  28.1 us
  transfers between devices with their start and end apart: 110, of which 53 were waited for; matrix products, arithmetic and copies ran while one was open for 18% of the time, Pallas kernels for 0%

profile of v1, /device:TPU:0, one launch (start us, length us, event | category | flops | bytes accessed | tf_op | source)
XLA Modules:
  0.0 916.3 jit_solution(15714423924570953423)
XLA Ops:
  33.9 22.0 %collective-permute-done.7 = bf16[256,2048]{1,0:T(8,128)(2,1)S(1)} collective-permute-done((bf16[256,2048]{1,0:T(8,128)(2,1)S(1)}, bf16[256,2048]{1,0:T(8,128)(2,1)S(1)}, u32[]{:S(2)}, u32[]{:S(2)}) %collective-permute-start.7) | collective-permute-done | bytes 1048608 | tf_op jit(solution)/shard_map/ppermute | solution.py:238
  113.2 11.9 %collective-permute-done.11 = bf16[256,2048]{1,0:T(8,128)(2,1)S(1)} collective-permute-done((bf16[256,2048]{1,0:T(8,128)(2,1)}, bf16[256,2048]{1,0:T(8,128)(2,1)S(1)}, u32[]{:S(2)}, u32[]{:S(2)}) %collective-permute-start.11) | collective-permute-done | bytes 1048608 | tf_op jit(solution)/shard_map/ppermute | solution.py:238
  138.4 13.9 %convolution_convert_fusion.7.q_ref.a_ref.v_ref.z_ref = bf16[1024,2048]{1,0:T(8,128)(2,1)} fusion(bf16[1024,2048]{1,0:T(8,128)(2,1)} %all-gather.5.cloned.1.call-done, bf16[2048,2048]{1,0:T(8,128)(2,1)} %constant_dynamic-update-slice_fusion.25), kind=kOutput, calls=%fused_computation.17 | convolution fusion | flops 8592031744 | bytes 16777216 | tf_op jit(solution)/shard_map/dot_general | solution.py:20
  152.3 13.9 %mixer_forward.1 = (bf16[1024,512]{1,0:T(8,128)(2,1)}, f32[1024,512]{1,0:T(8,128)}, f32[8,128,512]{2,1,0:T(8,128)}) custom-call(s32[1024]{0:T(1024)} %bitcast.101, bf16[1024,2048]{1,0:T(8,128)(2,1)} %convolution_convert_fusion.7.q_ref.a_ref.v_ref.z_ref, bf16[1024,2048]{1,0:T(8,128)(2,1)} %convolution_convert_fusion.7.q_ref.a_ref.v_ref.z_ref, ...), custom_call_target="tpu_custom_call" | custom-call | flops 30000001024 | bytes 10000000 | tf_op jit(solution)/shard_map/mixer_forward/pallas_call | solution.py:165
  171.9 45.0 %reduce-scatter.5.cloned.1.call-done = bf16[256,2048]{1,0:T(8,128)(2,1)} async-done(((bf16[1024,2048]{1,0:T(8,128)(2,1)}), bf16[256,2048]{1,0:T(8,128)(2,1)}) %reduce-scatter.5.cloned.1.call-update) | async-done | bytes 1048592 | tf_op jit(solution)/shard_map/reduce_scatter | solution.py:322
  233.8 37.9 %collective-permute-done.31 = bf16[1408,256]{1,0:T(8,128)(2,1)} collective-permute-done((bf16[1408,256]{1,0:T(8,128)(2,1)S(1)}, bf16[1408,256]{1,0:T(8,128)(2,1)}, u32[]{:S(2)}, u32[]{:S(2)}) %collective-permute-start.31) | collective-permute-done | bytes 720928 | tf_op jit(solution)/shard_map/ppermute | solution.py:238
  279.1 11.9 %collective-permute-done.33 = bf16[1408,256]{1,0:T(8,128)(2,1)S(1)} collective-permute-done((bf16[1408,256]{1,0:T(8,128)(2,1)}, bf16[1408,256]{1,0:T(8,128)(2,1)S(1)}, u32[]{:S(2)}, u32[]{:S(2)}) %collective-permute-start.33) | collective-permute-done | bytes 720928 | tf_op jit(solution)/shard_map/ppermute | solution.py:238
  298.4 36.8 %collective-permute-done.35 = bf16[1408,256]{1,0:T(8,128)(2,1)S(1)} collective-permute-done((bf16[1408,256]{1,0:T(8,128)(2,1)S(1)}, bf16[1408,256]{1,0:T(8,128)(2,1)S(1)}, u32[]{:S(2)}, u32[]{:S(2)}) %collective-permute-start.35) | collective-permute-done | bytes 720928 | tf_op jit(solution)/shard_map/ppermute | solution.py:238
  351.6 23.1 %collective-permute-done.27 = bf16[256,2816]{1,0:T(8,128)(2,1)S(1)} collective-permute-done((bf16[256,2816]{1,0:T(8,128)(2,1)S(1)}, bf16[256,2816]{1,0:T(8,128)(2,1)S(1)}, u32[]{:S(2)}, u32[]{:S(2)}) %collective-permute-start.27) | collective-permute-done | bytes 1441824 | tf_op jit(solution)/shard_map/ppermute | solution.py:238
  379.6 10.4 %collective-permute-done.29 = bf16[128,2816]{1,0:T(8,128)(2,1)S(1)} collective-permute-done((bf16[128,2816]{1,0:T(8,128)(2,1)S(1)}, bf16[128,2816]{1,0:T(8,128)(2,1)S(1)}, u32[]{:S(2)}, u32[]{:S(2)}) %collective-permute-start.29) | collective-permute-done | bytes 720928 | tf_op jit(solution)/shard_map/ppermute | solution.py:238
  392.4 18.7 %fusion.32 = f32[1024,2816]{1,0:T(8,128)} fusion(bf16[1024,2048]{1,0:T(8,128)(2,1)} %all-gather.7.cloned.1.call-done, bf16[2048,2816]{1,0:T(8,128)(2,1)} %constant_dynamic-update-slice_fusion.8), kind=kOutput, calls=%fused_computation.177 | convolution fusion | flops 11811160064 | bytes 27262976 | tf_op jit(solution)/shard_map/dot_general | solution.py:20
  411.1 15.6 %fusion.2 = (bf16[1024,1408]{1,0:T(8,128)(2,1)S(1)}, bf16[1024,1408]{1,0:T(8,128)(2,1)S(1)}, bf16[1024,1408]{1,0:T(8,128)(2,1)}) fusion(f32[1024,2816]{1,0:T(8,128)} %fusion.32, bf16[1408,2048]{1,0:T(8,128)(2,1)} %copy-done.8, bf16[1024,2048]{1,0:T(8,128)(2,1)} %all-gather.9.cloned.1.call-done), kind=kOutput, calls=%fused_computation.8 | convolution fusion | flops 5927206912 | bytes 30146560 | tf_op jit(solution)/shard_map/dot_general | solution.py:20
  429.2 16.3 %convolution_convert_fusion.3 = bf16[1024,2048]{1,0:T(8,128)(2,1)} fusion(bf16[2048,2816]{1,0:T(8,128)(2,1)} %constant_dynamic-update-slice_fusion.8, bf16[1024,1408]{1,0:T(8,128)(2,1)S(1)} %get-tuple-element.24, bf16[1024,1408]{1,0:T(8,128)(2,1)S(1)} %get-tuple-element.23), kind=kOutput, calls=%fused_computation.13 | convolution fusion | flops 11824791552 | bytes 21495808 | tf_op jit(solution)/shard_map/dot_general | solution.py:20
  445.9 43.7 %reduce-scatter.9.cloned.1.call-done = bf16[256,2048]{1,0:T(8,128)(2,1)} async-done(((bf16[1024,2048]{1,0:T(8,128)(2,1)}), bf16[256,2048]{1,0:T(8,128)(2,1)}) %reduce-scatter.9.cloned.1.call-update) | async-done | bytes 1048592 | tf_op jit(solution)/shard_map/reduce_scatter | solution.py:322
  495.7 10.6 %convolution_convert_fusion.1 = bf16[1408,2048]{1,0:T(8,128)(2,1)} fusion(bf16[1024,1408]{1,0:T(8,128)(2,1)} %get-tuple-element.41, bf16[1024,2048]{1,0:T(8,128)(2,1)} %all-gather.9.cloned.1.call-done), kind=kOutput, calls=%fused_computation.1 | convolution fusion | flops 5908463616 | bytes 12845056 | tf_op jit(solution)/shard_map/dot_general | solution.py:20
  506.3 24.0 %all-gather.11.cloned.1.call-done = bf16[1024,2048]{1,0:T(8,128)(2,1)} async-done(((bf16[256,2048]{1,0:T(8,128)(2,1)}), bf16[1024,2048]{1,0:T(8,128)(2,1)}) %all-gather.11.cloned.1.call-update) | async-done | bytes 4194320 | tf_op jit(solution)/shard_map/all_gather | solution.py:318
  536.2 19.0 %mixer_backward.1 = (bf16[1024,2048]{1,0:T(8,128)(2,1)}, f32[1,128]{1,0:T(1,128)}) custom-call(s32[1024]{0:T(1024)} %bitcast.102, bf16[1024,2048]{1,0:T(8,128)(2,1)} %convolution_convert_fusion.7.q_ref.a_ref.v_ref.z_ref, bf16[1024,2048]{1,0:T(8,128)(2,1)} %convolution_convert_fusion.7.q_ref.a_ref.v_ref.z_ref, ...), custom_call_target="tpu_custom_call" | custom-call | flops 60000002048 | bytes 14000000 | tf_op jit(solution)/shard_map/mixer_backward/pallas_call | solution.py:192
  555.2 14.0 %convolution_convert_fusion.4 = bf16[1024,2048]{1,0:T(8,128)(2,1)} fusion(bf16[1024,2048]{1,0:T(8,128)(2,1)} %get-tuple-element.17, bf16[2048,2048]{1,0:T(8,128)(2,1)} %constant_dynamic-update-slice_fusion.25), kind=kOutput, calls=%fused_computation.14 | convolution fusion | flops 8592031744 | bytes 16777216 | tf_op jit(solution)/shard_map/dot_general | solution.py:20
  573.3 16.6 %convolution_convert_fusion = bf16[2048,2816]{1,0:T(8,128)(2,1)S(1)} fusion(bf16[1024,2048]{1,0:T(8,128)(2,1)} %all-gather.7.cloned.1.call-done, bf16[1024,1408]{1,0:T(8,128)(2,1)} %copy-done.34, bf16[1024,1408]{1,0:T(8,128)(2,1)} %copy-done.33), kind=kOutput, calls=%fused_computation | convolution fusion | flops 11828461568 | bytes 21495808 | tf_op jit(solution)/shard_map/dot_general | solution.py:20
  600.6 19.1 %collective-permute-done.82 = bf16[704,256]{1,0:T(8,128)(2,1)S(1)} collective-permute-done((bf16[704,256]{1,0:T(8,128)(2,1)}, bf16[704,256]{1,0:T(8,128)(2,1)S(1)}, u32[]{:S(2)}, u32[]{:S(2)}) %collective-permute-start.82) | collective-permute-done | bytes 360480 | tf_op jit(solution)/shard_map/ppermute | solution.py:238
  644.4 9.8 %collective-permute-done.84 = bf16[704,256]{1,0:T(8,128)(2,1)S(1)} collective-permute-done((bf16[704,256]{1,0:T(8,128)(2,1)}, bf16[704,256]{1,0:T(8,128)(2,1)S(1)}, u32[]{:S(2)}, u32[]{:S(2)}) %collective-permute-start.84) | collective-permute-done | bytes 360480 | tf_op jit(solution)/shard_map/ppermute | solution.py:238
  673.9 8.2 convolution_convert_fusion.5
  703.4 9.8 %convolution_convert_fusion.2 = bf16[2048,2048]{1,0:T(8,128)(2,1)S(1)} fusion(bf16[1024,2048]{1,0:T(8,128)(2,1)S(1)} %copy-done.28, bf16[1024,2048]{1,0:T(8,128)(2,1)S(1)} %copy-done.35), kind=kOutput, calls=%fused_computation.2 | convolution fusion | flops 8594128896 | bytes 16777216 | tf_op jit(solution)/shard_map/dot_general | solution.py:20
  733.8 8.5 collective-permute-done.54
  748.6 12.8 %collective-permute-done.77 = bf16[128,2816]{1,0:T(8,128)(2,1)S(1)} collective-permute-done((bf16[128,2816]{1,0:T(8,128)(2,1)S(1)}, bf16[128,2816]{1,0:T(8,128)(2,1)S(1)}, u32[]{:S(2)}, u32[]{:S(2)}) %collective-permute-start.77) | collective-permute-done | bytes 720928 | tf_op jit(solution)/shard_map/ppermute | solution.py:241
  766.4 9.1 collective-permute-done.48
  780.3 10.6 %collective-permute-done.78 = bf16[128,2816]{1,0:T(8,128)(2,1)S(1)} collective-permute-done((bf16[128,2816]{1,0:T(8,128)(2,1)S(1)}, bf16[128,2816]{1,0:T(8,128)(2,1)S(1)}, u32[]{:S(2)}, u32[]{:S(2)}) %collective-permute-start.78) | collective-permute-done | bytes 720928 | tf_op jit(solution)/shard_map/ppermute | solution.py:241
  795.9 9.1 collective-permute-done.49
  809.8 10.6 %collective-permute-done.79 = bf16[128,2816]{1,0:T(8,128)(2,1)S(1)} collective-permute-done((bf16[128,2816]{1,0:T(8,128)(2,1)S(1)}, bf16[128,2816]{1,0:T(8,128)(2,1)S(1)}, u32[]{:S(2)}, u32[]{:S(2)}) %collective-permute-start.79) | collective-permute-done | bytes 720928 | tf_op jit(solution)/shard_map/ppermute | solution.py:241
  825.4 9.1 collective-permute-done.50
  839.3 10.6 %collective-permute-done.80 = bf16[128,2816]{1,0:T(8,128)(2,1)S(1)} collective-permute-done((bf16[128,2816]{1,0:T(8,128)(2,1)S(1)}, bf16[128,2816]{1,0:T(8,128)(2,1)S(1)}, u32[]{:S(2)}, u32[]{:S(2)}) %collective-permute-start.80) | collective-permute-done | bytes 720928 | tf_op jit(solution)/shard_map/ppermute | solution.py:241
  884.2 10.3 %psum.7 = f32[8,528]{1,0:T(8,128)S(1)} all-reduce(f32[8,528]{1,0:T(8,128)S(1)} %pad_maximum_fusion.7), channel_id=1, replica_groups=mesh['dp'=8,'tensor'=4] {'tensor'}, use_global_device_ids=true, to_apply=%region_10.11 | all-reduce | flops 4224 | bytes 33792 | tf_op jit(solution)/shard_map/psum | solution.py:381
  (425 shorter events, 336.8 us)
Async XLA Ops:
  7.2 131.2 %all-gather.5.cloned.1.call-start = ((), (), s32[]{:S(2)}) async-start(), calls=%async_computation.4 | async-start | bytes 5242880 | tf_op jit(solution)/shard_map/all_gather | solution.py:318
  29.5 187.5 %reduce-scatter.5.cloned.1.call-start = ((), (), s32[]{:S(2)}) async-start(), calls=%async_computation.5 | async-start | bytes 5242880 | tf_op jit(solution)/shard_map/reduce_scatter | solution.py:322
  30.5 33.2 %collective-permute-start.8 = (bf16[256,2048]{1,0:T(8,128)(2,1)S(1)}, bf16[256,2048]{1,0:T(8,128)(2,1)}, u32[]{:S(2)}, u32[]{:S(2)}) collective-permute-start(bf16[256,2048]{1,0:T(8,128)(2,1)S(1)} %bitcast.90), channel_id=1, source_target_pairs={{8,0},{16,8},{24,16},{28,24},{20,28},{12,20},{4,12},{0,4},{9,1},{1... | collective-permute-start | bytes 3145736 | tf_op jit(solution)/shard_map/ppermute | solution.py:241
  31.9 29.8 %collective-permute-start.15 = (bf16[512,256]{1,0:T(8,128)(2,1)S(1)}, bf16[512,256]{1,0:T(8,128)(2,1)}, u32[]{:S(2)}, u32[]{:S(2)}) collective-permute-start(bf16[512,256]{1,0:T(8,128)(2,1)S(1)} %copy-done.14), channel_id=1, source_target_pairs={{0,8},{8,16},{16,24},{24,28},{28,20},{20,12},{12,4},{4,0},{1,9},{9... | collective-permute-start | bytes 786440 | tf_op jit(solution)/shard_map/ppermute | solution.py:238
  32.6 29.8 %collective-permute-start.16 = (bf16[512,256]{1,0:T(8,128)(2,1)S(1)}, bf16[512,256]{1,0:T(8,128)(2,1)}, u32[]{:S(2)}, u32[]{:S(2)}) collective-permute-start(bf16[512,256]{1,0:T(8,128)(2,1)S(1)} %copy-done.14), channel_id=1, source_target_pairs={{8,0},{16,8},{24,16},{28,24},{20,28},{12,20},{4,12},{0,4},{9,1},{1... | collective-permute-start | bytes 786440 | tf_op jit(solution)/shard_map/ppermute | solution.py:241
  56.0 46.5 %collective-permute-start.9 = (bf16[256,2048]{1,0:T(8,128)(2,1)S(1)}, bf16[256,2048]{1,0:T(8,128)(2,1)}, u32[]{:S(2)}, u32[]{:S(2)}) collective-permute-start(bf16[256,2048]{1,0:T(8,128)(2,1)S(1)} %collective-permute-done.7), channel_id=1, source_target_pairs={{0,8},{8,16},{16,24},{24,28},{28,20},{20,12},{12,4},{4,0},{1,9},{9... | collective-permute-start | bytes 3145736 | tf_op jit(solution)/shard_map/ppermute | solution.py:238
  61.7 29.1 %collective-permute-start.17 = (bf16[512,256]{1,0:T(8,128)(2,1)}, bf16[512,256]{1,0:T(8,128)(2,1)}, u32[]{:S(2)}, u32[]{:S(2)}) collective-permute-start(bf16[512,256]{1,0:T(8,128)(2,1)} %collective-permute-done.15), channel_id=1, source_target_pairs={{0,8},{8,16},{16,24},{24,28},{28,20},{20,12},{12,4},{4,0},{1,9},{9... | collective-permute-start | bytes 786440 | tf_op jit(solution)/shard_map/ppermute | solution.py:238
  62.4 29.0 %collective-permute-start.18 = (bf16[512,256]{1,0:T(8,128)(2,1)}, bf16[512,256]{1,0:T(8,128)(2,1)}, u32[]{:S(2)}, u32[]{:S(2)}) collective-permute-start(bf16[512,256]{1,0:T(8,128)(2,1)} %collective-permute-done.16), channel_id=1, source_target_pairs={{8,0},{16,8},{24,16},{28,24},{20,28},{12,20},{4,12},{0,4},{9,1},{1... | collective-permute-start | bytes 786440 | tf_op jit(solution)/shard_map/ppermute | solution.py:241
  63.7 43.1 %collective-permute-start.10 = (bf16[256,2048]{1,0:T(8,128)(2,1)}, bf16[256,2048]{1,0:T(8,128)(2,1)}, u32[]{:S(2)}, u32[]{:S(2)}) collective-permute-start(bf16[256,2048]{1,0:T(8,128)(2,1)} %collective-permute-done.8), channel_id=1, source_target_pairs={{8,0},{16,8},{24,16},{28,24},{20,28},{12,20},{4,12},{0,4},{9,1},{1... | collective-permute-start | bytes 3145736 | tf_op jit(solution)/shard_map/ppermute | solution.py:241
  171.9 220.5 %all-gather.7.cloned.1.call-start = ((), (), s32[]{:S(2)}) async-start(), calls=%async_computation.6 | async-start | bytes 5242880 | tf_op jit(solution)/shard_map/all_gather | solution.py:318
  221.2 189.9 %all-gather.9.cloned.1.call-start = ((), (), s32[]{:S(2)}) async-start(), calls=%async_computation.8 | async-start | bytes 5242880 | tf_op jit(solution)/shard_map/all_gather | solution.py:318
  222.8 53.0 %collective-permute-start.23 = (bf16[256,2816]{1,0:T(8,128)(2,1)S(1)}, bf16[256,2816]{1,0:T(8,128)(2,1)}, u32[]{:S(2)}, u32[]{:S(2)}) collective-permute-start(bf16[256,2816]{1,0:T(8,128)(2,1)S(1)} %bitcast.86), channel_id=1, source_target_pairs={{0,8},{8,16},{16,24},{24,28},{28,20},{20,12},{12,4},{4,0},{1,9},{9... | collective-permute-start | bytes 4325384 | tf_op jit(solution)/shard_map/ppermute | solution.py:238
  224.3 53.0 %collective-permute-start.24 = (bf16[256,2816]{1,0:T(8,128)(2,1)S(1)}, bf16[256,2816]{1,0:T(8,128)(2,1)}, u32[]{:S(2)}, u32[]{:S(2)}) collective-permute-start(bf16[256,2816]{1,0:T(8,128)(2,1)S(1)} %bitcast.87), channel_id=1, source_target_pairs={{8,0},{16,8},{24,16},{28,24},{20,28},{12,20},{4,12},{0,4},{9,1},{1... | collective-permute-start | bytes 4325384 | tf_op jit(solution)/shard_map/ppermute | solution.py:241
  224.9 46.8 %collective-permute-start.31 = (bf16[1408,256]{1,0:T(8,128)(2,1)S(1)}, bf16[1408,256]{1,0:T(8,128)(2,1)}, u32[]{:S(2)}, u32[]{:S(2)}) collective-permute-start(bf16[1408,256]{1,0:T(8,128)(2,1)S(1)} %copy-done.13), channel_id=1, source_target_pairs={{0,8},{8,16},{16,24},{24,28},{28,20},{20,12},{12,4},{4,0},{1,9},{9... | collective-permute-start | bytes 2162696 | tf_op jit(solution)/shard_map/ppermute | solution.py:238
  226.3 46.9 %collective-permute-start.32 = (bf16[1408,256]{1,0:T(8,128)(2,1)S(1)}, bf16[1408,256]{1,0:T(8,128)(2,1)}, u32[]{:S(2)}, u32[]{:S(2)}) collective-permute-start(bf16[1408,256]{1,0:T(8,128)(2,1)S(1)} %copy-done.13), channel_id=1, source_target_pairs={{8,0},{16,8},{24,16},{28,24},{20,28},{12,20},{4,12},{0,4},{9,1},{1... | collective-permute-start | bytes 2162696 | tf_op jit(solution)/shard_map/ppermute | solution.py:241
  226.9 262.7 %reduce-scatter.9.cloned.1.call-start = ((), (), s32[]{:S(2)}) async-start(), calls=%async_computation.9 | async-start | bytes 5242880 | tf_op jit(solution)/shard_map/reduce_scatter | solution.py:322
  275.8 61.7 %collective-permute-start.25 = (bf16[256,2816]{1,0:T(8,128)(2,1)}, bf16[256,2816]{1,0:T(8,128)(2,1)S(1)}, u32[]{:S(2)}, u32[]{:S(2)}) collective-permute-start(bf16[256,2816]{1,0:T(8,128)(2,1)} %collective-permute-done.23), channel_id=1, source_target_pairs={{0,8},{8,16},{16,24},{24,28},{28,20},{20,12},{12,4},{4,0},{1,9},{9... | collective-permute-start | bytes 4325384 | tf_op jit(solution)/shard_map/ppermute | solution.py:238
  277.3 61.6 %collective-permute-start.26 = (bf16[256,2816]{1,0:T(8,128)(2,1)}, bf16[256,2816]{1,0:T(8,128)(2,1)S(1)}, u32[]{:S(2)}, u32[]{:S(2)}) collective-permute-start(bf16[256,2816]{1,0:T(8,128)(2,1)} %collective-permute-done.24), channel_id=1, source_target_pairs={{8,0},{16,8},{24,16},{28,24},{20,28},{12,20},{4,12},{0,4},{9,1},{1... | collective-permute-start | bytes 4325384 | tf_op jit(solution)/shard_map/ppermute | solution.py:241
  291.0 44.3 %collective-permute-start.35 = (bf16[1408,256]{1,0:T(8,128)(2,1)S(1)}, bf16[1408,256]{1,0:T(8,128)(2,1)S(1)}, u32[]{:S(2)}, u32[]{:S(2)}) collective-permute-start(bf16[1408,256]{1,0:T(8,128)(2,1)S(1)} %collective-permute-done.33), channel_id=1, source_target_pairs={{0,8},{8,16},{16,24},{24,28},{28,20},{20,12},{12,4},{4,0},{1,9},{9... | collective-permute-start | bytes 2162696 | tf_op jit(solution)/shard_map/ppermute | solution.py:238
  292.5 44.4 %collective-permute-start.36 = (bf16[1408,256]{1,0:T(8,128)(2,1)S(1)}, bf16[1408,256]{1,0:T(8,128)(2,1)S(1)}, u32[]{:S(2)}, u32[]{:S(2)}) collective-permute-start(bf16[1408,256]{1,0:T(8,128)(2,1)S(1)} %collective-permute-done.34), channel_id=1, source_target_pairs={{8,0},{16,8},{24,16},{28,24},{20,28},{12,20},{4,12},{0,4},{9,1},{1... | collective-permute-start | bytes 2162696 | tf_op jit(solution)/shard_map/ppermute | solution.py:241
  337.5 37.3 %collective-permute-start.27 = (bf16[256,2816]{1,0:T(8,128)(2,1)S(1)}, bf16[256,2816]{1,0:T(8,128)(2,1)S(1)}, u32[]{:S(2)}, u32[]{:S(2)}) collective-permute-start(bf16[256,2816]{1,0:T(8,128)(2,1)S(1)} %collective-permute-done.25), channel_id=1, source_target_pairs={{0,8},{8,16},{16,24},{24,28},{28,20},{20,12},{12,4},{4,0},{1,9},{9... | collective-permute-start | bytes 4325384 | tf_op jit(solution)/shard_map/ppermute | solution.py:238
  339.0 37.4 %collective-permute-start.28 = (bf16[256,2816]{1,0:T(8,128)(2,1)S(1)}, bf16[256,2816]{1,0:T(8,128)(2,1)S(1)}, u32[]{:S(2)}, u32[]{:S(2)}) collective-permute-start(bf16[256,2816]{1,0:T(8,128)(2,1)S(1)} %collective-permute-done.26), channel_id=1, source_target_pairs={{8,0},{16,8},{24,16},{28,24},{20,28},{12,20},{4,12},{0,4},{9,1},{1... | collective-permute-start | bytes 4325384 | tf_op jit(solution)/shard_map/ppermute | solution.py:241
  445.5 84.8 %all-gather.11.cloned.1.call-start = ((), (), s32[]{:S(2)}) async-start(), calls=%async_computation.10 | async-start | bytes 5242880 | tf_op jit(solution)/shard_map/all_gather | solution.py:318
  495.6 386.5 %reduce-scatter.11.cloned.1.call-start = ((), (), s32[]{:S(2)}) async-start(), calls=%async_computation.11 | async-start | bytes 5242880 | tf_op jit(solution)/shard_map/reduce_scatter | solution.py:322
  569.2 333.2 %reduce-scatter.7.cloned.1.call-start = ((), (), s32[]{:S(2)}) async-start(), calls=%async_computation.7 | async-start | bytes 5242880 | tf_op jit(solution)/shard_map/reduce_scatter | solution.py:322
  594.3 30.0 %collective-permute-start.67 = (bf16[128,2816]{1,0:T(8,128)(2,1)S(1)}, bf16[128,2816]{1,0:T(8,128)(2,1)S(1)}, u32[]{:S(2)}, u32[]{:S(2)}) collective-permute-start(bf16[128,2816]{1,0:T(8,128)(2,1)S(1)} %get-tuple-element.39), channel_id=1, source_target_pairs={{0,8},{8,16},{16,24},{24,28},{28,20},{20,12},{12,4},{4,0},{1,9},{9... | collective-permute-start | bytes 2162696 | tf_op jit(solution)/shard_map/ppermute | solution.py:238
  627.2 31.8 %collective-permute-start.68 = (bf16[128,2816]{1,0:T(8,128)(2,1)}, bf16[128,2816]{1,0:T(8,128)(2,1)S(1)}, u32[]{:S(2)}, u32[]{:S(2)}) collective-permute-start(bf16[128,2816]{1,0:T(8,128)(2,1)} %get-tuple-element.37), channel_id=1, source_target_pairs={{0,8},{8,16},{16,24},{24,28},{28,20},{20,12},{12,4},{4,0},{1,9},{9... | collective-permute-start | bytes 2162696 | tf_op jit(solution)/shard_map/ppermute | solution.py:238
  628.7 30.4 %collective-permute-start.75 = (bf16[128,2816]{1,0:T(8,128)(2,1)S(1)}, bf16[128,2816]{1,0:T(8,128)(2,1)}, u32[]{:S(2)}, u32[]{:S(2)}) collective-permute-start(bf16[128,2816]{1,0:T(8,128)(2,1)S(1)} %get-tuple-element.38), channel_id=1, source_target_pairs={{8,0},{16,8},{24,16},{28,24},{20,28},{12,20},{4,12},{0,4},{9,1},{1... | collective-permute-start | bytes 2162696 | tf_op jit(solution)/shard_map/ppermute | solution.py:241
  661.7 31.0 %collective-permute-start.69 = (bf16[128,2816]{1,0:T(8,128)(2,1)}, bf16[128,2816]{1,0:T(8,128)(2,1)S(1)}, u32[]{:S(2)}, u32[]{:S(2)}) collective-permute-start(bf16[128,2816]{1,0:T(8,128)(2,1)} %get-tuple-element.35), channel_id=1, source_target_pairs={{0,8},{8,16},{16,24},{24,28},{28,20},{20,12},{12,4},{4,0},{1,9},{9... | collective-permute-start | bytes 2162696 | tf_op jit(solution)/shard_map/ppermute | solution.py:238
  663.2 29.5 %collective-permute-start.76 = (bf16[128,2816]{1,0:T(8,128)(2,1)S(1)}, bf16[128,2816]{1,0:T(8,128)(2,1)}, u32[]{:S(2)}, u32[]{:S(2)}) collective-permute-start(bf16[128,2816]{1,0:T(8,128)(2,1)S(1)} %get-tuple-element.36), channel_id=1, source_target_pairs={{8,0},{16,8},{24,16},{28,24},{20,28},{12,20},{4,12},{0,4},{9,1},{1... | collective-permute-start | bytes 2162696 | tf_op jit(solution)/shard_map/ppermute | solution.py:241
  694.6 52.5 %collective-permute-start.70 = (bf16[128,2816]{1,0:T(8,128)(2,1)S(1)}, bf16[128,2816]{1,0:T(8,128)(2,1)S(1)}, u32[]{:S(2)}, u32[]{:S(2)}) collective-permute-start(bf16[128,2816]{1,0:T(8,128)(2,1)S(1)} %get-tuple-element.33), channel_id=1, source_target_pairs={{0,8},{8,16},{16,24},{24,28},{28,20},{20,12},{12,4},{4,0},{1,9},{9... | collective-permute-start | bytes 2162696 | tf_op jit(solution)/shard_map/ppermute | solution.py:238
  793.8 28.8 %collective-permute-start.57 = (bf16[256,256]{1,0:T(8,128)(2,1)S(1)}, bf16[256,256]{1,0:T(8,128)(2,1)S(1)}, u32[]{:S(2)}, u32[]{:S(2)}) collective-permute-start(bf16[256,256]{1,0:T(8,128)(2,1)S(1)} %get-tuple-element.80), channel_id=1, source_target_pairs={{0,8},{8,16},{16,24},{24,28},{28,20},{20,12},{12,4},{4,0},{1,9},{9... | collective-permute-start | bytes 393224 | tf_op jit(solution)/shard_map/ppermute | solution.py:238
  (119 other events, 3039.7 us)
Sparse Core Ops, SparseCore 0:
  29.6 35.2 all-gather.4
  172.0 44.9 reduce-scatter.4
  221.3 34.4 all-gather.6
  257.3 34.4 all-gather.8
  445.6 43.9 reduce-scatter.8
  495.8 34.4 all-gather.10
  569.3 44.4 reduce-scatter.10
  682.3 41.7 reduce-scatter.6

commit v2 on v1

--- a/solution.py
+++ b/solution.py
@@ -224,15 +224,14 @@
     def __init__(self, axis, count):
         order = ring_order(count)
         self.axis, self.count = axis, count
-        self.order = jnp.array(order, jnp.int32)
         self.ahead = [(order[i], order[(i + 1) % count]) for i in range(count)]
         self.behind = [(b, a) for a, b in self.ahead]
-        place = [order.index(i) for i in range(count)]
         self.me = lax.axis_index(axis)
-        self.place = jnp.array(place, jnp.int32)[self.me]
+        self.place = jnp.where(self.me % 2 == 0, self.me // 2, count - (self.me + 1) // 2)
 
     def owner(self, shift):
-        return self.order[(self.place + shift + 2 * self.count) % self.count]
+        at = (self.place + shift + 2 * self.count) % self.count
+        return jnp.where(2 * at < self.count, 2 * at, 2 * (self.count - at) - 1)
 
     def send_ahead(self, x):
         return lax.ppermute(x, self.axis, self.ahead)
@@ -241,47 +240,153 @@
         return lax.ppermute(x, self.axis, self.behind)
 
     def gather(self, x, dim):
-        size = x.shape[dim]
-        half = x.shape[0] // 2
+        return Gather(self, x, dim)
+
+    def scatter_sum(self, x, dim):
+        return ScatterSum(self, x, dim)
+
+
+def after(x, *earlier):
+    return lax.optimization_barrier((x, *earlier))[0]
+
+
+def first_kernel(at, block, whole):
+    whole[...] = block[...]
+
+
+def pair_kernel(at, left, right, before, whole):
+    @pl.when(pl.program_id(0) == 0)
+    def _():
+        whole[...] = left[...]
+
+    @pl.when(pl.program_id(0) == 1)
+    def _():
+        whole[...] = right[...]
+
+
+SMALL_COST = pl.CostEstimate(flops=0, bytes_accessed=4_000_000, transcendentals=0)
+
+
+class Gather:
+    def __init__(self, ring, x, dim):
+        self.ring, self.dim, self.half = ring, dim, x.shape[0] // 2
         shape = list(x.shape)
-        shape[dim] *= self.count
-
-        def put(whole, block, owner, row=0):
-            at = [row, 0]
-            at[dim] = at[dim] + owner * size
-            return lax.dynamic_update_slice(whole, block, at)
-
-        whole = put(jnp.zeros(shape, x.dtype), x, self.me)
-        left = right = x
-        steps = self.count // 2
-        for step in range(1, steps):
-            left, right = self.send_ahead(left), self.send_behind(right)
-            whole = put(whole, left, self.owner(-step))
-            whole = put(whole, right, self.owner(step))
-        left, right = self.send_ahead(left[:half]), self.send_behind(right[half:])
-        whole = put(whole, left, self.owner(-steps))
-        return put(whole, right, self.owner(steps), half)
-
-    def scatter_sum(self, x, dim):
+        shape[dim] *= ring.count
+        self.shape = jax.ShapeDtypeStruct(tuple(shape), x.dtype)
+        self.left = self.right = x
+        self.step, self.steps = 0, ring.count // 2
+        self.aligned = x.shape[1] % 128 == 0
+        if not self.aligned:
+            at = [0, 0]
+            at[dim] = ring.me * x.shape[dim]
+            self.whole = lax.dynamic_update_slice(jnp.zeros(shape, x.dtype), x, at)
+            return
+        to = (lambda i, at: (at[0], 0)) if self.dim == 0 else (lambda i, at: (0, at[0]))
+        self.whole = pl.pallas_call(
+            first_kernel,
+            grid_spec=pltpu.PrefetchScalarGridSpec(
+                num_scalar_prefetch=1, grid=(1,), in_specs=[pl.BlockSpec(x.shape, lambda i, at: (0, 0))],
+                out_specs=pl.BlockSpec(x.shape, to)),
+            out_shape=self.shape, cost_estimate=SMALL_COST, name="gather_first",
+        )(self.ring.me.reshape(1), x)
+
+    def hop(self, *earlier):
+        ring = self.ring
+        left, right = self.left, self.right
+        if self.step == self.steps:
+            return left, right
+        step = self.step + 1
+        if step == self.steps:
+            left, right = left[: self.half], right[self.half :]
+        if step > 1:
+            left, right, self.whole, *_ = lax.optimization_barrier((left, right, self.whole, *earlier))
+        elif earlier:
+            left, right = after(left, *earlier), after(right, *earlier)
+        left, right = ring.send_ahead(left), ring.send_behind(right)
+        if step > 1:
+            self.store()
+        self.left, self.right, self.step = left, right, step
+        return left, right
+
+    def settle(self, x):
+        x, self.whole = lax.optimization_barrier((x, self.whole))
+        return x
+
+    def result(self):
+        while self.step < self.steps:
+            self.hop()
+        self.store()
+        return self.whole
+
+    def store(self):
+        ring = self.ring
+        last = self.step == self.steps
+        if not self.aligned:
+            for block, shift in ((self.left, -self.step), (self.right, self.step)):
+                at = [self.half if last and shift > 0 else 0, 0]
+                at[self.dim] = at[self.dim] + ring.owner(shift) * self.shape.shape[self.dim] // ring.count
+                self.whole = lax.dynamic_update_slice(self.whole, block, at)
+            return
+        owners = jnp.stack([ring.owner(-self.step), ring.owner(self.step)])
+        if self.dim == 0 and last:
+            to = lambda i, at: (2 * at[i] + i, 0)
+        elif self.dim == 0:
+            to = lambda i, at: (at[i], 0)
+        elif last:
+            to = lambda i, at: (i, at[i])
+        else:
+            to = lambda i, at: (0, at[i])
+        block = pl.BlockSpec(self.left.shape, lambda i, at: (0, 0))
+        self.whole = pl.pallas_call(
+            pair_kernel,
+            grid_spec=pltpu.PrefetchScalarGridSpec(
+                num_scalar_prefetch=1, grid=(2,),
+                in_specs=[block, block, pl.BlockSpec(memory_space=pl.ANY)],
+                out_specs=pl.BlockSpec(self.left.shape, to)),
+            out_shape=self.shape, input_output_aliases={3: 0}, cost_estimate=SMALL_COST, name="gather_pair",
+        )(owners, self.left, self.right, self.whole)
+
+
+class ScatterSum:
+    def __init__(self, ring, x, dim):
+        self.ring, self.dim, self.x = ring, dim, x
         shape = list(x.shape)
-        shape[dim] //= self.count
-        size, half = shape[dim], shape[0] // 2
-        shape[0] = half
-
-        def part(shift, row):
-            at = [row, 0]
-            at[dim] = at[dim] + self.owner(shift) * size
-            return lax.dynamic_slice(x, at, shape)
-
-        left, right = part(-1, 0), part(1, half)
-        for step in range(1, self.count):
-            left, right = self.send_ahead(left), self.send_behind(right)
-            own_left, own_right = part(-1 - step, 0), part(1 + step, half)
-            if step == self.count - 1:
-                left, right = left.astype(F32), right.astype(F32)
-                own_left, own_right = own_left.astype(F32), own_right.astype(F32)
-            left, right = left + own_left, right + own_right
-        return jnp.concatenate([left, right], axis=0)
+        shape[dim] //= ring.count
+        self.size, self.half = shape[dim], shape[0] // 2
+        self.shape, self.step, self.steps = shape, 0, ring.count // 2
+        self.left = self.part(self.steps)[: self.half]
+        self.right = self.part(-self.steps)[self.half :]
+
+    def part(self, shift):
+        at = [0, 0]
+        at[self.dim] = self.ring.owner(shift) * self.size
+        return lax.dynamic_slice(self.x, at, self.shape)
+
+    def hop(self, before=(), during=()):
+        ring, left, right = self.ring, self.left, self.right
+        if self.step == self.steps:
+            return self.arrived
+        self.step += 1
+        if before:
+            left, right = after(left, *before), after(right, *before)
+        left, right = ring.send_ahead(left), ring.send_behind(right)
+        if during:
+            left, right = after(left, *during), after(right, *during)
+        self.arrived = left, right
+        shift = self.steps - self.step
+        if self.step == 1:
+            ahead, behind = self.part(shift), self.part(-shift)
+            self.left = jnp.concatenate([left + ahead[: self.half], ahead[self.half :]], axis=0)
+            self.right = jnp.concatenate([behind[: self.half], right + behind[self.half :]], axis=0)
+        elif shift:
+            self.left, self.right = left + self.part(shift), right + self.part(-shift)
+        return self.arrived
+
+    def result(self):
+        while self.step < self.steps:
+            self.hop()
+        left, right = self.arrived
+        return left.astype(F32) + right.astype(F32) + self.part(0).astype(F32)
 
 
 def gather_small(row, axis, count):
@@ -326,65 +431,127 @@
          norm_gain, group_gain, ffn_gain, cotangent):
     ring = Ring("dp", n_dp)
     seg = segment_ids[0]
-    x = tokens.astype(F32)
     part, small = norm_gain.shape[0], group_gain.shape[0]
     model = part * n_dp
     width = mixer_out.shape[0]
     hidden_width = down.shape[0]
 
-    gains = gather_small(jnp.concatenate([norm_gain, ffn_gain, group_gain]).astype(F32)[None], "dp", n_dp)
+    gain_row = jnp.concatenate([norm_gain, ffn_gain, group_gain]).astype(F32)[None]
+    in_part = mixer_in.reshape(part, 4 * width)
+    gu_part = gate_up.reshape(part, 2 * hidden_width)
+    seq = tensor_gather(tokens)
+    cot = tensor_gather(cotangent)
+    gains = gather_small(gain_row, "dp", n_dp)
     gain_in = gains[:, :part].reshape(1, model)
     gain_ffn = gains[:, part : 2 * part].reshape(1, model)
     gain_group = gains[:, 2 * part :].reshape(1, HD)
 
-    w_in = ring.gather(mixer_in.reshape(part, 4 * width), 0)
-    w_out = ring.gather(mixer_out, 1)
-    w_gu = ring.gather(gate_up.reshape(part, 2 * hidden_width), 0)
-    w_down = ring.gather(down, 1)
-
-    h1_own, r1 = norm_forward(x, gain_in)
-    h1 = tensor_gather(h1_own)
-    cot = tensor_gather(cotangent)
+    g_in, g_out = ring.gather(in_part, 0), ring.gather(mixer_out, 1)
+    done = g_out.hop()
+    done = g_in.hop(*done)
+    done = g_out.hop(*done)
+    done = g_in.hop(*done)
+    g_gu, g_down = ring.gather(gu_part, 0), ring.gather(down, 1)
+    done = g_out.hop(*done, gains)
+    h1, _ = norm_forward(after(seq, *done).astype(F32), gain_in)
+    done = g_in.hop(*done)
+    h1, g_gu.whole, g_down.whole = lax.optimization_barrier((h1, g_gu.whole, g_down.whole))
+    done = g_out.hop(*done, h1)
+    done = g_in.hop(*done)
+    w_in, w_out = g_in.result(), g_out.result()
+
+    gu1 = g_gu.hop(*done)
     proj = mm(h1, w_in, NN).astype(BF16)
     y, o, states = rec_forward(proj, seg, gain_group)
-    attn = tensor_scatter_sum(mm(y, w_out, NN).astype(BF16))
-    x2 = x + attn
+    attn_part = after(mm(y, w_out, NN).astype(BF16), *gu1)
+    gu2 = g_gu.hop(attn_part)
+    down1 = g_down.hop(attn_part)
+    attn = tensor_scatter_sum(attn_part)
+    x = tokens.astype(F32)
+    x2 = x + g_gu.settle(after(attn, *gu2, *down1))
     h2_own, r2 = norm_forward(x2, gain_ffn)
-    h2 = tensor_gather(h2_own)
-    gu = mm(h2, w_gu, NN)
+    gu3 = g_gu.hop(*down1)
+    h2 = g_gu.settle(after(tensor_gather(h2_own), *gu3))
+    gu4 = g_gu.hop()
+    down2 = g_down.hop(*gu4)
+    w_gu = g_gu.result()
+    gu = after(mm(h2, w_gu, NN), *down2)
+    down3 = g_down.hop(gu)
     gate, up = gu[:, :hidden_width], gu[:, hidden_width:]
     sg = jax.nn.sigmoid(gate)
     swish = gate * sg
     hidden = (swish * up).astype(BF16)
-    d_down = ring.scatter_sum(mm(hidden, cot, TN).astype(BF16), 1)
-    dh = mm(cot, w_down, NT)
+    d_down_part = g_down.settle(mm(hidden, cot, TN).astype(BF16))
+    s_down = ring.scatter_sum(d_down_part, 1)
+    step1 = s_down.hop()
+    down4 = g_down.hop(d_down_part)
+    w_down = g_down.result()
+    dh = mm(after(cot, d_down_part, *step1), w_down, NT)
     dgate = (dh * up * sg * (1.0 + gate * (1.0 - sg))).astype(BF16)
     dup = (dh * swish).astype(BF16)
     dgu = jnp.concatenate([dgate, dup], axis=1)
-    d_gu = ring.scatter_sum(mm(h2, dgu, TN).astype(BF16), 0)
-    dh2 = tensor_scatter_sum(mm(dgu, w_gu, NT).astype(BF16))
-    back2, d_gain_ffn = norm_backward(x2, r2, gain_ffn, dh2)
+    s_down.hop(during=(dgu,))
+    d_gu_part = mm(after(h2, s_down.left, s_down.right), dgu, TN).astype(BF16)
+    s_down.hop(during=(d_gu_part,))
+    s_gu = ring.scatter_sum(d_gu_part, 0)
+    dh2_part = mm(after(dgu, d_gu_part, s_down.left, s_down.right), w_gu, NT).astype(BF16)
+    step4 = s_down.hop(during=(dh2_part,))
+    t1 = s_gu.hop(during=(dh2_part,))
+    dh2_part = after(dh2_part, *step4, *t1)
+    dh2 = tensor_scatter_sum(dh2_part)
+    s_gu.hop()
+    d_down = after(s_down.result(), dh2_part)
+    back2, d_gain_ffn = norm_backward(x2, r2, gain_ffn, after(dh2, s_gu.left, s_gu.right, d_down))
     dx2 = cotangent.astype(F32) + back2
-    dattn = tensor_gather(dx2.astype(BF16))
-    d_out = ring.scatter_sum(mm(y, dattn, TN).astype(BF16), 1)
-    dy = mm(dattn, w_out, NT)
+    dattn_own = dx2.astype(BF16)
+    dattn = tensor_gather(dattn_own)
+    ffn_part = mm(after(hidden, dattn_own), w_down, NN).astype(BF16)
+    s_gu.hop(during=(ffn_part,))
+    dattn = after(dattn, s_gu.left, s_gu.right)
+    d_out_part = mm(y, dattn, TN).astype(BF16)
+    s_out = ring.scatter_sum(d_out_part, 1)
+    ffn = tensor_scatter_sum(after(ffn_part, dattn))
+    dy = mm(after(dattn, d_out_part), w_out, NT)
     dproj, d_group = rec_backward(proj, seg, gain_group, o, states, dy)
-    d_in = ring.scatter_sum(mm(h1, dproj, TN).astype(BF16), 0)
-    dh1 = tensor_scatter_sum(mm(dproj, w_in, NT).astype(BF16))
-    back1, d_gain_in = norm_backward(x, r1, gain_in, dh1)
+    t4 = s_gu.hop(during=(dproj,))
+    s_out.hop(during=(dproj,))
+    dproj = after(dproj, *t4, s_out.left, s_out.right)
+    s_qa = ring.scatter_sum(mm(h1, dproj[:, : 2 * width], TN).astype(BF16), 0)
+    s_out.hop(during=(s_qa.x,))
+    dh1_part = mm(after(dproj, s_qa.x, s_out.left, s_out.right), w_in, NT).astype(BF16)
+    s_out.hop(during=(dh1_part,))
+    s_qa.hop(during=(dh1_part,))
+    dh1_part = after(dh1_part, s_out.left, s_out.right, s_qa.left, s_qa.right)
+    dh1 = tensor_scatter_sum(dh1_part)
+    s_vz = ring.scatter_sum(mm(after(h1, dh1_part), dproj[:, 2 * width :], TN).astype(BF16), 0)
+    d_gate_up = after(s_gu.result(), s_vz.x)
+    d_gu = d_gate_up.reshape(part, 2, hidden_width)
+    s_out.hop(during=(s_vz.x,))
+    s_qa.hop(during=(s_vz.x, d_gu))
+    d_out = s_out.result()
+    s_vz.hop(during=(d_out,))
+    output = after((x2 + ffn).astype(BF16), s_qa.left, s_vz.left)
+    s_qa.hop(during=(output,))
+    s_vz.hop(during=(output,))
+    r1 = lax.rsqrt(jnp.mean(x * x, axis=-1, keepdims=True) + EPSILON)
+    back1, d_gain_in = norm_backward(x, r1, gain_in, after(dh1, s_qa.left, s_qa.right, s_vz.left, s_vz.right))
     d_tokens = (dx2 + back1).astype(BF16)
-    output = (x2 + tensor_scatter_sum(mm(hidden, w_down, NN).astype(BF16))).astype(BF16)
-
     d_gains = jnp.concatenate(
         [d_gain_in.reshape(n_dp, part), d_gain_ffn.reshape(n_dp, part), d_group.reshape(n_dp, small)], axis=1
     )
-    d_gains = scatter_sum_small(lax.psum(d_gains, "tensor"), "dp", n_dp)[0]
+    d_gains = lax.psum(d_gains, "tensor")
+    qa4 = s_qa.hop(during=(d_gains,))
+    s_vz.hop(during=(d_gains,))
+    d_gains = scatter_sum_small(after(d_gains, *qa4, s_vz.left, s_vz.right), "dp", n_dp)[0]
+    d_qa = s_qa.result().reshape(part, 2, width)
+    s_vz.hop(during=(d_qa,))
+    d_in = jnp.concatenate([d_qa, s_vz.result().reshape(part, 2, width)], axis=1)
     return (
         output,
         d_tokens,
-        d_in.reshape(part, 4, width),
+        d_in,
         d_out,
-        d_gu.reshape(part, 2, hidden_width),
+        d_gu,
         d_down,
         d_gains[:part],
         d_gains[2 * part :],

time: 923 us -> 755 us (0.82)
  waiting for transfers between devices: 455 us -> 248 us
  Pallas kernels: 32.9 us -> 94.8 us
  other arithmetic: 55 us -> 98.2 us
  local copies, waits for them, and re-layouts: 69.1 us -> 38.1 us
  starting transfers between devices: 120 us -> 97.4 us
  between operations: 36.7 us -> 15.2 us
    ppermute x44 -> x36, waiting for transfers between devices: 244 us -> 101 us  [send_ahead(): return lax.ppermute(x, self.axis, self.ahead)]
    pallas_call x0 -> x20, Pallas kernels: none -> 61.7 us  [the longest x16 53.1 us: store(): pl.pallas_call(pair_kernel, grid_spec=pltpu.PrefetchScalarGridSpec(num_sc...]
    reduce_scatter x4, waiting for transfers between devices: 88.7 us -> 44.3 us  [tensor_scatter_sum(): lax.psum_scatter(x, 'tensor', scatter_dimension=0, tiled=True).astype(F32)]
    dynamic_update_slice x36 -> x0, local copies, waits for them, and re-layouts: 33.9 us -> none  [put(): return lax.dynamic_update_slice(whole, block, at)]
    all_gather x4, waiting for transfers between devices: 24 us -> 0.03 us  [tensor_gather(): return lax.all_gather(x, 'tensor', axis=0, tiled=True)]
    add x28 -> x18, other arithmetic: 28.1 us -> 45.1 us  [the longest x10 30.7 us: hop(): self.left, self.right = (left + self.part(shift), right + self.part(-shift))]
    ppermute x7, waiting for transfers between devices: 1.61 us -> 17 us  [gather_small(): lax.ppermute(row, axis, [(i, (i + turn) % count) for i in range(count)])]
    slice x8 -> x13, local copies, waits for them, and re-layouts: 0.24 us -> 13.4 us  [the longest x8 8.99 us: hop(): left, right = (left[:self.half], right[self.half:])]
  transfers between devices with their start and end apart: 110 -> 94, of which waited for: 53 -> 40; matrix products, arithmetic and copies ran while one was open for 18% -> 32% of each run, Pallas kernels for 0% -> 13%
where the time goes in v2:
time: 755 us; the launch traced here: 747 us
  waiting for transfers between devices  248 us (33%)
  matrix products  144 us (19%)
  other arithmetic  98.2 us (13%)
  starting transfers between devices  97.4 us (13%)
  Pallas kernels  94.8 us (13%)
  local copies, waits for them, and re-layouts  38.1 us (5%)
  between operations  15.2 us (2%)
  blocking collectives  10.7 us (1%)
    dot_general x13, matrix products, mm(): return lax.dot_general(a, b, dims, preferred_element_type=F32)  144 us
    ppermute x36, waiting for transfers between devices, send_ahead(): return lax.ppermute(x, self.axis, self.ahead)  101 us
    ppermute x36, waiting for transfers between devices, send_behind(): return lax.ppermute(x, self.axis, self.behind)  84.4 us
    pallas_call x16, Pallas kernels, store(): pl.pallas_call(pair_kernel, grid_spec=pltpu.PrefetchScalarGridSpec(num_sc...  53.1 us
    ppermute x36, starting transfers between devices, send_ahead(): return lax.ppermute(x, self.axis, self.ahead)  48.7 us
    reduce_scatter x4, waiting for transfers between devices, tensor_scatter_sum(): lax.psum_scatter(x, 'tensor', scatter_dimension=0, tiled=True).astype(F32)  44.3 us
    add x10, other arithmetic, hop(): self.left, self.right = (left + self.part(shift), right + self.part(-shift))  30.7 us
    ppermute x36, starting transfers between devices, send_behind(): return lax.ppermute(x, self.axis, self.behind)  27.8 us
  transfers between devices with their start and end apart: 94, of which 40 were waited for; matrix products, arithmetic and copies ran while one was open for 32% of the time, Pallas kernels for 13%

profile of v2, /device:TPU:0, one launch (start us, length us, event | category | flops | bytes accessed | tf_op | source)
XLA Modules:
  0.0 747.0 jit_solution(1464411351812092028)
XLA Ops:
  12.6 4.9 collective-permute-done.left
  23.5 20.0 %collective-permute-done.2.left = bf16[256,2048]{1,0:T(8,128)(2,1)S(1)} collective-permute-done((bf16[256,2048]{1,0:T(8,128)(2,1)S(1)}, bf16[256,2048]{1,0:T(8,128)(2,1)S(1)}, u32[]{:S(2)}, u32[]{:S(2)}) %collective-permute-start.2) | collective-permute-done | bytes 1048608 | tf_op jit(solution)/shard_map/ppermute | solution.py:237
  59.4 15.6 %collective-permute-done.8 = f32[1,528]{1,0:T(1,128)S(1)} collective-permute-done((f32[1,528]{1,0:T(1,128)S(1)}, f32[1,528]{1,0:T(1,128)S(1)}, u32[]{:S(2)}, u32[]{:S(2)}) %collective-permute-start.8) | collective-permute-done | bytes 2144 | tf_op jit(solution)/shard_map/ppermute | solution.py:396
  112.1 9.3 %collective-permute-done.17.left = bf16[256,2048]{1,0:T(8,128)(2,1)S(1)} collective-permute-done((bf16[256,2048]{1,0:T(8,128)(2,1)S(1)}, bf16[256,2048]{1,0:T(8,128)(2,1)S(1)}, u32[]{:S(2)}, u32[]{:S(2)}) %collective-permute-start.17) | collective-permute-done | bytes 1048608 | tf_op jit(solution)/shard_map/ppermute | solution.py:237
  149.5 13.9 %convolution_convert_fusion.6.q_ref.a_ref.v_ref.z_ref = bf16[1024,2048]{1,0:T(8,128)(2,1)} fusion(bf16[1024,2048]{1,0:T(8,128)(2,1)} %fusion.2, bf16[2048,2048]{1,0:T(8,128)(2,1)} %gather_pair.21), kind=kOutput, calls=%fused_computation.17 | convolution fusion | flops 8592031744 | bytes 16777216 | tf_op jit(solution)/shard_map/dot_general | solution.py:20
  163.4 14.0 %mixer_forward.1 = (bf16[1024,512]{1,0:T(8,128)(2,1)}, f32[1024,512]{1,0:T(8,128)}, f32[8,128,512]{2,1,0:T(8,128)}) custom-call(s32[1024]{0:T(1024)} %bitcast.72, bf16[1024,2048]{1,0:T(8,128)(2,1)} %convolution_convert_fusion.6.q_ref.a_ref.v_ref.z_ref, bf16[1024,2048]{1,0:T(8,128)(2,1)} %convolution_convert_fusion.6.q_ref.a_ref.v_ref.z_ref, ...), custom_call_target="tpu_custom_call" | custom-call | flops 30000001024 | bytes 10000000 | tf_op jit(solution)/shard_map/mixer_forward/pallas_call | solution.py:165
  177.4 5.5 convolution_convert_fusion.5
  192.1 35.6 %reduce-scatter.5.cloned.1.call-done = bf16[256,2048]{1,0:T(8,128)(2,1)} async-done(((bf16[1024,2048]{1,0:T(8,128)(2,1)}), bf16[256,2048]{1,0:T(8,128)(2,1)}) %reduce-scatter.5.cloned.1.call-update) | async-done | bytes 1048592 | tf_op jit(solution)/shard_map/reduce_scatter | solution.py:427
  240.2 27.4 %collective-permute-done.29.left = bf16[256,2816]{1,0:T(8,128)(2,1)} collective-permute-done((bf16[256,2816]{1,0:T(8,128)(2,1)}, bf16[256,2816]{1,0:T(8,128)(2,1)}, u32[]{:S(2)}, u32[]{:S(2)}) %collective-permute-start.29) | collective-permute-done | bytes 1441824 | tf_op jit(solution)/shard_map/ppermute | solution.py:237
  277.0 10.9 %collective-permute-done.31.left = bf16[128,2816]{1,0:T(8,128)(2,1)} collective-permute-done((bf16[128,2816]{1,0:T(8,128)(2,1)S(1)}, bf16[128,2816]{1,0:T(8,128)(2,1)}, u32[]{:S(2)}, u32[]{:S(2)}) %collective-permute-start.31) | collective-permute-done | bytes 720928 | tf_op jit(solution)/shard_map/ppermute | solution.py:237
  294.9 18.8 %fusion.22 = f32[1024,2816]{1,0:T(8,128)} fusion(bf16[1024,2048]{1,0:T(8,128)(2,1)} %all-gather.7.cloned.1.call-done, bf16[2048,2816]{1,0:T(8,128)(2,1)} %gather_pair.27), kind=kOutput, calls=%fused_computation.133 | convolution fusion | flops 11811160064 | bytes 27262976 | tf_op jit(solution)/shard_map/dot_general | solution.py:20
  320.1 6.3 multiply_convert_fusion.2
  326.4 8.9 %convolution_convert_fusion.1 = bf16[1408,2048]{1,0:T(8,128)(2,1)S(1)} fusion(bf16[1024,1408]{1,0:T(8,128)(2,1)} %multiply_convert_fusion.2, bf16[1024,2048]{1,0:T(8,128)(2,1)} %all-gather.9.cloned.1.call-done), kind=kOutput, calls=%fused_computation.6 | convolution fusion | flops 5908463616 | bytes 12845056 | tf_op jit(solution)/shard_map/dot_general | solution.py:20
  340.7 17.7 %collective-permute-done.35 = bf16[704,256]{1,0:T(8,128)(2,1)S(1)} collective-permute-done((bf16[704,256]{1,0:T(8,128)(2,1)}, bf16[704,256]{1,0:T(8,128)(2,1)S(1)}, u32[]{:S(2)}, u32[]{:S(2)}) %collective-permute-start.35) | collective-permute-done | bytes 360480 | tf_op jit(solution)/shard_map/ppermute | solution.py:237
  379.8 14.1 %multiply_convert_fusion.1 = (bf16[1024,1408]{1,0:T(8,128)(2,1)S(1)}, bf16[1024,1408]{1,0:T(8,128)(2,1)S(1)}) fusion(f32[1024,2816]{1,0:T(8,128)} %fusion.22, bf16[1024,2048]{1,0:T(8,128)(2,1)} %all-gather.9.cloned.1.call-done, bf16[1408,2048]{1,0:T(8,128)(2,1)} %gather_pair.31), kind=kOutput, calls=%fused_computation.9 | convolution fusion | flops 5924323328 | bytes 27262976 | tf_op jit(solution)/shard_map/dot_general | solution.py:20
  403.4 18.8 %convolution_convert_fusion = bf16[2048,2816]{1,0:T(8,128)(2,1)} fusion(bf16[1024,2048]{1,0:T(8,128)(2,1)} %all-gather.7.cloned.1.call-done, bf16[1024,1408]{1,0:T(8,128)(2,1)} %copy-done.13, bf16[1024,1408]{1,0:T(8,128)(2,1)} %copy-done.12), kind=kOutput, calls=%fused_computation | convolution fusion | flops 11828461568 | bytes 21495808 | tf_op jit(solution)/shard_map/dot_general | solution.py:20
  432.0 15.2 %convolution_convert_fusion.2 = bf16[1024,2048]{1,0:T(8,128)(2,1)} fusion(bf16[1024,2816]{1,0:T(8,128)(2,1)} %pad_maximum_fusion, bf16[2048,2816]{1,0:T(8,128)(2,1)S(1)} %bitcast.52), kind=kOutput, calls=%fused_computation.13 | convolution fusion | flops 11813257216 | bytes 21495808 | tf_op jit(solution)/shard_map/dot_general | solution.py:20
  462.6 18.9 %collective-permute-done.50 = bf16[256,2816]{1,0:T(8,128)(2,1)} collective-permute-done((bf16[256,2816]{1,0:T(8,128)(2,1)}, bf16[256,2816]{1,0:T(8,128)(2,1)}, u32[]{:S(2)}, u32[]{:S(2)}) %collective-permute-start.50) | collective-permute-done | bytes 1441824 | tf_op jit(solution)/shard_map/ppermute | solution.py:240
  481.6 5.0 dynamic-slice_add_fusion.2
  486.5 8.7 %reduce-scatter.7.cloned.1.call-done = bf16[256,2048]{1,0:T(8,128)(2,1)} async-done(((bf16[1024,2048]{1,0:T(8,128)(2,1)}), bf16[256,2048]{1,0:T(8,128)(2,1)}) %reduce-scatter.7.cloned.1.call-update) | async-done | bytes 1048592 | tf_op jit(solution)/shard_map/reduce_scatter | solution.py:427
  502.5 11.0 %convolution_convert_fusion.4 = bf16[1024,2048]{1,0:T(8,128)(2,1)} fusion(bf16[1024,1408]{1,0:T(8,128)(2,1)} %multiply_convert_fusion.2, bf16[1408,2048]{1,0:T(8,128)(2,1)} %gather_pair.31), kind=kOutput, calls=%fused_computation.15 | convolution fusion | flops 5907677184 | bytes 12845056 | tf_op jit(solution)/shard_map/dot_general | solution.py:20
  513.5 20.6 %collective-permute-done.52 = bf16[256,2816]{1,0:T(8,128)(2,1)} collective-permute-done((bf16[256,2816]{1,0:T(8,128)(2,1)}, bf16[256,2816]{1,0:T(8,128)(2,1)}, u32[]{:S(2)}, u32[]{:S(2)}) %collective-permute-start.52) | collective-permute-done | bytes 1441824 | tf_op jit(solution)/shard_map/ppermute | solution.py:240
  535.3 4.9 dynamic-slice_add_fusion
  549.0 6.5 fusion.23.dy_ref
  556.1 19.1 %mixer_backward.1 = (bf16[1024,2048]{1,0:T(8,128)(2,1)}, f32[1,128]{1,0:T(1,128)}) custom-call(s32[1024]{0:T(1024)} %bitcast.73, bf16[1024,2048]{1,0:T(8,128)(2,1)} %convolution_convert_fusion.6.q_ref.a_ref.v_ref.z_ref, bf16[1024,2048]{1,0:T(8,128)(2,1)} %convolution_convert_fusion.6.q_ref.a_ref.v_ref.z_ref, ...), custom_call_target="tpu_custom_call" | custom-call | flops 60000002048 | bytes 14000000 | tf_op jit(solution)/shard_map/mixer_backward/pallas_call | solution.py:192
  584.1 8.2 %convolution_convert_fusion.8 = bf16[2048,1024]{0,1:T(8,128)(2,1)S(1)} fusion(bf16[1024,2048]{1,0:T(8,128)(2,1)} %fusion.2, bf16[1024,2048]{1,0:T(8,128)(2,1)} %get-tuple-element.205), kind=kOutput, calls=%fused_computation.19 | convolution fusion | flops 4297064448 | bytes 10485760 | tf_op jit(solution)/shard_map/dot_general | solution.py:20
  595.8 10.4 %convolution_convert_fusion.3 = bf16[1024,2048]{1,0:T(8,128)(2,1)} fusion(bf16[1024,2048]{1,0:T(8,128)(2,1)S(1)} %copy-done.43, bf16[2048,2048]{1,0:T(8,128)(2,1)S(1)} %bitcast.54), kind=kOutput, calls=%fused_computation.14 | convolution fusion | flops 8592031744 | bytes 16777216 | tf_op jit(solution)/shard_map/dot_general | solution.py:20
  624.5 8.1 %convolution_convert_fusion.7 = bf16[2048,1024]{0,1:T(8,128)(2,1)S(1)} fusion(bf16[1024,2048]{1,0:T(8,128)(2,1)} %fusion.2, bf16[1024,2048]{1,0:T(8,128)(2,1)} %get-tuple-element.205), kind=kOutput, calls=%fused_computation.18 | convolution fusion | flops 4297064448 | bytes 10485760 | tf_op jit(solution)/shard_map/dot_general | solution.py:20
  661.0 8.7 %collective-permute-done.69 = bf16[256,1024]{0,1:T(8,128)(2,1)} collective-permute-done((bf16[256,1024]{0,1:T(8,128)(2,1)}, bf16[256,1024]{0,1:T(8,128)(2,1)}, u32[]{:S(2)}, u32[]{:S(2)}) %collective-permute-start.69) | collective-permute-done | bytes 524320 | tf_op jit(solution)/shard_map/ppermute | solution.py:240
  669.8 6.7 collective-permute-done.72
  692.2 10.7 %psum.7 = f32[8,528]{1,0:T(8,128)S(1)} all-reduce(f32[8,528]{1,0:T(8,128)S(1)} %pad_maximum_fusion.12), channel_id=1, replica_groups=mesh['dp'=8,'tensor'=4] {'tensor'}, use_global_device_ids=true, to_apply=%region_11.12 | all-reduce | flops 4224 | bytes 33792 | tf_op jit(solution)/shard_map/psum | solution.py:542
  726.8 7.3 collective-permute-done.78
  (403 shorter events, 320.0 us)
Async XLA Ops:
  7.2 98.5 %all-gather.5.cloned.1.call-start = ((), (), s32[]{:S(2)}) async-start(), calls=%async_computation.4 | async-start | bytes 5242880 | tf_op jit(solution)/shard_map/all_gather | solution.py:423
  7.9 219.8 %reduce-scatter.5.cloned.1.call-start = ((), (), s32[]{:S(2)}) async-start(), calls=%async_computation.5 | async-start | bytes 5242880 | tf_op jit(solution)/shard_map/reduce_scatter | solution.py:427
  53.0 32.7 %collective-permute-start.6 = (bf16[256,2048]{1,0:T(8,128)(2,1)}, bf16[256,2048]{1,0:T(8,128)(2,1)S(1)}, u32[]{:S(2)}, u32[]{:S(2)}) collective-permute-start(bf16[256,2048]{1,0:T(8,128)(2,1)} %copy-done.21), channel_id=1, source_target_pairs={{0,8},{8,16},{16,24},{24,28},{28,20},{20,12},{12,4},{4,0},{1,9},{9... | collective-permute-start | bytes 3145736 | tf_op jit(solution)/shard_map/ppermute | solution.py:237
  54.6 31.2 %collective-permute-start.7 = (bf16[256,2048]{1,0:T(8,128)(2,1)}, bf16[256,2048]{1,0:T(8,128)(2,1)}, u32[]{:S(2)}, u32[]{:S(2)}) collective-permute-start(bf16[256,2048]{1,0:T(8,128)(2,1)} %copy-done.22), channel_id=1, source_target_pairs={{8,0},{16,8},{24,16},{28,24},{20,28},{12,20},{4,12},{0,4},{9,1},{1... | collective-permute-start | bytes 3145736 | tf_op jit(solution)/shard_map/ppermute | solution.py:240
  144.3 38.7 %collective-permute-start.23 = (bf16[256,2816]{1,0:T(8,128)(2,1)S(1)}, bf16[256,2816]{1,0:T(8,128)(2,1)}, u32[]{:S(2)}, u32[]{:S(2)}) collective-permute-start(bf16[256,2816]{1,0:T(8,128)(2,1)S(1)} %bitcast.56), channel_id=1, source_target_pairs={{0,8},{8,16},{16,24},{24,28},{28,20},{20,12},{12,4},{4,0},{1,9},{9... | collective-permute-start | bytes 4325384 | tf_op jit(solution)/shard_map/ppermute | solution.py:237
  146.4 36.6 %collective-permute-start.24 = (bf16[256,2816]{1,0:T(8,128)(2,1)S(1)}, bf16[256,2816]{1,0:T(8,128)(2,1)}, u32[]{:S(2)}, u32[]{:S(2)}) collective-permute-start(bf16[256,2816]{1,0:T(8,128)(2,1)S(1)} %bitcast.57), channel_id=1, source_target_pairs={{8,0},{16,8},{24,16},{28,24},{20,28},{12,20},{4,12},{0,4},{9,1},{1... | collective-permute-start | bytes 4325384 | tf_op jit(solution)/shard_map/ppermute | solution.py:240
  183.0 87.8 %all-gather.7.cloned.1.call-start = ((), (), s32[]{:S(2)}) async-start(), calls=%async_computation.6 | async-start | bytes 5242880 | tf_op jit(solution)/shard_map/all_gather | solution.py:423
  183.0 46.3 %collective-permute-start.25 = (bf16[256,2816]{1,0:T(8,128)(2,1)}, bf16[256,2816]{1,0:T(8,128)(2,1)S(1)}, u32[]{:S(2)}, u32[]{:S(2)}) collective-permute-start(bf16[256,2816]{1,0:T(8,128)(2,1)} %collective-permute-done.23.left), channel_id=1, source_target_pairs={{0,8},{8,16},{16,24},{24,28},{28,20},{20,12},{12,4},{4,0},{1,9},{9... | collective-permute-start | bytes 4325384 | tf_op jit(solution)/shard_map/ppermute | solution.py:237
  185.1 46.4 %collective-permute-start.26 = (bf16[256,2816]{1,0:T(8,128)(2,1)}, bf16[256,2816]{1,0:T(8,128)(2,1)}, u32[]{:S(2)}, u32[]{:S(2)}) collective-permute-start(bf16[256,2816]{1,0:T(8,128)(2,1)} %collective-permute-done.24.right), channel_id=1, source_target_pairs={{8,0},{16,8},{24,16},{28,24},{20,28},{12,20},{4,12},{0,4},{9,1},{1... | collective-permute-start | bytes 4325384 | tf_op jit(solution)/shard_map/ppermute | solution.py:240
  185.1 44.1 %collective-permute-start.27 = (bf16[1408,256]{1,0:T(8,128)(2,1)}, bf16[1408,256]{1,0:T(8,128)(2,1)S(1)}, u32[]{:S(2)}, u32[]{:S(2)}) collective-permute-start(bf16[1408,256]{1,0:T(8,128)(2,1)} %block.3), channel_id=1, source_target_pairs={{0,8},{8,16},{16,24},{24,28},{28,20},{20,12},{12,4},{4,0},{1,9},{9... | collective-permute-start | bytes 2162696 | tf_op jit(solution)/shard_map/ppermute | solution.py:237
  187.2 42.1 %collective-permute-start.28 = (bf16[1408,256]{1,0:T(8,128)(2,1)}, bf16[1408,256]{1,0:T(8,128)(2,1)S(1)}, u32[]{:S(2)}, u32[]{:S(2)}) collective-permute-start(bf16[1408,256]{1,0:T(8,128)(2,1)} %block.3), channel_id=1, source_target_pairs={{8,0},{16,8},{24,16},{28,24},{20,28},{12,20},{4,12},{0,4},{9,1},{1... | collective-permute-start | bytes 2162696 | tf_op jit(solution)/shard_map/ppermute | solution.py:240
  233.8 92.6 %all-gather.9.cloned.1.call-start = ((), (), s32[]{:S(2)}) async-start(), calls=%async_computation.7 | async-start | bytes 5242880 | tf_op jit(solution)/shard_map/all_gather | solution.py:423
  233.9 33.7 %collective-permute-start.29 = (bf16[256,2816]{1,0:T(8,128)(2,1)}, bf16[256,2816]{1,0:T(8,128)(2,1)}, u32[]{:S(2)}, u32[]{:S(2)}) collective-permute-start(bf16[256,2816]{1,0:T(8,128)(2,1)} %copy-done.19), channel_id=1, source_target_pairs={{0,8},{8,16},{16,24},{24,28},{28,20},{20,12},{12,4},{4,0},{1,9},{9... | collective-permute-start | bytes 4325384 | tf_op jit(solution)/shard_map/ppermute | solution.py:237
  235.4 33.4 %collective-permute-start.30 = (bf16[256,2816]{1,0:T(8,128)(2,1)}, bf16[256,2816]{1,0:T(8,128)(2,1)}, u32[]{:S(2)}, u32[]{:S(2)}) collective-permute-start(bf16[256,2816]{1,0:T(8,128)(2,1)} %collective-permute-done.26.right), channel_id=1, source_target_pairs={{8,0},{16,8},{24,16},{28,24},{20,28},{12,20},{4,12},{0,4},{9,1},{1... | collective-permute-start | bytes 4325384 | tf_op jit(solution)/shard_map/ppermute | solution.py:240
  236.0 259.3 %reduce-scatter.7.cloned.1.call-start = ((), (), s32[]{:S(2)}) async-start(), calls=%async_computation.8 | async-start | bytes 5242880 | tf_op jit(solution)/shard_map/reduce_scatter | solution.py:427
  289.3 27.6 %collective-permute-start.33 = (bf16[1408,256]{1,0:T(8,128)(2,1)}, bf16[1408,256]{1,0:T(8,128)(2,1)}, u32[]{:S(2)}, u32[]{:S(2)}) collective-permute-start(bf16[1408,256]{1,0:T(8,128)(2,1)} %copy-done.23), channel_id=1, source_target_pairs={{0,8},{8,16},{16,24},{24,28},{28,20},{20,12},{12,4},{4,0},{1,9},{9... | collective-permute-start | bytes 2162696 | tf_op jit(solution)/shard_map/ppermute | solution.py:237
  290.8 26.1 %collective-permute-start.34 = (bf16[1408,256]{1,0:T(8,128)(2,1)}, bf16[1408,256]{1,0:T(8,128)(2,1)}, u32[]{:S(2)}, u32[]{:S(2)}) collective-permute-start(bf16[1408,256]{1,0:T(8,128)(2,1)} %copy-done.24), channel_id=1, source_target_pairs={{8,0},{16,8},{24,16},{28,24},{20,28},{12,20},{4,12},{0,4},{9,1},{1... | collective-permute-start | bytes 2162696 | tf_op jit(solution)/shard_map/ppermute | solution.py:240
  335.3 26.2 %collective-permute-start.37 = (bf16[1408,256]{1,0:T(8,128)(2,1)}, bf16[1408,256]{1,0:T(8,128)(2,1)S(1)}, u32[]{:S(2)}, u32[]{:S(2)}) collective-permute-start(bf16[1408,256]{1,0:T(8,128)(2,1)} %collective-permute-done.33.left), channel_id=1, source_target_pairs={{0,8},{8,16},{16,24},{24,28},{28,20},{20,12},{12,4},{4,0},{1,9},{9... | collective-permute-start | bytes 2162696 | tf_op jit(solution)/shard_map/ppermute | solution.py:237
  336.9 25.4 %collective-permute-start.38 = (bf16[1408,256]{1,0:T(8,128)(2,1)}, bf16[1408,256]{1,0:T(8,128)(2,1)}, u32[]{:S(2)}, u32[]{:S(2)}) collective-permute-start(bf16[1408,256]{1,0:T(8,128)(2,1)} %collective-permute-done.34.right), channel_id=1, source_target_pairs={{8,0},{16,8},{24,16},{28,24},{20,28},{12,20},{4,12},{0,4},{9,1},{1... | collective-permute-start | bytes 2162696 | tf_op jit(solution)/shard_map/ppermute | solution.py:240
  367.0 31.0 %collective-permute-start.42 = (bf16[1408,256]{1,0:T(8,128)(2,1)}, bf16[1408,256]{1,0:T(8,128)(2,1)}, u32[]{:S(2)}, u32[]{:S(2)}) collective-permute-start(bf16[1408,256]{1,0:T(8,128)(2,1)} %pad_maximum_fusion.5), channel_id=1, source_target_pairs={{8,0},{16,8},{24,16},{28,24},{20,28},{12,20},{4,12},{0,4},{9,1},{1... | collective-permute-start | bytes 2162696 | tf_op jit(solution)/shard_map/ppermute | solution.py:240
  368.3 29.8 %collective-permute-start.41 = (bf16[1408,256]{1,0:T(8,128)(2,1)}, bf16[1408,256]{1,0:T(8,128)(2,1)}, u32[]{:S(2)}, u32[]{:S(2)}) collective-permute-start(bf16[1408,256]{1,0:T(8,128)(2,1)} %pad_maximum_fusion.4), channel_id=1, source_target_pairs={{0,8},{8,16},{16,24},{24,28},{28,20},{20,12},{12,4},{4,0},{1,9},{9... | collective-permute-start | bytes 2162696 | tf_op jit(solution)/shard_map/ppermute | solution.py:237
  401.4 25.4 %collective-permute-start.44 = (bf16[1408,256]{1,0:T(8,128)(2,1)}, bf16[1408,256]{1,0:T(8,128)(2,1)S(1)}, u32[]{:S(2)}, u32[]{:S(2)}) collective-permute-start(bf16[1408,256]{1,0:T(8,128)(2,1)} %get-tuple-element.253), channel_id=1, source_target_pairs={{8,0},{16,8},{24,16},{28,24},{20,28},{12,20},{4,12},{0,4},{9,1},{1... | collective-permute-start | bytes 2162696 | tf_op jit(solution)/shard_map/ppermute | solution.py:240
  402.1 24.6 %collective-permute-start.43 = (bf16[1408,256]{1,0:T(8,128)(2,1)}, bf16[1408,256]{1,0:T(8,128)(2,1)}, u32[]{:S(2)}, u32[]{:S(2)}) collective-permute-start(bf16[1408,256]{1,0:T(8,128)(2,1)} %get-tuple-element.254), channel_id=1, source_target_pairs={{0,8},{8,16},{16,24},{24,28},{28,20},{20,12},{12,4},{4,0},{1,9},{9... | collective-permute-start | bytes 2162696 | tf_op jit(solution)/shard_map/ppermute | solution.py:237
  452.8 89.4 %all-gather.11.cloned.1.call-start = ((), (), s32[]{:S(2)}) async-start(), calls=%async_computation.9 | async-start | bytes 5242880 | tf_op jit(solution)/shard_map/all_gather | solution.py:423
  456.7 24.9 %collective-permute-start.50 = (bf16[256,2816]{1,0:T(8,128)(2,1)}, bf16[256,2816]{1,0:T(8,128)(2,1)}, u32[]{:S(2)}, u32[]{:S(2)}) collective-permute-start(bf16[256,2816]{1,0:T(8,128)(2,1)} %pad_maximum_fusion.3), channel_id=1, source_target_pairs={{8,0},{16,8},{24,16},{28,24},{20,28},{12,20},{4,12},{0,4},{9,1},{1... | collective-permute-start | bytes 4325384 | tf_op jit(solution)/shard_map/ppermute | solution.py:240
  500.3 158.2 %reduce-scatter.9.cloned.1.call-start = ((), (), s32[]{:S(2)}) async-start(), calls=%async_computation.10 | async-start | bytes 5242880 | tf_op jit(solution)/shard_map/reduce_scatter | solution.py:427
  500.4 33.7 %collective-permute-start.52 = (bf16[256,2816]{1,0:T(8,128)(2,1)}, bf16[256,2816]{1,0:T(8,128)(2,1)}, u32[]{:S(2)}, u32[]{:S(2)}) collective-permute-start(bf16[256,2816]{1,0:T(8,128)(2,1)} %get-tuple-element.243), channel_id=1, source_target_pairs={{8,0},{16,8},{24,16},{28,24},{20,28},{12,20},{4,12},{0,4},{9,1},{1... | collective-permute-start | bytes 4325384 | tf_op jit(solution)/shard_map/ppermute | solution.py:240
  501.9 33.4 %collective-permute-start.51 = (bf16[256,2816]{1,0:T(8,128)(2,1)}, bf16[256,2816]{1,0:T(8,128)(2,1)}, u32[]{:S(2)}, u32[]{:S(2)}) collective-permute-start(bf16[256,2816]{1,0:T(8,128)(2,1)} %get-tuple-element.244), channel_id=1, source_target_pairs={{0,8},{8,16},{16,24},{24,28},{28,20},{20,12},{12,4},{4,0},{1,9},{9... | collective-permute-start | bytes 4325384 | tf_op jit(solution)/shard_map/ppermute | solution.py:237
  540.2 37.8 %collective-permute-start.53 = (bf16[256,2816]{1,0:T(8,128)(2,1)}, bf16[256,2816]{1,0:T(8,128)(2,1)}, u32[]{:S(2)}, u32[]{:S(2)}) collective-permute-start(bf16[256,2816]{1,0:T(8,128)(2,1)} %get-tuple-element.242), channel_id=1, source_target_pairs={{0,8},{8,16},{16,24},{24,28},{28,20},{20,12},{12,4},{4,0},{1,9},{9... | collective-permute-start | bytes 4325384 | tf_op jit(solution)/shard_map/ppermute | solution.py:237
  540.8 37.3 %collective-permute-start.54 = (bf16[256,2816]{1,0:T(8,128)(2,1)}, bf16[256,2816]{1,0:T(8,128)(2,1)}, u32[]{:S(2)}, u32[]{:S(2)}) collective-permute-start(bf16[256,2816]{1,0:T(8,128)(2,1)} %get-tuple-element.241), channel_id=1, source_target_pairs={{8,0},{16,8},{24,16},{28,24},{20,28},{12,20},{4,12},{0,4},{9,1},{1... | collective-permute-start | bytes 4325384 | tf_op jit(solution)/shard_map/ppermute | solution.py:240
  548.5 138.9 %reduce-scatter.11.cloned.1.call-start = ((), (), s32[]{:S(2)}) async-start(), calls=%async_computation.11 | async-start | bytes 5242880 | tf_op jit(solution)/shard_map/reduce_scatter | solution.py:427
  649.1 27.4 %collective-permute-start.70 = (bf16[256,1024]{0,1:T(8,128)(2,1)}, bf16[256,1024]{0,1:T(8,128)(2,1)}, u32[]{:S(2)}, u32[]{:S(2)}) collective-permute-start(bf16[256,1024]{0,1:T(8,128)(2,1)} %pad_maximum_fusion.8), channel_id=1, source_target_pairs={{0,8},{8,16},{16,24},{24,28},{28,20},{20,12},{12,4},{4,0},{1,9},{9... | collective-permute-start | bytes 1572872 | tf_op jit(solution)/shard_map/ppermute | solution.py:237
  (111 other events, 1445.7 us)
Sparse Core Ops, SparseCore 0:
  9.6 37.1 all-gather.4
  183.1 44.5 reduce-scatter.4
  233.9 34.4 all-gather.6
  270.0 34.4 all-gather.8
  453.0 42.2 reduce-scatter.6
  500.5 34.4 all-gather.10
  548.6 43.6 reduce-scatter.8
  621.6 44.1 reduce-scatter.10

commit v3 on v2

--- a/solution.py
+++ b/solution.py
@@ -274,7 +274,7 @@
         shape[dim] *= ring.count
         self.shape = jax.ShapeDtypeStruct(tuple(shape), x.dtype)
         self.left = self.right = x
-        self.step, self.steps = 0, ring.count // 2
+        self.step, self.steps, self.pending = 0, ring.count // 2, False
         self.aligned = x.shape[1] % 128 == 0
         if not self.aligned:
             at = [0, 0]
@@ -301,12 +301,22 @@
         if step > 1:
             left, right, self.whole, *_ = lax.optimization_barrier((left, right, self.whole, *earlier))
         elif earlier:
-            left, right = after(left, *earlier), after(right, *earlier)
+            left, right, *_ = lax.optimization_barrier((left, right, *earlier))
         left, right = ring.send_ahead(left), ring.send_behind(right)
         if step > 1:
             self.store()
-        self.left, self.right, self.step = left, right, step
+        self.left, self.right, self.step, self.pending = left, right, step, True
         return left, right
+
+    def halves(self):
+        if self.step + 1 == self.steps:
+            return self.left[: self.half], self.right[self.half :]
+        return self.left, self.right
+
+    def send(self, left, right):
+        left, right = self.ring.send_ahead(left), self.ring.send_behind(right)
+        self.store()
+        self.left, self.right, self.step, self.pending = left, right, self.step + 1, True
 
     def settle(self, x):
         x, self.whole = lax.optimization_barrier((x, self.whole))
@@ -319,6 +329,9 @@
         return self.whole
 
     def store(self):
+        if not self.pending:
+            return
+        self.pending = False
         ring = self.ring
         last = self.step == self.steps
         if not self.aligned:
@@ -347,6 +360,16 @@
         )(owners, self.left, self.right, self.whole)
 
 
+def hop_together(one, two):
+    if one.step == one.steps:
+        return
+    blocks = *one.halves(), *two.halves()
+    if one.step:
+        *blocks, one.whole, two.whole = lax.optimization_barrier((*blocks, one.whole, two.whole))
+    one.send(*blocks[:2])
+    two.send(*blocks[2:])
+
+
 class ScatterSum:
     def __init__(self, ring, x, dim):
         self.ring, self.dim, self.x = ring, dim, x
@@ -367,17 +390,16 @@
         if self.step == self.steps:
             return self.arrived
         self.step += 1
-        if before:
-            left, right = after(left, *before), after(right, *before)
+        left, right, *_ = lax.optimization_barrier((left, right, *before))
         left, right = ring.send_ahead(left), ring.send_behind(right)
-        if during:
-            left, right = after(left, *during), after(right, *during)
+        left, right, *_ = lax.optimization_barrier((left, right, *during))
         self.arrived = left, right
         shift = self.steps - self.step
         if self.step == 1:
             ahead, behind = self.part(shift), self.part(-shift)
-            self.left = jnp.concatenate([left + ahead[: self.half], ahead[self.half :]], axis=0)
-            self.right = jnp.concatenate([behind[: self.half], right + behind[self.half :]], axis=0)
+            rest, zero = ahead.shape[0] - self.half, jnp.zeros((), left.dtype)
+            self.left = lax.pad(left, zero, ((0, rest, 0), (0, 0, 0))) + ahead
+            self.right = lax.pad(right, zero, ((self.half, 0, 0), (0, 0, 0))) + behind
         elif shift:
             self.left, self.right = left + self.part(shift), right + self.part(-shift)
         return self.arrived
@@ -400,11 +422,16 @@
 
 def scatter_sum_small(rows, axis, count):
     me = lax.axis_index(axis)
-    total = lax.dynamic_slice_in_dim(rows, me, 1, 0)
-    for turn in range(1, count):
-        mine = lax.dynamic_slice_in_dim(rows, (me + turn) % count, 1, 0)
-        total = total + lax.ppermute(mine, axis, [(i, (i + turn) % count) for i in range(count)])
-    return total
+    if count & (count - 1):
+        return lax.dynamic_slice_in_dim(lax.psum(rows, axis), me, 1, 0)
+    while count > 1:
+        count //= 2
+        side = me // count % 2
+        mine = lax.dynamic_slice_in_dim(rows, side * count, count, 0)
+        other = lax.dynamic_slice_in_dim(rows, (1 - side) * count, count, 0)
+        whole = lax.axis_size(axis)
+        rows = mine + lax.ppermute(other, axis, [(i, i ^ count) for i in range(whole)])
+    return rows
 
 
 def norm_forward(values, gain):
@@ -436,57 +463,59 @@
     width = mixer_out.shape[0]
     hidden_width = down.shape[0]
 
-    gain_row = jnp.concatenate([norm_gain, ffn_gain, group_gain]).astype(F32)[None]
     in_part = mixer_in.reshape(part, 4 * width)
     gu_part = gate_up.reshape(part, 2 * hidden_width)
+    extra = 32
+    gain_rows = jnp.concatenate([norm_gain, ffn_gain, group_gain])
+    gain_rows = jnp.pad(gain_rows, (0, extra * mixer_out.shape[1] - gain_rows.shape[0]))
+    out_part = jnp.concatenate([mixer_out, gain_rows.reshape(extra, mixer_out.shape[1])], axis=0)
     seq = tensor_gather(tokens)
     cot = tensor_gather(cotangent)
-    gains = gather_small(gain_row, "dp", n_dp)
+
+    g_in, g_out = ring.gather(in_part, 0), ring.gather(out_part, 1)
+    hop_together(g_out, g_in)
+    g_gu, g_down = ring.gather(gu_part, 0), ring.gather(down, 1)
+    hop_together(g_out, g_in)
+    g_in.left, g_gu.whole, g_down.whole = lax.optimization_barrier((g_in.left, g_gu.whole, g_down.whole))
+    while g_out.step < g_out.steps:
+        hop_together(g_out, g_in)
+    done = (g_out.left, g_out.right, g_in.left, g_in.right)
+    w_out = g_out.result()
+    gains = w_out[width:].reshape(extra, n_dp, -1).transpose(1, 0, 2).reshape(n_dp, -1).astype(F32)
+    w_out = w_out[:width]
     gain_in = gains[:, :part].reshape(1, model)
     gain_ffn = gains[:, part : 2 * part].reshape(1, model)
-    gain_group = gains[:, 2 * part :].reshape(1, HD)
-
-    g_in, g_out = ring.gather(in_part, 0), ring.gather(mixer_out, 1)
-    done = g_out.hop()
-    done = g_in.hop(*done)
-    done = g_out.hop(*done)
-    done = g_in.hop(*done)
-    g_gu, g_down = ring.gather(gu_part, 0), ring.gather(down, 1)
-    done = g_out.hop(*done, gains)
-    h1, _ = norm_forward(after(seq, *done).astype(F32), gain_in)
-    done = g_in.hop(*done)
-    h1, g_gu.whole, g_down.whole = lax.optimization_barrier((h1, g_gu.whole, g_down.whole))
-    done = g_out.hop(*done, h1)
-    done = g_in.hop(*done)
-    w_in, w_out = g_in.result(), g_out.result()
+    gain_group = gains[:, 2 * part : 2 * part + small].reshape(1, HD)
+    h1, _ = norm_forward(seq.astype(F32), gain_in)
+    w_in = g_in.result()
 
     gu1 = g_gu.hop(*done)
+    down1 = g_down.hop(*done)
     proj = mm(h1, w_in, NN).astype(BF16)
     y, o, states = rec_forward(proj, seg, gain_group)
-    attn_part = after(mm(y, w_out, NN).astype(BF16), *gu1)
+    attn_part = after(mm(y, w_out, NN).astype(BF16), *gu1, *down1)
     gu2 = g_gu.hop(attn_part)
-    down1 = g_down.hop(attn_part)
+    down2 = g_down.hop(attn_part)
     attn = tensor_scatter_sum(attn_part)
     x = tokens.astype(F32)
-    x2 = x + g_gu.settle(after(attn, *gu2, *down1))
+    x2 = x + g_down.settle(g_gu.settle(after(attn, *gu2, *down2)))
     h2_own, r2 = norm_forward(x2, gain_ffn)
-    gu3 = g_gu.hop(*down1)
-    h2 = g_gu.settle(after(tensor_gather(h2_own), *gu3))
+    gu3 = g_gu.hop()
+    g_down.store()
+    h2 = g_down.settle(g_gu.settle(after(tensor_gather(h2_own), *gu3)))
     gu4 = g_gu.hop()
-    down2 = g_down.hop(*gu4)
+    down3 = g_down.hop(*gu3)
     w_gu = g_gu.result()
-    gu = after(mm(h2, w_gu, NN), *down2)
-    down3 = g_down.hop(gu)
+    gu = after(mm(h2, w_gu, NN), *down3)
+    down4 = g_down.hop(gu)
     gate, up = gu[:, :hidden_width], gu[:, hidden_width:]
     sg = jax.nn.sigmoid(gate)
     swish = gate * sg
     hidden = (swish * up).astype(BF16)
-    d_down_part = g_down.settle(mm(hidden, cot, TN).astype(BF16))
+    d_down_part = after(mm(hidden, cot, TN).astype(BF16), *down4)
     s_down = ring.scatter_sum(d_down_part, 1)
-    step1 = s_down.hop()
-    down4 = g_down.hop(d_down_part)
     w_down = g_down.result()
-    dh = mm(after(cot, d_down_part, *step1), w_down, NT)
+    dh = mm(after(cot, s_down.left, s_down.right), w_down, NT)
     dgate = (dh * up * sg * (1.0 + gate * (1.0 - sg))).astype(BF16)
     dup = (dh * swish).astype(BF16)
     dgu = jnp.concatenate([dgate, dup], axis=1)
@@ -494,57 +523,58 @@
     d_gu_part = mm(after(h2, s_down.left, s_down.right), dgu, TN).astype(BF16)
     s_down.hop(during=(d_gu_part,))
     s_gu = ring.scatter_sum(d_gu_part, 0)
-    dh2_part = mm(after(dgu, d_gu_part, s_down.left, s_down.right), w_gu, NT).astype(BF16)
-    step4 = s_down.hop(during=(dh2_part,))
+    dh2_part = mm(after(dgu, s_gu.left, s_gu.right, s_down.left, s_down.right), w_gu, NT).astype(BF16)
     t1 = s_gu.hop(during=(dh2_part,))
-    dh2_part = after(dh2_part, *step4, *t1)
+    s_down.hop(during=(dh2_part,))
+    dh2_part = after(dh2_part, s_down.left, s_down.right)
     dh2 = tensor_scatter_sum(dh2_part)
+    step4 = s_down.hop(during=(s_gu.left, s_gu.right))
     s_gu.hop()
-    d_down = after(s_down.result(), dh2_part)
-    back2, d_gain_ffn = norm_backward(x2, r2, gain_ffn, after(dh2, s_gu.left, s_gu.right, d_down))
+    back2, d_gain_ffn = norm_backward(x2, r2, gain_ffn, after(dh2, s_gu.left, s_gu.right, *step4))
     dx2 = cotangent.astype(F32) + back2
     dattn_own = dx2.astype(BF16)
     dattn = tensor_gather(dattn_own)
+    d_down = after(s_down.result(), dattn_own)
     ffn_part = mm(after(hidden, dattn_own), w_down, NN).astype(BF16)
-    s_gu.hop(during=(ffn_part,))
+    s_gu.hop(during=(ffn_part, d_down))
     dattn = after(dattn, s_gu.left, s_gu.right)
     d_out_part = mm(y, dattn, TN).astype(BF16)
     s_out = ring.scatter_sum(d_out_part, 1)
     ffn = tensor_scatter_sum(after(ffn_part, dattn))
     dy = mm(after(dattn, d_out_part), w_out, NT)
-    dproj, d_group = rec_backward(proj, seg, gain_group, o, states, dy)
+    dproj, d_group = rec_backward(proj, seg, gain_group, o, states, after(dy, s_out.left, s_out.right))
     t4 = s_gu.hop(during=(dproj,))
     s_out.hop(during=(dproj,))
-    dproj = after(dproj, *t4, s_out.left, s_out.right)
-    s_qa = ring.scatter_sum(mm(h1, dproj[:, : 2 * width], TN).astype(BF16), 0)
-    s_out.hop(during=(s_qa.x,))
-    dh1_part = mm(after(dproj, s_qa.x, s_out.left, s_out.right), w_in, NT).astype(BF16)
+    dh1_part = mm(after(dproj, *t4, s_out.left, s_out.right), w_in, NT).astype(BF16)
+    dh1 = tensor_scatter_sum(dh1_part)
     s_out.hop(during=(dh1_part,))
-    s_qa.hop(during=(dh1_part,))
-    dh1_part = after(dh1_part, s_out.left, s_out.right, s_qa.left, s_qa.right)
-    dh1 = tensor_scatter_sum(dh1_part)
-    s_vz = ring.scatter_sum(mm(after(h1, dh1_part), dproj[:, 2 * width :], TN).astype(BF16), 0)
-    d_gate_up = after(s_gu.result(), s_vz.x)
+    s_qa = ring.scatter_sum(
+        mm(after(h1, dh1_part, s_out.left, s_out.right), dproj[:, : 2 * width], TN).astype(BF16), 0)
+    s_out.hop(during=(s_qa.left, s_qa.right))
+    s_vz = ring.scatter_sum(
+        mm(after(h1, s_qa.left, s_qa.right, s_out.left, s_out.right), dproj[:, 2 * width :], TN).astype(BF16), 0)
+    s_qa.hop(during=(s_vz.left, s_vz.right))
+    o4 = s_out.hop(during=(s_vz.left, s_vz.right))
+    d_gate_up = after(s_gu.result(), s_vz.left, s_vz.right, s_qa.left, s_qa.right, *o4)
     d_gu = d_gate_up.reshape(part, 2, hidden_width)
-    s_out.hop(during=(s_vz.x,))
-    s_qa.hop(during=(s_vz.x, d_gu))
-    d_out = s_out.result()
-    s_vz.hop(during=(d_out,))
-    output = after((x2 + ffn).astype(BF16), s_qa.left, s_vz.left)
-    s_qa.hop(during=(output,))
-    s_vz.hop(during=(output,))
+    s_vz.hop(during=(d_gu,))
+    s_qa.hop(during=(d_gu,))
+    output = after((x2 + ffn).astype(BF16), s_qa.left, s_qa.right, s_vz.left, s_vz.right)
     r1 = lax.rsqrt(jnp.mean(x * x, axis=-1, keepdims=True) + EPSILON)
-    back1, d_gain_in = norm_backward(x, r1, gain_in, after(dh1, s_qa.left, s_qa.right, s_vz.left, s_vz.right))
-    d_tokens = (dx2 + back1).astype(BF16)
+    back1, d_gain_in = norm_backward(x, r1, gain_in, after(dh1, output))
     d_gains = jnp.concatenate(
         [d_gain_in.reshape(n_dp, part), d_gain_ffn.reshape(n_dp, part), d_group.reshape(n_dp, small)], axis=1
     )
     d_gains = lax.psum(d_gains, "tensor")
-    qa4 = s_qa.hop(during=(d_gains,))
     s_vz.hop(during=(d_gains,))
-    d_gains = scatter_sum_small(after(d_gains, *qa4, s_vz.left, s_vz.right), "dp", n_dp)[0]
+    s_qa.hop(during=(d_gains,))
+    d_tokens = (dx2 + back1).astype(BF16)
+    d_gains = scatter_sum_small(after(d_gains, s_qa.left, s_qa.right, s_vz.left, s_vz.right), "dp", n_dp)[0]
+    qa4 = s_qa.hop(during=(d_gains, d_tokens))
+    s_vz.hop(during=(d_gains, d_tokens))
+    d_out = after(s_out.result(), *qa4, s_vz.left, s_vz.right)
     d_qa = s_qa.result().reshape(part, 2, width)
-    s_vz.hop(during=(d_qa,))
+    s_vz.hop(during=(d_qa, d_out))
     d_in = jnp.concatenate([d_qa, s_vz.result().reshape(part, 2, width)], axis=1)
     return (
         output,

time: 755 us -> 695 us (0.921)
  other arithmetic: 98.2 us -> 75.7 us
  waiting for transfers between devices: 248 us -> 227 us
  starting transfers between devices: 97.4 us -> 79.7 us
    ppermute x36, waiting for transfers between devices: 84.4 us -> 16.2 us  [send_behind(): return lax.ppermute(x, self.axis, self.behind)]
    ppermute x36, waiting for transfers between devices: 101 us -> 169 us  [send_ahead(): return lax.ppermute(x, self.axis, self.ahead)]
    ppermute x14 -> x3, starting transfers between devices: 20.2 us -> 4.05 us  [scatter_sum_small(): lax.ppermute(other, axis, [(i, i ^ count) for i in range(whole)])]
    reduce_scatter x4, waiting for transfers between devices: 44.3 us -> 32.3 us  [tensor_scatter_sum(): lax.psum_scatter(x, 'tensor', scatter_dimension=0, tiled=True).astype(F32)]
    ppermute x14 -> x3, waiting for transfers between devices: 18 us -> 8.98 us  [scatter_sum_small(): lax.ppermute(other, axis, [(i, i ^ count) for i in range(whole)])]
    add x10 -> x9, other arithmetic: 30.7 us -> 22.6 us  [hop(): self.left, self.right = (left + self.part(shift), right + self.part(-shift))]
    slice x5 -> x0, other arithmetic: 8.01 us -> none  [hop(): behind[:self.half]]
  transfers between devices with their start and end apart: 94 -> 83, of which waited for: 40 -> 33; matrix products, arithmetic and copies ran while one was open for 32% -> 33% of each run, Pallas kernels for 13% -> 14%
where the time goes in v3:
time: 695 us; the launch traced here: 689 us
  waiting for transfers between devices  227 us (33%)
  matrix products  144 us (21%)
  Pallas kernels  94.9 us (14%)
  starting transfers between devices  79.7 us (11%)
  other arithmetic  75.7 us (11%)
  local copies, waits for them, and re-layouts  41.6 us (6%)
  between operations  15.2 us (2%)
  blocking collectives  10.7 us (2%)
    ppermute x36, waiting for transfers between devices, send_ahead(): return lax.ppermute(x, self.axis, self.ahead)  169 us
    dot_general x13, matrix products, mm(): return lax.dot_general(a, b, dims, preferred_element_type=F32)  144 us
    pallas_call x16, Pallas kernels, store(): pl.pallas_call(pair_kernel, grid_spec=pltpu.PrefetchScalarGridSpec(num_sc...  53.3 us
    ppermute x36, starting transfers between devices, send_ahead(): return lax.ppermute(x, self.axis, self.ahead)  53.1 us
    reduce_scatter x4, waiting for transfers between devices, tensor_scatter_sum(): lax.psum_scatter(x, 'tensor', scatter_dimension=0, tiled=True).astype(F32)  32.3 us
    add x9, other arithmetic, hop(): self.left, self.right = (left + self.part(shift), right + self.part(-shift))  22.6 us
    ppermute x36, starting transfers between devices, send_behind(): return lax.ppermute(x, self.axis, self.behind)  22.3 us
    pallas_call x1, Pallas kernels, rec_backward(): pl.pallas_call(backward_kernel, grid_spec=pltpu.PrefetchScalarGridSpec(nu...  19 us
  transfers between devices with their start and end apart: 83, of which 33 were waited for; matrix products, arithmetic and copies ran while one was open for 33% of the time, Pallas kernels for 14%

profile of v3, /device:TPU:0, one launch (start us, length us, event | category | flops | bytes accessed | tf_op | source)
XLA Modules:
  0.0 688.9 jit_solution(742568155907719306)
XLA Ops:
  19.0 22.7 %collective-permute-done.left = bf16[544,256]{1,0:T(8,128)(2,1)S(1)} collective-permute-done((bf16[544,256]{1,0:T(8,128)(2,1)S(1)}, bf16[544,256]{1,0:T(8,128)(2,1)S(1)}, u32[]{:S(2)}, u32[]{:S(2)}) %collective-permute-start) | collective-permute-done | bytes 278560 | tf_op jit(solution)/shard_map/ppermute | solution.py:237
  59.9 9.7 %collective-permute-done.6.left = bf16[256,2048]{1,0:T(8,128)(2,1)} collective-permute-done((bf16[256,2048]{1,0:T(8,128)(2,1)}, bf16[256,2048]{1,0:T(8,128)(2,1)}, u32[]{:S(2)}, u32[]{:S(2)}) %collective-permute-start.6) | collective-permute-done | bytes 1048608 | tf_op jit(solution)/shard_map/ppermute | solution.py:237
  86.5 17.6 %collective-permute-done.8.left = bf16[544,256]{1,0:T(8,128)(2,1)S(1)} collective-permute-done((bf16[544,256]{1,0:T(8,128)(2,1)}, bf16[544,256]{1,0:T(8,128)(2,1)S(1)}, u32[]{:S(2)}, u32[]{:S(2)}) %collective-permute-start.8) | collective-permute-done | bytes 278560 | tf_op jit(solution)/shard_map/ppermute | solution.py:237
  139.5 10.4 %convolution_convert_fusion.6.q_ref.a_ref.v_ref.z_ref = bf16[1024,2048]{1,0:T(8,128)(2,1)} fusion(bf16[1024,2048]{1,0:T(8,128)(2,1)S(1)} %fusion.2, bf16[2048,2048]{1,0:T(8,128)(2,1)S(1)} %copy-done), kind=kOutput, calls=%fused_computation.17 | convolution fusion | flops 8592031744 | bytes 16777216 | tf_op jit(solution)/shard_map/dot_general | solution.py:20
  149.9 13.9 %mixer_forward.1 = (bf16[1024,512]{1,0:T(8,128)(2,1)}, f32[1024,512]{1,0:T(8,128)}, f32[8,128,512]{2,1,0:T(8,128)}) custom-call(s32[1024]{0:T(1024)} %bitcast.76, bf16[1024,2048]{1,0:T(8,128)(2,1)} %convolution_convert_fusion.6.q_ref.a_ref.v_ref.z_ref, bf16[1024,2048]{1,0:T(8,128)(2,1)} %convolution_convert_fusion.6.q_ref.a_ref.v_ref.z_ref, ...), custom_call_target="tpu_custom_call" | custom-call | flops 30000001024 | bytes 10000000 | tf_op jit(solution)/shard_map/mixer_forward/pallas_call | solution.py:165
  163.8 6.3 convolution_convert_fusion.5
  176.5 4.8 gather_pair.24.before
  184.6 32.3 %reduce-scatter.5.cloned.1.call-done = bf16[256,2048]{1,0:T(8,128)(2,1)} async-done(((bf16[1024,2048]{1,0:T(8,128)(2,1)}), bf16[256,2048]{1,0:T(8,128)(2,1)}) %reduce-scatter.5.cloned.1.call-update) | async-done | bytes 1048592 | tf_op jit(solution)/shard_map/reduce_scatter | solution.py:454
  228.7 27.3 %collective-permute-done.24.left = bf16[256,2816]{1,0:T(8,128)(2,1)S(1)} collective-permute-done((bf16[256,2816]{1,0:T(8,128)(2,1)}, bf16[256,2816]{1,0:T(8,128)(2,1)S(1)}, u32[]{:S(2)}, u32[]{:S(2)}) %collective-permute-start.24) | collective-permute-done | bytes 1441824 | tf_op jit(solution)/shard_map/ppermute | solution.py:237
  271.1 7.6 %collective-permute-done.26.left = bf16[128,2816]{1,0:T(8,128)(2,1)} collective-permute-done((bf16[128,2816]{1,0:T(8,128)(2,1)}, bf16[128,2816]{1,0:T(8,128)(2,1)}, u32[]{:S(2)}, u32[]{:S(2)}) %collective-permute-start.26) | collective-permute-done | bytes 720928 | tf_op jit(solution)/shard_map/ppermute | solution.py:237
  283.5 17.3 %fusion.33 = f32[1024,2816]{1,0:T(8,128)S(1)} fusion(bf16[1024,2048]{1,0:T(8,128)(2,1)} %all-gather.7.cloned.1.call-done, bf16[2048,2816]{1,0:T(8,128)(2,1)} %gather_pair.29), kind=kOutput, calls=%fused_computation.125 | convolution fusion | flops 11811160064 | bytes 27262976 | tf_op jit(solution)/shard_map/dot_general | solution.py:20
  309.7 10.4 %convolution_convert_fusion.1 = bf16[1408,2048]{1,0:T(8,128)(2,1)} fusion(bf16[1024,1408]{1,0:T(8,128)(2,1)} %multiply_convert_fusion.2, bf16[1024,2048]{1,0:T(8,128)(2,1)} %all-gather.9.cloned.1.call-done), kind=kOutput, calls=%fused_computation.6 | convolution fusion | flops 5908463616 | bytes 12845056 | tf_op jit(solution)/shard_map/dot_general | solution.py:20
  330.6 14.1 %multiply_convert_fusion.1 = (bf16[1024,1408]{1,0:T(8,128)(2,1)S(1)}, bf16[1024,1408]{1,0:T(8,128)(2,1)S(1)}) fusion(f32[1024,2816]{1,0:T(8,128)} %copy-done.8, bf16[1024,2048]{1,0:T(8,128)(2,1)} %all-gather.9.cloned.1.call-done, bf16[1408,2048]{1,0:T(8,128)(2,1)} %gather_pair.31), kind=kOutput, calls=%fused_computation.9 | convolution fusion | flops 5924323328 | bytes 27262976 | tf_op jit(solution)/shard_map/dot_general | solution.py:20
  354.0 18.5 %convolution_convert_fusion = bf16[2048,2816]{1,0:T(8,128)(2,1)} fusion(bf16[1024,2048]{1,0:T(8,128)(2,1)} %all-gather.7.cloned.1.call-done, bf16[1024,1408]{1,0:T(8,128)(2,1)} %copy-done.20, bf16[1024,1408]{1,0:T(8,128)(2,1)} %copy-done.19), kind=kOutput, calls=%fused_computation | convolution fusion | flops 11828461568 | bytes 21495808 | tf_op jit(solution)/shard_map/dot_general | solution.py:20
  380.3 15.3 %convolution_convert_fusion.2 = bf16[1024,2048]{1,0:T(8,128)(2,1)} fusion(bf16[1024,2816]{1,0:T(8,128)(2,1)} %pad_maximum_fusion, bf16[2048,2816]{1,0:T(8,128)(2,1)S(1)} %bitcast.55), kind=kOutput, calls=%fused_computation.13 | convolution fusion | flops 11813257216 | bytes 21495808 | tf_op jit(solution)/shard_map/dot_general | solution.py:20
  400.8 10.9 %collective-permute-done.38 = bf16[128,2816]{1,0:T(8,128)(2,1)S(1)} collective-permute-done((bf16[128,2816]{1,0:T(8,128)(2,1)}, bf16[128,2816]{1,0:T(8,128)(2,1)S(1)}, u32[]{:S(2)}, u32[]{:S(2)}) %collective-permute-start.38) | collective-permute-done | bytes 720928 | tf_op jit(solution)/shard_map/ppermute | solution.py:237
  419.1 37.5 %collective-permute-done.42 = bf16[1408,256]{1,0:T(8,128)(2,1)S(1)} collective-permute-done((bf16[1408,256]{1,0:T(8,128)(2,1)S(1)}, bf16[1408,256]{1,0:T(8,128)(2,1)S(1)}, u32[]{:S(2)}, u32[]{:S(2)}) %collective-permute-start.42) | collective-permute-done | bytes 720928 | tf_op jit(solution)/shard_map/ppermute | solution.py:237
  472.9 11.7 %convolution_convert_fusion.4 = bf16[1024,2048]{1,0:T(8,128)(2,1)} fusion(bf16[1024,1408]{1,0:T(8,128)(2,1)S(1)} %copy-done.18, bf16[1408,2048]{1,0:T(8,128)(2,1)} %gather_pair.31), kind=kOutput, calls=%fused_computation.15 | convolution fusion | flops 5907677184 | bytes 12845056 | tf_op jit(solution)/shard_map/dot_general | solution.py:20
  484.6 11.9 %collective-permute-done.44 = bf16[256,2816]{1,0:T(8,128)(2,1)} collective-permute-done((bf16[256,2816]{1,0:T(8,128)(2,1)}, bf16[256,2816]{1,0:T(8,128)(2,1)}, u32[]{:S(2)}, u32[]{:S(2)}) %collective-permute-start.44) | collective-permute-done | bytes 1441824 | tf_op jit(solution)/shard_map/ppermute | solution.py:237
  497.8 4.5 dynamic-slice_add_fusion
  504.9 6.3 convolution_convert_fusion.9
  513.0 7.2 %fusion.16.dy_ref = f32[1024,512]{1,0:T(8,128)} fusion(bf16[1024,2048]{1,0:T(8,128)(2,1)} %all-gather.11.cloned.1.call-done, bf16[544,2048]{1,0:T(8,128)(2,1)} %gather_pair.21), kind=kOutput, calls=%fused_computation.44 | convolution fusion | flops 2147483648 | bytes 8388608 | tf_op jit(solution)/shard_map/dot_general | solution.py:20
  522.2 19.0 %mixer_backward.1 = (bf16[1024,2048]{1,0:T(8,128)(2,1)}, f32[1,128]{1,0:T(1,128)}) custom-call(s32[1024]{0:T(1024)} %bitcast.77, bf16[1024,2048]{1,0:T(8,128)(2,1)} %convolution_convert_fusion.6.q_ref.a_ref.v_ref.z_ref, bf16[1024,2048]{1,0:T(8,128)(2,1)} %convolution_convert_fusion.6.q_ref.a_ref.v_ref.z_ref, ...), custom_call_target="tpu_custom_call" | custom-call | flops 60000002048 | bytes 14000000 | tf_op jit(solution)/shard_map/mixer_backward/pallas_call | solution.py:192
  542.5 14.0 %convolution_convert_fusion.3 = bf16[1024,2048]{1,0:T(8,128)(2,1)} fusion(bf16[1024,2048]{1,0:T(8,128)(2,1)} %get-tuple-element.276, bf16[2048,2048]{1,0:T(8,128)(2,1)} %gather_pair.23), kind=kOutput, calls=%fused_computation.14 | convolution fusion | flops 8592031744 | bytes 16777216 | tf_op jit(solution)/shard_map/dot_general | solution.py:20
  558.6 5.1 collective-permute-done.50
  569.7 7.5 %convolution_convert_fusion.8 = bf16[2048,1024]{0,1:T(8,128)(2,1)S(1)} fusion(bf16[1024,2048]{1,0:T(8,128)(2,1)} %copy-done.13, bf16[1024,2048]{1,0:T(8,128)(2,1)} %get-tuple-element.276), kind=kOutput, calls=%fused_computation.19 | convolution fusion | flops 4297064448 | bytes 10485760 | tf_op jit(solution)/shard_map/dot_general | solution.py:20
  581.3 5.0 convolution_convert_fusion.7
  602.4 4.7 reshape.104
  621.9 10.7 %psum.7 = f32[8,528]{1,0:T(8,128)S(1)} all-reduce(f32[8,528]{1,0:T(8,128)S(1)} %pad_maximum_fusion.2), channel_id=1, replica_groups=mesh['dp'=8,'tensor'=4] {'tensor'}, use_global_device_ids=true, to_apply=%region_11.12 | all-reduce | flops 4224 | bytes 33792 | tf_op jit(solution)/shard_map/psum | solution.py:568
  649.9 8.0 %collective-permute-done.70 = f32[1,528]{1,0:T(1,128)S(1)} collective-permute-done((f32[1,528]{1,0:T(1,128)S(1)}, f32[1,528]{1,0:T(1,128)S(1)}, u32[]{:S(2)}, u32[]{:S(2)}) %collective-permute-start.70) | collective-permute-done | bytes 2144 | tf_op jit(solution)/shard_map/ppermute | solution.py:433
  663.6 5.5 collective-permute-done.64
  671.2 5.9 collective-permute-done.73
  (384 shorter events, 270.4 us)
Async XLA Ops:
  7.2 125.4 %all-gather.5.cloned.1.call-start = ((), (), s32[]{:S(2)}) async-start(), calls=%async_computation.4 | async-start | bytes 5242880 | tf_op jit(solution)/shard_map/all_gather | solution.py:450
  8.0 208.9 %reduce-scatter.5.cloned.1.call-start = ((), (), s32[]{:S(2)}) async-start(), calls=%async_computation.5 | async-start | bytes 5242880 | tf_op jit(solution)/shard_map/reduce_scatter | solution.py:454
  9.5 33.7 %collective-permute-start.2 = (bf16[256,2048]{1,0:T(8,128)(2,1)S(1)}, bf16[256,2048]{1,0:T(8,128)(2,1)}, u32[]{:S(2)}, u32[]{:S(2)}) collective-permute-start(bf16[256,2048]{1,0:T(8,128)(2,1)S(1)} %bitcast.59), channel_id=1, source_target_pairs={{0,8},{8,16},{16,24},{24,28},{28,20},{20,12},{12,4},{4,0},{1,9},{9... | collective-permute-start | bytes 3145736 | tf_op jit(solution)/shard_map/ppermute | solution.py:237
  12.6 30.6 %collective-permute-start.3 = (bf16[256,2048]{1,0:T(8,128)(2,1)S(1)}, bf16[256,2048]{1,0:T(8,128)(2,1)}, u32[]{:S(2)}, u32[]{:S(2)}) collective-permute-start(bf16[256,2048]{1,0:T(8,128)(2,1)S(1)} %bitcast.60), channel_id=1, source_target_pairs={{8,0},{16,8},{24,16},{28,24},{20,28},{12,20},{4,12},{0,4},{9,1},{1... | collective-permute-start | bytes 3145736 | tf_op jit(solution)/shard_map/ppermute | solution.py:240
  12.7 29.0 %collective-permute-start = (bf16[544,256]{1,0:T(8,128)(2,1)S(1)}, bf16[544,256]{1,0:T(8,128)(2,1)S(1)}, u32[]{:S(2)}, u32[]{:S(2)}) collective-permute-start(bf16[544,256]{1,0:T(8,128)(2,1)S(1)} %constant_dynamic-update-slice_fusion.block), channel_id=1, source_target_pairs={{0,8},{8,16},{16,24},{24,28},{28,20},{20,12},{12,4},{4,0},{1,9},{9... | collective-permute-start | bytes 835592 | tf_op jit(solution)/shard_map/ppermute | solution.py:237
  44.8 30.4 %collective-permute-start.7 = (bf16[256,2048]{1,0:T(8,128)(2,1)}, bf16[256,2048]{1,0:T(8,128)(2,1)}, u32[]{:S(2)}, u32[]{:S(2)}) collective-permute-start(bf16[256,2048]{1,0:T(8,128)(2,1)} %collective-permute-done.3.right), channel_id=1, source_target_pairs={{8,0},{16,8},{24,16},{28,24},{20,28},{12,20},{4,12},{0,4},{9,1},{1... | collective-permute-start | bytes 3145736 | tf_op jit(solution)/shard_map/ppermute | solution.py:240
  75.2 30.8 %collective-permute-start.10 = (bf16[256,2048]{1,0:T(8,128)(2,1)}, bf16[256,2048]{1,0:T(8,128)(2,1)S(1)}, u32[]{:S(2)}, u32[]{:S(2)}) collective-permute-start(bf16[256,2048]{1,0:T(8,128)(2,1)} %collective-permute-done.6.left), channel_id=1, source_target_pairs={{0,8},{8,16},{16,24},{24,28},{28,20},{20,12},{12,4},{4,0},{1,9},{9... | collective-permute-start | bytes 3145736 | tf_op jit(solution)/shard_map/ppermute | solution.py:237
  76.8 30.1 %collective-permute-start.11 = (bf16[256,2048]{1,0:T(8,128)(2,1)}, bf16[256,2048]{1,0:T(8,128)(2,1)S(1)}, u32[]{:S(2)}, u32[]{:S(2)}) collective-permute-start(bf16[256,2048]{1,0:T(8,128)(2,1)} %collective-permute-done.7.right), channel_id=1, source_target_pairs={{8,0},{16,8},{24,16},{28,24},{20,28},{12,20},{4,12},{0,4},{9,1},{1... | collective-permute-start | bytes 3145736 | tf_op jit(solution)/shard_map/ppermute | solution.py:240
  125.5 46.9 %collective-permute-start.16 = (bf16[256,2816]{1,0:T(8,128)(2,1)S(1)}, bf16[256,2816]{1,0:T(8,128)(2,1)}, u32[]{:S(2)}, u32[]{:S(2)}) collective-permute-start(bf16[256,2816]{1,0:T(8,128)(2,1)S(1)} %bitcast.57), channel_id=1, source_target_pairs={{0,8},{8,16},{16,24},{24,28},{28,20},{20,12},{12,4},{4,0},{1,9},{9... | collective-permute-start | bytes 4325384 | tf_op jit(solution)/shard_map/ppermute | solution.py:237
  127.0 45.3 %collective-permute-start.17 = (bf16[256,2816]{1,0:T(8,128)(2,1)S(1)}, bf16[256,2816]{1,0:T(8,128)(2,1)}, u32[]{:S(2)}, u32[]{:S(2)}) collective-permute-start(bf16[256,2816]{1,0:T(8,128)(2,1)S(1)} %bitcast.58), channel_id=1, source_target_pairs={{8,0},{16,8},{24,16},{28,24},{20,28},{12,20},{4,12},{0,4},{9,1},{1... | collective-permute-start | bytes 4325384 | tf_op jit(solution)/shard_map/ppermute | solution.py:240
  127.5 43.3 %collective-permute-start.18 = (bf16[1408,256]{1,0:T(8,128)(2,1)S(1)}, bf16[1408,256]{1,0:T(8,128)(2,1)}, u32[]{:S(2)}, u32[]{:S(2)}) collective-permute-start(bf16[1408,256]{1,0:T(8,128)(2,1)S(1)} %copy-done.27), channel_id=1, source_target_pairs={{0,8},{8,16},{16,24},{24,28},{28,20},{20,12},{12,4},{4,0},{1,9},{9... | collective-permute-start | bytes 2162696 | tf_op jit(solution)/shard_map/ppermute | solution.py:237
  129.1 43.2 %collective-permute-start.19 = (bf16[1408,256]{1,0:T(8,128)(2,1)S(1)}, bf16[1408,256]{1,0:T(8,128)(2,1)}, u32[]{:S(2)}, u32[]{:S(2)}) collective-permute-start(bf16[1408,256]{1,0:T(8,128)(2,1)S(1)} %copy-done.27), channel_id=1, source_target_pairs={{8,0},{16,8},{24,16},{28,24},{20,28},{12,20},{4,12},{0,4},{9,1},{1... | collective-permute-start | bytes 2162696 | tf_op jit(solution)/shard_map/ppermute | solution.py:240
  172.4 87.0 %all-gather.7.cloned.1.call-start = ((), (), s32[]{:S(2)}) async-start(), calls=%async_computation.6 | async-start | bytes 5242880 | tf_op jit(solution)/shard_map/all_gather | solution.py:450
  172.4 46.0 %collective-permute-start.20 = (bf16[256,2816]{1,0:T(8,128)(2,1)}, bf16[256,2816]{1,0:T(8,128)(2,1)S(1)}, u32[]{:S(2)}, u32[]{:S(2)}) collective-permute-start(bf16[256,2816]{1,0:T(8,128)(2,1)} %collective-permute-done.16.left), channel_id=1, source_target_pairs={{0,8},{8,16},{16,24},{24,28},{28,20},{20,12},{12,4},{4,0},{1,9},{9... | collective-permute-start | bytes 4325384 | tf_op jit(solution)/shard_map/ppermute | solution.py:237
  174.5 45.0 %collective-permute-start.21 = (bf16[256,2816]{1,0:T(8,128)(2,1)}, bf16[256,2816]{1,0:T(8,128)(2,1)}, u32[]{:S(2)}, u32[]{:S(2)}) collective-permute-start(bf16[256,2816]{1,0:T(8,128)(2,1)} %collective-permute-done.17.right), channel_id=1, source_target_pairs={{8,0},{16,8},{24,16},{28,24},{20,28},{12,20},{4,12},{0,4},{9,1},{1... | collective-permute-start | bytes 4325384 | tf_op jit(solution)/shard_map/ppermute | solution.py:240
  174.5 43.9 %collective-permute-start.22 = (bf16[1408,256]{1,0:T(8,128)(2,1)}, bf16[1408,256]{1,0:T(8,128)(2,1)}, u32[]{:S(2)}, u32[]{:S(2)}) collective-permute-start(bf16[1408,256]{1,0:T(8,128)(2,1)} %collective-permute-done.18.left), channel_id=1, source_target_pairs={{0,8},{8,16},{16,24},{24,28},{28,20},{20,12},{12,4},{4,0},{1,9},{9... | collective-permute-start | bytes 2162696 | tf_op jit(solution)/shard_map/ppermute | solution.py:237
  176.5 41.8 %collective-permute-start.23 = (bf16[1408,256]{1,0:T(8,128)(2,1)}, bf16[1408,256]{1,0:T(8,128)(2,1)}, u32[]{:S(2)}, u32[]{:S(2)}) collective-permute-start(bf16[1408,256]{1,0:T(8,128)(2,1)} %collective-permute-done.19.right), channel_id=1, source_target_pairs={{8,0},{16,8},{24,16},{28,24},{20,28},{12,20},{4,12},{0,4},{9,1},{1... | collective-permute-start | bytes 2162696 | tf_op jit(solution)/shard_map/ppermute | solution.py:240
  222.4 87.3 %all-gather.9.cloned.1.call-start = ((), (), s32[]{:S(2)}) async-start(), calls=%async_computation.7 | async-start | bytes 5242880 | tf_op jit(solution)/shard_map/all_gather | solution.py:450
  222.4 33.6 %collective-permute-start.24 = (bf16[256,2816]{1,0:T(8,128)(2,1)}, bf16[256,2816]{1,0:T(8,128)(2,1)S(1)}, u32[]{:S(2)}, u32[]{:S(2)}) collective-permute-start(bf16[256,2816]{1,0:T(8,128)(2,1)} %copy-done.25), channel_id=1, source_target_pairs={{0,8},{8,16},{16,24},{24,28},{28,20},{20,12},{12,4},{4,0},{1,9},{9... | collective-permute-start | bytes 4325384 | tf_op jit(solution)/shard_map/ppermute | solution.py:237
  224.0 33.4 %collective-permute-start.25 = (bf16[256,2816]{1,0:T(8,128)(2,1)}, bf16[256,2816]{1,0:T(8,128)(2,1)}, u32[]{:S(2)}, u32[]{:S(2)}) collective-permute-start(bf16[256,2816]{1,0:T(8,128)(2,1)} %collective-permute-done.21.right), channel_id=1, source_target_pairs={{8,0},{16,8},{24,16},{28,24},{20,28},{12,20},{4,12},{0,4},{9,1},{1... | collective-permute-start | bytes 4325384 | tf_op jit(solution)/shard_map/ppermute | solution.py:240
  224.5 238.1 %reduce-scatter.7.cloned.1.call-start = ((), (), s32[]{:S(2)}) async-start(), calls=%async_computation.8 | async-start | bytes 5242880 | tf_op jit(solution)/shard_map/reduce_scatter | solution.py:454
  264.6 36.2 %collective-permute-start.28 = (bf16[1408,256]{1,0:T(8,128)(2,1)}, bf16[1408,256]{1,0:T(8,128)(2,1)}, u32[]{:S(2)}, u32[]{:S(2)}) collective-permute-start(bf16[1408,256]{1,0:T(8,128)(2,1)} %collective-permute-done.22.left), channel_id=1, source_target_pairs={{0,8},{8,16},{16,24},{24,28},{28,20},{20,12},{12,4},{4,0},{1,9},{9... | collective-permute-start | bytes 2162696 | tf_op jit(solution)/shard_map/ppermute | solution.py:237
  266.1 34.7 %collective-permute-start.29 = (bf16[1408,256]{1,0:T(8,128)(2,1)}, bf16[1408,256]{1,0:T(8,128)(2,1)S(1)}, u32[]{:S(2)}, u32[]{:S(2)}) collective-permute-start(bf16[1408,256]{1,0:T(8,128)(2,1)} %collective-permute-done.23.right), channel_id=1, source_target_pairs={{8,0},{16,8},{24,16},{28,24},{20,28},{12,20},{4,12},{0,4},{9,1},{1... | collective-permute-start | bytes 2162696 | tf_op jit(solution)/shard_map/ppermute | solution.py:240
  398.6 106.3 %all-gather.11.cloned.1.call-start = ((), (), s32[]{:S(2)}) async-start(), calls=%async_computation.9 | async-start | bytes 5242880 | tf_op jit(solution)/shard_map/all_gather | solution.py:450
  415.0 43.0 %collective-permute-start.40 = (bf16[256,2816]{1,0:T(8,128)(2,1)S(1)}, bf16[256,2816]{1,0:T(8,128)(2,1)S(1)}, u32[]{:S(2)}, u32[]{:S(2)}) collective-permute-start(bf16[256,2816]{1,0:T(8,128)(2,1)S(1)} %get-tuple-element.246), channel_id=1, source_target_pairs={{0,8},{8,16},{16,24},{24,28},{28,20},{20,12},{12,4},{4,0},{1,9},{9... | collective-permute-start | bytes 4325384 | tf_op jit(solution)/shard_map/ppermute | solution.py:237
  416.3 42.6 %collective-permute-start.41 = (bf16[256,2816]{1,0:T(8,128)(2,1)S(1)}, bf16[256,2816]{1,0:T(8,128)(2,1)S(1)}, u32[]{:S(2)}, u32[]{:S(2)}) collective-permute-start(bf16[256,2816]{1,0:T(8,128)(2,1)S(1)} %get-tuple-element.247), channel_id=1, source_target_pairs={{8,0},{16,8},{24,16},{28,24},{20,28},{12,20},{4,12},{0,4},{9,1},{1... | collective-permute-start | bytes 4325384 | tf_op jit(solution)/shard_map/ppermute | solution.py:240
  417.1 39.5 %collective-permute-start.42 = (bf16[1408,256]{1,0:T(8,128)(2,1)S(1)}, bf16[1408,256]{1,0:T(8,128)(2,1)S(1)}, u32[]{:S(2)}, u32[]{:S(2)}) collective-permute-start(bf16[1408,256]{1,0:T(8,128)(2,1)S(1)} %get-tuple-element.250), channel_id=1, source_target_pairs={{0,8},{8,16},{16,24},{24,28},{28,20},{20,12},{12,4},{4,0},{1,9},{9... | collective-permute-start | bytes 2162696 | tf_op jit(solution)/shard_map/ppermute | solution.py:237
  418.9 39.1 %collective-permute-start.43 = (bf16[1408,256]{1,0:T(8,128)(2,1)S(1)}, bf16[1408,256]{1,0:T(8,128)(2,1)S(1)}, u32[]{:S(2)}, u32[]{:S(2)}) collective-permute-start(bf16[1408,256]{1,0:T(8,128)(2,1)S(1)} %get-tuple-element.251), channel_id=1, source_target_pairs={{8,0},{16,8},{24,16},{28,24},{20,28},{12,20},{4,12},{0,4},{9,1},{1... | collective-permute-start | bytes 2162696 | tf_op jit(solution)/shard_map/ppermute | solution.py:240
  467.7 148.1 %reduce-scatter.9.cloned.1.call-start = ((), (), s32[]{:S(2)}) async-start(), calls=%async_computation.10 | async-start | bytes 5242880 | tf_op jit(solution)/shard_map/reduce_scatter | solution.py:454
  502.3 39.0 %collective-permute-start.46 = (bf16[256,2816]{1,0:T(8,128)(2,1)}, bf16[256,2816]{1,0:T(8,128)(2,1)}, u32[]{:S(2)}, u32[]{:S(2)}) collective-permute-start(bf16[256,2816]{1,0:T(8,128)(2,1)} %get-tuple-element.268), channel_id=1, source_target_pairs={{0,8},{8,16},{16,24},{24,28},{28,20},{20,12},{12,4},{4,0},{1,9},{9... | collective-permute-start | bytes 4325384 | tf_op jit(solution)/shard_map/ppermute | solution.py:237
  504.7 36.5 %collective-permute-start.47 = (bf16[256,2816]{1,0:T(8,128)(2,1)S(1)}, bf16[256,2816]{1,0:T(8,128)(2,1)}, u32[]{:S(2)}, u32[]{:S(2)}) collective-permute-start(bf16[256,2816]{1,0:T(8,128)(2,1)S(1)} %get-tuple-element.269), channel_id=1, source_target_pairs={{8,0},{16,8},{24,16},{28,24},{20,28},{12,20},{4,12},{0,4},{9,1},{1... | collective-permute-start | bytes 4325384 | tf_op jit(solution)/shard_map/ppermute | solution.py:240
  511.2 107.1 %reduce-scatter.11.cloned.1.call-start = ((), (), s32[]{:S(2)}) async-start(), calls=%async_computation.11 | async-start | bytes 5242880 | tf_op jit(solution)/shard_map/reduce_scatter | solution.py:454
  (110 other events, 1394.2 us)
Sparse Core Ops, SparseCore 0:
  9.6 37.1 all-gather.4
  172.5 44.3 reduce-scatter.4
  222.5 34.4 all-gather.6
  258.5 34.4 all-gather.8
  398.7 43.2 reduce-scatter.6
  467.9 32.7 all-gather.10
  511.3 42.5 reduce-scatter.8
  556.7 44.5 reduce-scatter.10

commit v4 on v3

--- a/solution.py
+++ b/solution.py
@@ -1,4 +1,5 @@
 import functools
+import math
 import jax
 import jax.numpy as jnp
 from jax import lax
@@ -268,27 +269,38 @@
 
 
 class Gather:
-    def __init__(self, ring, x, dim):
+    def __init__(self, ring, x, dim, partner=None):
         self.ring, self.dim, self.half = ring, dim, x.shape[0] // 2
+        self.column, self.left, self.right = 0, x, x
+        self.step, self.steps, self.pending = 0, ring.count // 2, False
+        if partner is not None:
+            self.box, self.shape, self.column = partner.box, partner.shape, 1
+            return
         shape = list(x.shape)
         shape[dim] *= ring.count
         self.shape = jax.ShapeDtypeStruct(tuple(shape), x.dtype)
-        self.left = self.right = x
-        self.step, self.steps, self.pending = 0, ring.count // 2, False
         self.aligned = x.shape[1] % 128 == 0
         if not self.aligned:
             at = [0, 0]
             at[dim] = ring.me * x.shape[dim]
-            self.whole = lax.dynamic_update_slice(jnp.zeros(shape, x.dtype), x, at)
+            self.box = [lax.dynamic_update_slice(jnp.zeros(shape, x.dtype), x, at)]
             return
         to = (lambda i, at: (at[0], 0)) if self.dim == 0 else (lambda i, at: (0, at[0]))
-        self.whole = pl.pallas_call(
+        self.box = [pl.pallas_call(
             first_kernel,
             grid_spec=pltpu.PrefetchScalarGridSpec(
                 num_scalar_prefetch=1, grid=(1,), in_specs=[pl.BlockSpec(x.shape, lambda i, at: (0, 0))],
                 out_specs=pl.BlockSpec(x.shape, to)),
             out_shape=self.shape, cost_estimate=SMALL_COST, name="gather_first",
-        )(self.ring.me.reshape(1), x)
+        )(self.ring.me.reshape(1), x)]
+
+    @property
+    def whole(self):
+        return self.box[0]
+
+    @whole.setter
+    def whole(self, value):
+        self.box[0] = value
 
     def hop(self, *earlier):
         ring = self.ring
@@ -318,6 +330,12 @@
         self.store()
         self.left, self.right, self.step, self.pending = left, right, self.step + 1, True
 
+    def split(self, x, y):
+        self.left = self.right = x
+        other = Gather(self.ring, y, self.dim, self)
+        other.aligned = self.aligned
+        return other
+
     def settle(self, x):
         x, self.whole = lax.optimization_barrier((x, self.whole))
         return x
@@ -342,9 +360,9 @@
             return
         owners = jnp.stack([ring.owner(-self.step), ring.owner(self.step)])
         if self.dim == 0 and last:
-            to = lambda i, at: (2 * at[i] + i, 0)
+            to = lambda i, at: (2 * at[i] + i, self.column)
         elif self.dim == 0:
-            to = lambda i, at: (at[i], 0)
+            to = lambda i, at: (at[i], self.column)
         elif last:
             to = lambda i, at: (i, at[i])
         else:
@@ -368,6 +386,13 @@
         *blocks, one.whole, two.whole = lax.optimization_barrier((*blocks, one.whole, two.whole))
     one.send(*blocks[:2])
     two.send(*blocks[2:])
+
+
+def finish_kernel(parts, at, left, right, own, total):
+    both = left[...].astype(F32) + right[...].astype(F32) + own[...].astype(F32)
+    width = both.shape[1] // parts
+    for k in range(parts):
+        total[:, k, :] = both[:, k * width : (k + 1) * width]
 
 
 class ScatterSum:
@@ -404,6 +429,23 @@
             self.left, self.right = left + self.part(shift), right + self.part(-shift)
         return self.arrived
 
+    def finish(self, parts):
+        while self.step < self.steps:
+            self.hop()
+        left, right = self.arrived
+        rows, columns = left.shape
+        tile = min(64, rows)
+        near = pl.BlockSpec((tile, columns), lambda i, at: (i, 0))
+        mine = pl.BlockSpec((tile, columns), lambda i, at: (at[0] * (rows // tile) + i, 0))
+        return pl.pallas_call(
+            functools.partial(finish_kernel, parts),
+            grid_spec=pltpu.PrefetchScalarGridSpec(
+                num_scalar_prefetch=1, grid=(rows // tile,), in_specs=[near, near, mine],
+                out_specs=pl.BlockSpec((tile, parts, columns // parts), lambda i, at: (i, 0, 0))),
+            out_shape=jax.ShapeDtypeStruct((rows, parts, columns // parts), F32),
+            cost_estimate=SMALL_COST, name="finish",
+        )(self.ring.me.reshape(1), left, right, self.x)
+
     def result(self):
         while self.step < self.steps:
             self.hop()
@@ -475,6 +517,7 @@
     g_in, g_out = ring.gather(in_part, 0), ring.gather(out_part, 1)
     hop_together(g_out, g_in)
     g_gu, g_down = ring.gather(gu_part, 0), ring.gather(down, 1)
+    g_up = g_gu.split(gu_part[:, :hidden_width], gu_part[:, hidden_width:])
     hop_together(g_out, g_in)
     g_in.left, g_gu.whole, g_down.whole = lax.optimization_barrier((g_in.left, g_gu.whole, g_down.whole))
     while g_out.step < g_out.steps:
@@ -489,31 +532,37 @@
     h1, _ = norm_forward(seq.astype(F32), gain_in)
     w_in = g_in.result()
 
-    gu1 = g_gu.hop(*done)
+    gate1 = g_gu.hop(*done)
+    up1 = g_up.hop(*done)
     down1 = g_down.hop(*done)
     proj = mm(h1, w_in, NN).astype(BF16)
     y, o, states = rec_forward(proj, seg, gain_group)
-    attn_part = after(mm(y, w_out, NN).astype(BF16), *gu1, *down1)
-    gu2 = g_gu.hop(attn_part)
-    down2 = g_down.hop(attn_part)
+    attn_part = after(mm(y, w_out, NN).astype(BF16), *gate1, *up1, *down1)
+    g_gu.hop(attn_part)
+    g_up.hop(attn_part)
     attn = tensor_scatter_sum(attn_part)
     x = tokens.astype(F32)
-    x2 = x + g_down.settle(g_gu.settle(after(attn, *gu2, *down2)))
+    gate3 = g_gu.hop()
+    g_down.store()
+    x2 = x + g_down.settle(g_gu.settle(after(attn, *gate3, g_up.left, g_up.right)))
     h2_own, r2 = norm_forward(x2, gain_ffn)
-    gu3 = g_gu.hop()
-    g_down.store()
-    h2 = g_down.settle(g_gu.settle(after(tensor_gather(h2_own), *gu3)))
-    gu4 = g_gu.hop()
-    down3 = g_down.hop(*gu3)
-    w_gu = g_gu.result()
-    gu = after(mm(h2, w_gu, NN), *down3)
-    down4 = g_down.hop(gu)
+    g_up.hop()
+    g_gu.hop()
+    g_up.hop()
+    h2 = g_gu.settle(after(tensor_gather(h2_own), g_gu.left, g_gu.right, g_up.left, g_up.right))
+    down2 = g_down.hop(g_up.left, g_up.right)
+    g_gu.store()
+    w_gu = g_up.result()
+    gu = after(mm(h2, w_gu, NN), *down2)
+    down3 = g_down.hop(gu)
     gate, up = gu[:, :hidden_width], gu[:, hidden_width:]
     sg = jax.nn.sigmoid(gate)
     swish = gate * sg
     hidden = (swish * up).astype(BF16)
-    d_down_part = after(mm(hidden, cot, TN).astype(BF16), *down4)
+    d_down_part = after(mm(hidden, cot, TN).astype(BF16), *down3)
+    down4 = g_down.hop(d_down_part)
     s_down = ring.scatter_sum(d_down_part, 1)
+    step1 = s_down.hop()
     w_down = g_down.result()
     dh = mm(after(cot, s_down.left, s_down.right), w_down, NT)
     dgate = (dh * up * sg * (1.0 + gate * (1.0 - sg))).astype(BF16)
@@ -525,57 +574,49 @@
     s_gu = ring.scatter_sum(d_gu_part, 0)
     dh2_part = mm(after(dgu, s_gu.left, s_gu.right, s_down.left, s_down.right), w_gu, NT).astype(BF16)
     t1 = s_gu.hop(during=(dh2_part,))
-    s_down.hop(during=(dh2_part,))
-    dh2_part = after(dh2_part, s_down.left, s_down.right)
+    dh2_part = after(dh2_part, *t1)
     dh2 = tensor_scatter_sum(dh2_part)
-    step4 = s_down.hop(during=(s_gu.left, s_gu.right))
     s_gu.hop()
-    back2, d_gain_ffn = norm_backward(x2, r2, gain_ffn, after(dh2, s_gu.left, s_gu.right, *step4))
+    back2, d_gain_ffn = norm_backward(x2, r2, gain_ffn, after(dh2, s_gu.left, s_gu.right))
     dx2 = cotangent.astype(F32) + back2
     dattn_own = dx2.astype(BF16)
     dattn = tensor_gather(dattn_own)
-    d_down = after(s_down.result(), dattn_own)
     ffn_part = mm(after(hidden, dattn_own), w_down, NN).astype(BF16)
-    s_gu.hop(during=(ffn_part, d_down))
+    s_gu.hop(during=(ffn_part,))
     dattn = after(dattn, s_gu.left, s_gu.right)
     d_out_part = mm(y, dattn, TN).astype(BF16)
     s_out = ring.scatter_sum(d_out_part, 1)
     ffn = tensor_scatter_sum(after(ffn_part, dattn))
     dy = mm(after(dattn, d_out_part), w_out, NT)
-    dproj, d_group = rec_backward(proj, seg, gain_group, o, states, after(dy, s_out.left, s_out.right))
+    dproj, d_group = rec_backward(proj, seg, gain_group, o, states, dy)
     t4 = s_gu.hop(during=(dproj,))
-    s_out.hop(during=(dproj,))
-    dh1_part = mm(after(dproj, *t4, s_out.left, s_out.right), w_in, NT).astype(BF16)
+    dh1_part = mm(after(dproj, *t4), w_in, NT).astype(BF16)
     dh1 = tensor_scatter_sum(dh1_part)
-    s_out.hop(during=(dh1_part,))
-    s_qa = ring.scatter_sum(
-        mm(after(h1, dh1_part, s_out.left, s_out.right), dproj[:, : 2 * width], TN).astype(BF16), 0)
-    s_out.hop(during=(s_qa.left, s_qa.right))
-    s_vz = ring.scatter_sum(
-        mm(after(h1, s_qa.left, s_qa.right, s_out.left, s_out.right), dproj[:, 2 * width :], TN).astype(BF16), 0)
-    s_qa.hop(during=(s_vz.left, s_vz.right))
-    o4 = s_out.hop(during=(s_vz.left, s_vz.right))
-    d_gate_up = after(s_gu.result(), s_vz.left, s_vz.right, s_qa.left, s_qa.right, *o4)
-    d_gu = d_gate_up.reshape(part, 2, hidden_width)
-    s_vz.hop(during=(d_gu,))
-    s_qa.hop(during=(d_gu,))
-    output = after((x2 + ffn).astype(BF16), s_qa.left, s_qa.right, s_vz.left, s_vz.right)
+    step4 = s_down.hop(before=(dproj,), during=(dh1_part,))
+    s_out.hop(before=(dproj,), during=(dh1_part,))
+    s_in = ring.scatter_sum(mm(after(h1, dh1_part), dproj, TN).astype(BF16), 0)
+    o2 = s_out.hop(before=(s_in.left, s_in.right))
+    s_in.hop(before=step4)
     r1 = lax.rsqrt(jnp.mean(x * x, axis=-1, keepdims=True) + EPSILON)
-    back1, d_gain_in = norm_backward(x, r1, gain_in, after(dh1, output))
+    back1, d_gain_in = norm_backward(x, r1, gain_in, after(dh1, s_in.left, s_in.right))
     d_gains = jnp.concatenate(
         [d_gain_in.reshape(n_dp, part), d_gain_ffn.reshape(n_dp, part), d_group.reshape(n_dp, small)], axis=1
     )
     d_gains = lax.psum(d_gains, "tensor")
-    s_vz.hop(during=(d_gains,))
-    s_qa.hop(during=(d_gains,))
-    d_tokens = (dx2 + back1).astype(BF16)
-    d_gains = scatter_sum_small(after(d_gains, s_qa.left, s_qa.right, s_vz.left, s_vz.right), "dp", n_dp)[0]
-    qa4 = s_qa.hop(during=(d_gains, d_tokens))
-    s_vz.hop(during=(d_gains, d_tokens))
-    d_out = after(s_out.result(), *qa4, s_vz.left, s_vz.right)
-    d_qa = s_qa.result().reshape(part, 2, width)
-    s_vz.hop(during=(d_qa, d_out))
-    d_in = jnp.concatenate([d_qa, s_vz.result().reshape(part, 2, width)], axis=1)
+    s_in.hop(before=o2, during=(d_gains,))
+    o3 = s_out.hop()
+    d_tokens = after((dx2 + back1).astype(BF16), s_in.left, s_in.right)
+    d_gains = scatter_sum_small(after(d_gains, s_in.left, s_in.right), "dp", n_dp)[0]
+    s_in.hop(before=o3, during=(d_tokens,))
+    o4 = s_out.hop()
+    d_gu = after(s_gu.arrived[0], s_in.left, s_in.right)
+    s_gu.arrived = d_gu, s_gu.arrived[1]
+    d_gu = s_gu.finish(2)
+    d_down = after(s_down.result(), s_in.left, s_in.right)
+    d_out = after(s_out.result(), s_in.left, s_in.right)
+    output = (x2 + after(ffn, s_in.left, s_in.right)).astype(BF16)
+    s_in.hop(before=o4, during=(d_gu, d_down, d_out, output))
+    d_in = s_in.finish(4)
     return (
         output,
         d_tokens,

time: 695 us -> 690 us (level)
  Pallas kernels: 94.9 us -> 113 us
  waiting for transfers between devices: 227 us -> 214 us
  matrix products: 144 us -> 137 us
    ppermute x36, waiting for transfers between devices: 169 us -> 134 us  [send_ahead(): return lax.ppermute(x, self.axis, self.ahead)]
    ppermute x36, waiting for transfers between devices: 16.2 us -> 40.1 us  [send_behind(): return lax.ppermute(x, self.axis, self.behind)]
    reduce_scatter x4, waiting for transfers between devices: 32.3 us -> 20.7 us  [tensor_scatter_sum(): lax.psum_scatter(x, 'tensor', scatter_dimension=0, tiled=True).astype(F32)]
    pallas_call x16 -> x20, Pallas kernels: 53.3 us -> 62.6 us  [store(): pl.pallas_call(pair_kernel, grid_spec=pltpu.PrefetchScalarGridSpec(num_sc...]
    pallas_call x0 -> x2, Pallas kernels: none -> 8.89 us  [finish(): pl.pallas_call(functools.partial(finish_kernel, parts), grid_spec=pltpu.P...]
    unnamed x125 -> x147, local copies, waits for them, and re-layouts: 14.1 us -> 22 us
    add x5 -> x2, other arithmetic: 11.8 us -> 4.48 us  [result(): return left.astype(F32) + right.astype(F32) + self.part(0).astype(F32)]
    dot_general x13 -> x12, matrix products: 144 us -> 137 us  [mm(): return lax.dot_general(a, b, dims, preferred_element_type=F32)]
  transfers between devices with their start and end apart: 83 -> 83, of which waited for: 33 -> 35; matrix products, arithmetic and copies ran while one was open for 33% -> 30% of each run, Pallas kernels for 14% -> 16%
where the time goes in v4:
time: 690 us; the launch traced here: 680 us
  waiting for transfers between devices  214 us (31%)
  matrix products  137 us (20%)
  Pallas kernels  113 us (16%)
  starting transfers between devices  80.4 us (12%)
  other arithmetic  71.7 us (10%)
  local copies, waits for them, and re-layouts  37.9 us (5%)
  between operations  15.2 us (2%)
  blocking collectives  11.6 us (2%)
    dot_general x12, matrix products, mm(): return lax.dot_general(a, b, dims, preferred_element_type=F32)  137 us
    ppermute x36, waiting for transfers between devices, send_ahead(): return lax.ppermute(x, self.axis, self.ahead)  134 us
    pallas_call x20, Pallas kernels, store(): pl.pallas_call(pair_kernel, grid_spec=pltpu.PrefetchScalarGridSpec(num_sc...  62.6 us
    ppermute x36, starting transfers between devices, send_ahead(): return lax.ppermute(x, self.axis, self.ahead)  49.8 us
    ppermute x36, waiting for transfers between devices, send_behind(): return lax.ppermute(x, self.axis, self.behind)  40.1 us
    ppermute x36, starting transfers between devices, send_behind(): return lax.ppermute(x, self.axis, self.behind)  26.9 us
    add x8, other arithmetic, hop(): self.left, self.right = (left + self.part(shift), right + self.part(-shift))  25.8 us
    unnamed x147, local copies, waits for them, and re-layouts  22 us
  transfers between devices with their start and end apart: 83, of which 35 were waited for; matrix products, arithmetic and copies ran while one was open for 30% of the time, Pallas kernels for 16%

profile of v4, /device:TPU:0, one launch (start us, length us, event | category | flops | bytes accessed | tf_op | source)
XLA Modules:
  0.0 680.5 jit_solution(17188684953075221798)
XLA Ops:
  19.0 22.7 %collective-permute-done.1.right = bf16[544,256]{1,0:T(8,128)(2,1)S(1)} collective-permute-done((bf16[544,256]{1,0:T(8,128)(2,1)S(1)}, bf16[544,256]{1,0:T(8,128)(2,1)S(1)}, u32[]{:S(2)}, u32[]{:S(2)}) %collective-permute-start.1) | collective-permute-done | bytes 278560 | tf_op jit(solution)/shard_map/ppermute | solution.py:241
  60.7 9.6 %collective-permute-done.6.left = bf16[256,2048]{1,0:T(8,128)(2,1)} collective-permute-done((bf16[256,2048]{1,0:T(8,128)(2,1)}, bf16[256,2048]{1,0:T(8,128)(2,1)}, u32[]{:S(2)}, u32[]{:S(2)}) %collective-permute-start.6) | collective-permute-done | bytes 1048608 | tf_op jit(solution)/shard_map/ppermute | solution.py:238
  87.6 16.9 %collective-permute-done.8.left = bf16[544,256]{1,0:T(8,128)(2,1)} collective-permute-done((bf16[544,256]{1,0:T(8,128)(2,1)}, bf16[544,256]{1,0:T(8,128)(2,1)}, u32[]{:S(2)}, u32[]{:S(2)}) %collective-permute-start.8) | collective-permute-done | bytes 278560 | tf_op jit(solution)/shard_map/ppermute | solution.py:238
  143.8 10.4 %convolution_convert_fusion.7.q_ref.a_ref.v_ref.z_ref = bf16[1024,2048]{1,0:T(8,128)(2,1)} fusion(bf16[1024,2048]{1,0:T(8,128)(2,1)S(1)} %fusion.2, bf16[2048,2048]{1,0:T(8,128)(2,1)S(1)} %copy-done), kind=kOutput, calls=%fused_computation.18 | convolution fusion | flops 8592031744 | bytes 16777216 | tf_op jit(solution)/shard_map/dot_general | solution.py:21
  155.2 14.0 %mixer_forward.1 = (bf16[1024,512]{1,0:T(8,128)(2,1)}, f32[1024,512]{1,0:T(8,128)}, f32[8,128,512]{2,1,0:T(8,128)}) custom-call(s32[1024]{0:T(1024)} %bitcast.71, bf16[1024,2048]{1,0:T(8,128)(2,1)} %convolution_convert_fusion.7.q_ref.a_ref.v_ref.z_ref, bf16[1024,2048]{1,0:T(8,128)(2,1)} %convolution_convert_fusion.7.q_ref.a_ref.v_ref.z_ref, ...), custom_call_target="tpu_custom_call" | custom-call | flops 30000001024 | bytes 10000000 | tf_op jit(solution)/shard_map/mixer_forward/pallas_call | solution.py:166
  169.2 5.6 convolution_convert_fusion.6
  186.9 8.2 %collective-permute-done.22.left = bf16[256,1408]{1,0:T(8,128)(2,1)} collective-permute-done((bf16[256,1408]{1,0:T(8,128)(2,1)S(1)}, bf16[256,1408]{1,0:T(8,128)(2,1)}, u32[]{:S(2)}, u32[]{:S(2)}) %collective-permute-start.22) | collective-permute-done | bytes 720928 | tf_op jit(solution)/shard_map/ppermute | solution.py:238
  205.4 14.8 %reduce-scatter.5.cloned.1.call-done = bf16[256,2048]{1,0:T(8,128)(2,1)} async-done(((bf16[1024,2048]{1,0:T(8,128)(2,1)}), bf16[256,2048]{1,0:T(8,128)(2,1)}) %reduce-scatter.5.cloned.1.call-update) | async-done | bytes 1048592 | tf_op jit(solution)/shard_map/reduce_scatter | solution.py:496
  235.8 8.5 %collective-permute-done.30.left = bf16[256,1408]{1,0:T(8,128)(2,1)S(1)} collective-permute-done((bf16[256,1408]{1,0:T(8,128)(2,1)}, bf16[256,1408]{1,0:T(8,128)(2,1)S(1)}, u32[]{:S(2)}, u32[]{:S(2)}) %collective-permute-start.30) | collective-permute-done | bytes 720928 | tf_op jit(solution)/shard_map/ppermute | solution.py:238
  260.6 4.2 collective-permute-done.28.left
  272.0 17.2 %fusion.29 = f32[1024,2816]{1,0:T(8,128)S(1)} fusion(bf16[1024,2048]{1,0:T(8,128)(2,1)} %all-gather.7.cloned.1.call-done, bf16[2048,2816]{1,0:T(8,128)(2,1)} %gather_pair.36), kind=kOutput, calls=%fused_computation.109 | convolution fusion | flops 11811160064 | bytes 27262976 | tf_op jit(solution)/shard_map/dot_general | solution.py:21
  296.3 8.0 %convolution_convert_fusion.2 = bf16[1408,2048]{1,0:T(8,128)(2,1)S(1)} fusion(bf16[1024,1408]{1,0:T(8,128)(2,1)S(1)} %multiply_convert_fusion.2, bf16[1024,2048]{1,0:T(8,128)(2,1)} %all-gather.9.cloned.1.call-done), kind=kOutput, calls=%fused_computation.7 | convolution fusion | flops 5908463616 | bytes 12845056 | tf_op jit(solution)/shard_map/dot_general | solution.py:21
  330.7 14.1 %multiply_convert_fusion.1 = (bf16[1024,1408]{1,0:T(8,128)(2,1)S(1)}, bf16[1024,1408]{1,0:T(8,128)(2,1)S(1)}) fusion(f32[1024,2816]{1,0:T(8,128)} %copy-done.14, bf16[1024,2048]{1,0:T(8,128)(2,1)} %all-gather.9.cloned.1.call-done, bf16[1408,2048]{1,0:T(8,128)(2,1)} %gather_pair.39), kind=kOutput, calls=%fused_computation.10 | convolution fusion | flops 5924323328 | bytes 27262976 | tf_op jit(solution)/shard_map/dot_general | solution.py:21
  353.7 18.2 %convolution_convert_fusion.own = bf16[2048,2816]{1,0:T(8,128)(2,1)} fusion(bf16[1024,2048]{1,0:T(8,128)(2,1)} %all-gather.7.cloned.1.call-done, bf16[1024,1408]{1,0:T(8,128)(2,1)} %copy-done.21, bf16[1024,1408]{1,0:T(8,128)(2,1)S(1)} %get-tuple-element.319), kind=kOutput, calls=%fused_computation | convolution fusion | flops 11828461568 | bytes 21495808 | tf_op jit(solution)/shard_map/dot_general | solution.py:21
  378.8 15.3 %convolution_convert_fusion.3 = bf16[1024,2048]{1,0:T(8,128)(2,1)} fusion(bf16[1024,2816]{1,0:T(8,128)(2,1)} %pad_maximum_fusion, bf16[2048,2816]{1,0:T(8,128)(2,1)S(1)} %bitcast.53), kind=kOutput, calls=%fused_computation.14 | convolution fusion | flops 11813257216 | bytes 21495808 | tf_op jit(solution)/shard_map/dot_general | solution.py:21
  398.8 28.3 %collective-permute-done.48 = bf16[256,2816]{1,0:T(8,128)(2,1)S(1)} collective-permute-done((bf16[256,2816]{1,0:T(8,128)(2,1)S(1)}, bf16[256,2816]{1,0:T(8,128)(2,1)S(1)}, u32[]{:S(2)}, u32[]{:S(2)}) %collective-permute-start.48) | collective-permute-done | bytes 1441824 | tf_op jit(solution)/shard_map/ppermute | solution.py:238
  432.3 5.8 reduce-scatter.7.cloned.1.call-done
  445.3 10.9 %convolution_convert_fusion.5 = bf16[1024,2048]{1,0:T(8,128)(2,1)} fusion(bf16[1024,1408]{1,0:T(8,128)(2,1)} %copy-done.20, bf16[1408,2048]{1,0:T(8,128)(2,1)} %gather_pair.39), kind=kOutput, calls=%fused_computation.16 | convolution fusion | flops 5907677184 | bytes 12845056 | tf_op jit(solution)/shard_map/dot_general | solution.py:21
  456.2 20.8 %collective-permute-done.50 = bf16[256,2816]{1,0:T(8,128)(2,1)} collective-permute-done((bf16[256,2816]{1,0:T(8,128)(2,1)}, bf16[256,2816]{1,0:T(8,128)(2,1)}, u32[]{:S(2)}, u32[]{:S(2)}) %collective-permute-start.50) | collective-permute-done | bytes 1441824 | tf_op jit(solution)/shard_map/ppermute | solution.py:238
  478.0 4.4 dynamic-slice_add_fusion
  484.4 6.4 convolution_convert_fusion.8
  494.5 19.0 %mixer_backward.1 = (bf16[1024,2048]{1,0:T(8,128)(2,1)}, f32[1,128]{1,0:T(1,128)}) custom-call(s32[1024]{0:T(1024)} %bitcast.72, bf16[1024,2048]{1,0:T(8,128)(2,1)} %convolution_convert_fusion.7.q_ref.a_ref.v_ref.z_ref, bf16[1024,2048]{1,0:T(8,128)(2,1)} %convolution_convert_fusion.7.q_ref.a_ref.v_ref.z_ref, ...), custom_call_target="tpu_custom_call" | custom-call | flops 60000002048 | bytes 14000000 | tf_op jit(solution)/shard_map/mixer_backward/pallas_call | solution.py:193
  515.8 13.9 %convolution_convert_fusion.4 = bf16[1024,2048]{1,0:T(8,128)(2,1)} fusion(bf16[1024,2048]{1,0:T(8,128)(2,1)} %get-tuple-element.267, bf16[2048,2048]{1,0:T(8,128)(2,1)} %gather_pair.27), kind=kOutput, calls=%fused_computation.15 | convolution fusion | flops 8592031744 | bytes 16777216 | tf_op jit(solution)/shard_map/dot_general | solution.py:21
  535.8 13.0 %convolution_convert_fusion.1.own = bf16[2048,2048]{1,0:T(8,128)(2,1)S(1)} fusion(bf16[1024,2048]{1,0:T(8,128)(2,1)} %copy-done.19, bf16[1024,2048]{1,0:T(8,128)(2,1)} %get-tuple-element.267), kind=kOutput, calls=%fused_computation.6 | convolution fusion | flops 8594128896 | bytes 16777216 | tf_op jit(solution)/shard_map/dot_general | solution.py:21
  555.4 4.7 collective-permute-done.60
  570.2 7.8 %collective-permute-done.64 = bf16[512,256]{1,0:T(8,128)(2,1)} collective-permute-done((bf16[512,256]{1,0:T(8,128)(2,1)}, bf16[512,256]{1,0:T(8,128)(2,1)}, u32[]{:S(2)}, u32[]{:S(2)}) %collective-permute-start.64) | collective-permute-done | bytes 262176 | tf_op jit(solution)/shard_map/ppermute | solution.py:238
  597.5 11.6 %psum.7 = f32[8,528]{1,0:T(8,128)S(1)} all-reduce(f32[8,528]{1,0:T(8,128)S(1)} %pad_maximum_fusion.1), channel_id=1, replica_groups=mesh['dp'=8,'tensor'=4] {'tensor'}, use_global_device_ids=true, to_apply=%region_10.11 | all-reduce | flops 4224 | bytes 33792 | tf_op jit(solution)/shard_map/psum | solution.py:605
  609.2 4.6 dynamic-slice_add_fusion.8
  624.9 15.2 %collective-permute-done.73 = f32[2,528]{1,0:T(2,128)S(1)} collective-permute-done((f32[2,528]{1,0:T(2,128)S(1)}, f32[2,528]{1,0:T(2,128)S(1)}, u32[]{:S(2)}, u32[]{:S(2)}) %collective-permute-start.73) | collective-permute-done | bytes 4256 | tf_op jit(solution)/shard_map/ppermute | solution.py:475
  640.2 4.4 dynamic-slice_add_fusion.6
  647.7 4.7 finish.2
  655.2 12.7 %collective-permute-done.70.left = bf16[256,2048]{1,0:T(8,128)(2,1)S(1)} collective-permute-done((bf16[256,2048]{1,0:T(8,128)(2,1)}, bf16[256,2048]{1,0:T(8,128)(2,1)S(1)}, u32[]{:S(2)}, u32[]{:S(2)}) %collective-permute-start.70) | collective-permute-done | bytes 1048608 | tf_op jit(solution)/shard_map/ppermute | solution.py:238
  (405 shorter events, 289.3 us)
Async XLA Ops:
  7.2 129.7 %all-gather.5.cloned.1.call-start = ((), (), s32[]{:S(2)}) async-start(), calls=%async_computation.4 | async-start | bytes 5242880 | tf_op jit(solution)/shard_map/all_gather | solution.py:492
  8.0 212.3 %reduce-scatter.5.cloned.1.call-start = ((), (), s32[]{:S(2)}) async-start(), calls=%async_computation.5 | async-start | bytes 5242880 | tf_op jit(solution)/shard_map/reduce_scatter | solution.py:496
  9.5 33.6 %collective-permute-start.3 = (bf16[256,2048]{1,0:T(8,128)(2,1)S(1)}, bf16[256,2048]{1,0:T(8,128)(2,1)}, u32[]{:S(2)}, u32[]{:S(2)}) collective-permute-start(bf16[256,2048]{1,0:T(8,128)(2,1)S(1)} %bitcast.56), channel_id=1, source_target_pairs={{8,0},{16,8},{24,16},{28,24},{20,28},{12,20},{4,12},{0,4},{9,1},{1... | collective-permute-start | bytes 3145736 | tf_op jit(solution)/shard_map/ppermute | solution.py:241
  12.5 30.6 %collective-permute-start.2 = (bf16[256,2048]{1,0:T(8,128)(2,1)S(1)}, bf16[256,2048]{1,0:T(8,128)(2,1)}, u32[]{:S(2)}, u32[]{:S(2)}) collective-permute-start(bf16[256,2048]{1,0:T(8,128)(2,1)S(1)} %bitcast.57), channel_id=1, source_target_pairs={{0,8},{8,16},{16,24},{24,28},{28,20},{20,12},{12,4},{4,0},{1,9},{9... | collective-permute-start | bytes 3145736 | tf_op jit(solution)/shard_map/ppermute | solution.py:238
  12.8 29.0 %collective-permute-start.1 = (bf16[544,256]{1,0:T(8,128)(2,1)S(1)}, bf16[544,256]{1,0:T(8,128)(2,1)S(1)}, u32[]{:S(2)}, u32[]{:S(2)}) collective-permute-start(bf16[544,256]{1,0:T(8,128)(2,1)S(1)} %constant_dynamic-update-slice_fusion.block), channel_id=1, source_target_pairs={{8,0},{16,8},{24,16},{28,24},{20,28},{12,20},{4,12},{0,4},{9,1},{1... | collective-permute-start | bytes 835592 | tf_op jit(solution)/shard_map/ppermute | solution.py:241
  14.7 28.4 %collective-permute-start = (bf16[544,256]{1,0:T(8,128)(2,1)S(1)}, bf16[544,256]{1,0:T(8,128)(2,1)S(1)}, u32[]{:S(2)}, u32[]{:S(2)}) collective-permute-start(bf16[544,256]{1,0:T(8,128)(2,1)S(1)} %constant_dynamic-update-slice_fusion.block), channel_id=1, source_target_pairs={{0,8},{8,16},{16,24},{24,28},{28,20},{20,12},{12,4},{4,0},{1,9},{9... | collective-permute-start | bytes 835592 | tf_op jit(solution)/shard_map/ppermute | solution.py:238
  44.3 30.1 %collective-permute-start.7 = (bf16[256,2048]{1,0:T(8,128)(2,1)}, bf16[256,2048]{1,0:T(8,128)(2,1)S(1)}, u32[]{:S(2)}, u32[]{:S(2)}) collective-permute-start(bf16[256,2048]{1,0:T(8,128)(2,1)} %collective-permute-done.3.right), channel_id=1, source_target_pairs={{8,0},{16,8},{24,16},{28,24},{20,28},{12,20},{4,12},{0,4},{9,1},{1... | collective-permute-start | bytes 3145736 | tf_op jit(solution)/shard_map/ppermute | solution.py:241
  45.9 28.1 %collective-permute-start.4 = (bf16[544,256]{1,0:T(8,128)(2,1)}, bf16[544,256]{1,0:T(8,128)(2,1)}, u32[]{:S(2)}, u32[]{:S(2)}) collective-permute-start(bf16[544,256]{1,0:T(8,128)(2,1)} %copy-done.49), channel_id=1, source_target_pairs={{0,8},{8,16},{16,24},{24,28},{28,20},{20,12},{12,4},{4,0},{1,9},{9... | collective-permute-start | bytes 835592 | tf_op jit(solution)/shard_map/ppermute | solution.py:238
  46.3 28.1 %collective-permute-start.5 = (bf16[544,256]{1,0:T(8,128)(2,1)}, bf16[544,256]{1,0:T(8,128)(2,1)}, u32[]{:S(2)}, u32[]{:S(2)}) collective-permute-start(bf16[544,256]{1,0:T(8,128)(2,1)} %copy-done.48), channel_id=1, source_target_pairs={{8,0},{16,8},{24,16},{28,24},{20,28},{12,20},{4,12},{0,4},{9,1},{1... | collective-permute-start | bytes 835592 | tf_op jit(solution)/shard_map/ppermute | solution.py:241
  75.4 32.3 %collective-permute-start.10 = (bf16[256,2048]{1,0:T(8,128)(2,1)}, bf16[256,2048]{1,0:T(8,128)(2,1)S(1)}, u32[]{:S(2)}, u32[]{:S(2)}) collective-permute-start(bf16[256,2048]{1,0:T(8,128)(2,1)} %collective-permute-done.6.left), channel_id=1, source_target_pairs={{0,8},{8,16},{16,24},{24,28},{28,20},{20,12},{12,4},{4,0},{1,9},{9... | collective-permute-start | bytes 3145736 | tf_op jit(solution)/shard_map/ppermute | solution.py:238
  76.9 31.7 %collective-permute-start.11 = (bf16[256,2048]{1,0:T(8,128)(2,1)}, bf16[256,2048]{1,0:T(8,128)(2,1)S(1)}, u32[]{:S(2)}, u32[]{:S(2)}) collective-permute-start(bf16[256,2048]{1,0:T(8,128)(2,1)} %copy-done.32), channel_id=1, source_target_pairs={{8,0},{16,8},{24,16},{28,24},{20,28},{12,20},{4,12},{0,4},{9,1},{1... | collective-permute-start | bytes 3145736 | tf_op jit(solution)/shard_map/ppermute | solution.py:241
  130.0 44.9 %collective-permute-start.17 = (bf16[256,1408]{1,0:T(8,128)(2,1)}, bf16[256,1408]{1,0:T(8,128)(2,1)}, u32[]{:S(2)}, u32[]{:S(2)}) collective-permute-start(bf16[256,1408]{1,0:T(8,128)(2,1)} %get-tuple-element.182), channel_id=1, source_target_pairs={{8,0},{16,8},{24,16},{28,24},{20,28},{12,20},{4,12},{0,4},{9,1},{1... | collective-permute-start | bytes 2162696 | tf_op jit(solution)/shard_map/ppermute | solution.py:241
  130.4 44.4 %collective-permute-start.18 = (bf16[256,1408]{1,0:T(8,128)(2,1)}, bf16[256,1408]{1,0:T(8,128)(2,1)}, u32[]{:S(2)}, u32[]{:S(2)}) collective-permute-start(bf16[256,1408]{1,0:T(8,128)(2,1)} %get-tuple-element.184), channel_id=1, source_target_pairs={{0,8},{8,16},{16,24},{24,28},{28,20},{20,12},{12,4},{4,0},{1,9},{9... | collective-permute-start | bytes 2162696 | tf_op jit(solution)/shard_map/ppermute | solution.py:238
  132.0 42.9 %collective-permute-start.19 = (bf16[256,1408]{1,0:T(8,128)(2,1)}, bf16[256,1408]{1,0:T(8,128)(2,1)}, u32[]{:S(2)}, u32[]{:S(2)}) collective-permute-start(bf16[256,1408]{1,0:T(8,128)(2,1)} %get-tuple-element.184), channel_id=1, source_target_pairs={{8,0},{16,8},{24,16},{28,24},{20,28},{12,20},{4,12},{0,4},{9,1},{1... | collective-permute-start | bytes 2162696 | tf_op jit(solution)/shard_map/ppermute | solution.py:241
  132.5 42.4 %collective-permute-start.20 = (bf16[1408,256]{1,0:T(8,128)(2,1)S(1)}, bf16[1408,256]{1,0:T(8,128)(2,1)}, u32[]{:S(2)}, u32[]{:S(2)}) collective-permute-start(bf16[1408,256]{1,0:T(8,128)(2,1)S(1)} %copy-done.33), channel_id=1, source_target_pairs={{0,8},{8,16},{16,24},{24,28},{28,20},{20,12},{12,4},{4,0},{1,9},{9... | collective-permute-start | bytes 2162696 | tf_op jit(solution)/shard_map/ppermute | solution.py:238
  175.2 91.2 %all-gather.7.cloned.1.call-start = ((), (), s32[]{:S(2)}) async-start(), calls=%async_computation.6 | async-start | bytes 5242880 | tf_op jit(solution)/shard_map/all_gather | solution.py:492
  181.2 40.5 %collective-permute-start.26 = (bf16[256,1408]{1,0:T(8,128)(2,1)}, bf16[256,1408]{1,0:T(8,128)(2,1)}, u32[]{:S(2)}, u32[]{:S(2)}) collective-permute-start(bf16[256,1408]{1,0:T(8,128)(2,1)} %collective-permute-done.18.left), channel_id=1, source_target_pairs={{0,8},{8,16},{16,24},{24,28},{28,20},{20,12},{12,4},{4,0},{1,9},{9... | collective-permute-start | bytes 2162696 | tf_op jit(solution)/shard_map/ppermute | solution.py:238
  182.7 39.0 %collective-permute-start.27 = (bf16[256,1408]{1,0:T(8,128)(2,1)}, bf16[256,1408]{1,0:T(8,128)(2,1)S(1)}, u32[]{:S(2)}, u32[]{:S(2)}) collective-permute-start(bf16[256,1408]{1,0:T(8,128)(2,1)} %collective-permute-done.19.right), channel_id=1, source_target_pairs={{8,0},{16,8},{24,16},{28,24},{20,28},{12,20},{4,12},{0,4},{9,1},{1... | collective-permute-start | bytes 2162696 | tf_op jit(solution)/shard_map/ppermute | solution.py:241
  225.6 70.6 %all-gather.9.cloned.1.call-start = ((), (), s32[]{:S(2)}) async-start(), calls=%async_computation.7 | async-start | bytes 5242880 | tf_op jit(solution)/shard_map/all_gather | solution.py:492
  226.2 211.9 %reduce-scatter.7.cloned.1.call-start = ((), (), s32[]{:S(2)}) async-start(), calls=%async_computation.8 | async-start | bytes 5242880 | tf_op jit(solution)/shard_map/reduce_scatter | solution.py:496
  258.6 30.6 %collective-permute-start.34 = (bf16[1408,256]{1,0:T(8,128)(2,1)}, bf16[1408,256]{1,0:T(8,128)(2,1)}, u32[]{:S(2)}, u32[]{:S(2)}) collective-permute-start(bf16[1408,256]{1,0:T(8,128)(2,1)} %collective-permute-done.20.left), channel_id=1, source_target_pairs={{0,8},{8,16},{16,24},{24,28},{28,20},{20,12},{12,4},{4,0},{1,9},{9... | collective-permute-start | bytes 2162696 | tf_op jit(solution)/shard_map/ppermute | solution.py:238
  260.1 29.1 %collective-permute-start.35 = (bf16[1408,256]{1,0:T(8,128)(2,1)}, bf16[1408,256]{1,0:T(8,128)(2,1)}, u32[]{:S(2)}, u32[]{:S(2)}) collective-permute-start(bf16[1408,256]{1,0:T(8,128)(2,1)} %collective-permute-done.21.right), channel_id=1, source_target_pairs={{8,0},{16,8},{24,16},{28,24},{20,28},{12,20},{4,12},{0,4},{9,1},{1... | collective-permute-start | bytes 2162696 | tf_op jit(solution)/shard_map/ppermute | solution.py:241
  394.1 90.4 %all-gather.11.cloned.1.call-start = ((), (), s32[]{:S(2)}) async-start(), calls=%async_computation.9 | async-start | bytes 5242880 | tf_op jit(solution)/shard_map/all_gather | solution.py:492
  396.2 30.8 %collective-permute-start.48 = (bf16[256,2816]{1,0:T(8,128)(2,1)S(1)}, bf16[256,2816]{1,0:T(8,128)(2,1)S(1)}, u32[]{:S(2)}, u32[]{:S(2)}) collective-permute-start(bf16[256,2816]{1,0:T(8,128)(2,1)S(1)} %get-tuple-element.247), channel_id=1, source_target_pairs={{0,8},{8,16},{16,24},{24,28},{28,20},{20,12},{12,4},{4,0},{1,9},{9... | collective-permute-start | bytes 4325384 | tf_op jit(solution)/shard_map/ppermute | solution.py:238
  397.8 30.8 %collective-permute-start.49 = (bf16[256,2816]{1,0:T(8,128)(2,1)S(1)}, bf16[256,2816]{1,0:T(8,128)(2,1)S(1)}, u32[]{:S(2)}, u32[]{:S(2)}) collective-permute-start(bf16[256,2816]{1,0:T(8,128)(2,1)S(1)} %get-tuple-element.248), channel_id=1, source_target_pairs={{8,0},{16,8},{24,16},{28,24},{20,28},{12,20},{4,12},{0,4},{9,1},{1... | collective-permute-start | bytes 4325384 | tf_op jit(solution)/shard_map/ppermute | solution.py:241
  443.2 150.5 %reduce-scatter.11.cloned.1.call-start = ((), (), s32[]{:S(2)}) async-start(), calls=%async_computation.11 | async-start | bytes 5242880 | tf_op jit(solution)/shard_map/reduce_scatter | solution.py:496
  443.3 33.7 %collective-permute-start.50 = (bf16[256,2816]{1,0:T(8,128)(2,1)}, bf16[256,2816]{1,0:T(8,128)(2,1)}, u32[]{:S(2)}, u32[]{:S(2)}) collective-permute-start(bf16[256,2816]{1,0:T(8,128)(2,1)} %get-tuple-element.253), channel_id=1, source_target_pairs={{0,8},{8,16},{16,24},{24,28},{28,20},{20,12},{12,4},{4,0},{1,9},{9... | collective-permute-start | bytes 4325384 | tf_op jit(solution)/shard_map/ppermute | solution.py:238
  444.8 33.2 %collective-permute-start.51 = (bf16[256,2816]{1,0:T(8,128)(2,1)S(1)}, bf16[256,2816]{1,0:T(8,128)(2,1)}, u32[]{:S(2)}, u32[]{:S(2)}) collective-permute-start(bf16[256,2816]{1,0:T(8,128)(2,1)S(1)} %get-tuple-element.254), channel_id=1, source_target_pairs={{8,0},{16,8},{24,16},{28,24},{20,28},{12,20},{4,12},{0,4},{9,1},{1... | collective-permute-start | bytes 4325384 | tf_op jit(solution)/shard_map/ppermute | solution.py:241
  482.4 32.5 %collective-permute-start.52 = (bf16[256,2816]{1,0:T(8,128)(2,1)}, bf16[256,2816]{1,0:T(8,128)(2,1)}, u32[]{:S(2)}, u32[]{:S(2)}) collective-permute-start(bf16[256,2816]{1,0:T(8,128)(2,1)} %get-tuple-element.263), channel_id=1, source_target_pairs={{0,8},{8,16},{16,24},{24,28},{28,20},{20,12},{12,4},{4,0},{1,9},{9... | collective-permute-start | bytes 4325384 | tf_op jit(solution)/shard_map/ppermute | solution.py:238
  483.9 32.0 %collective-permute-start.53 = (bf16[256,2816]{1,0:T(8,128)(2,1)S(1)}, bf16[256,2816]{1,0:T(8,128)(2,1)}, u32[]{:S(2)}, u32[]{:S(2)}) collective-permute-start(bf16[256,2816]{1,0:T(8,128)(2,1)S(1)} %get-tuple-element.264), channel_id=1, source_target_pairs={{8,0},{16,8},{24,16},{28,24},{20,28},{12,20},{4,12},{0,4},{9,1},{1... | collective-permute-start | bytes 4325384 | tf_op jit(solution)/shard_map/ppermute | solution.py:241
  529.8 92.3 %reduce-scatter.9.cloned.1.call-start = ((), (), s32[]{:S(2)}) async-start(), calls=%async_computation.10 | async-start | bytes 5242880 | tf_op jit(solution)/shard_map/reduce_scatter | solution.py:496
  533.6 28.4 %collective-permute-start.54 = (bf16[1408,256]{1,0:T(8,128)(2,1)S(1)}, bf16[1408,256]{1,0:T(8,128)(2,1)S(1)}, u32[]{:S(2)}, u32[]{:S(2)}) collective-permute-start(bf16[1408,256]{1,0:T(8,128)(2,1)S(1)} %copy-done.35), channel_id=1, source_target_pairs={{0,8},{8,16},{16,24},{24,28},{28,20},{20,12},{12,4},{4,0},{1,9},{9... | collective-permute-start | bytes 2162696 | tf_op jit(solution)/shard_map/ppermute | solution.py:238
  (121 other events, 1455.0 us)
Sparse Core Ops, SparseCore 0:
  9.6 37.1 all-gather.4
  175.3 44.9 reduce-scatter.4
  225.7 34.4 all-gather.6
  261.7 34.4 all-gather.8
  394.2 43.8 reduce-scatter.6
  443.3 34.4 all-gather.10
  529.9 42.9 reduce-scatter.10
  575.6 45.0 reduce-scatter.8

commit v5 on v4

--- a/solution.py
+++ b/solution.py
@@ -551,8 +551,8 @@
     g_up.hop()
     h2 = g_gu.settle(after(tensor_gather(h2_own), g_gu.left, g_gu.right, g_up.left, g_up.right))
     down2 = g_down.hop(g_up.left, g_up.right)
-    g_gu.store()
-    w_gu = g_up.result()
+    g_up.store()
+    w_gu = g_gu.result()
     gu = after(mm(h2, w_gu, NN), *down2)
     down3 = g_down.hop(gu)
     gate, up = gu[:, :hidden_width], gu[:, hidden_width:]
@@ -595,8 +595,8 @@
     step4 = s_down.hop(before=(dproj,), during=(dh1_part,))
     s_out.hop(before=(dproj,), during=(dh1_part,))
     s_in = ring.scatter_sum(mm(after(h1, dh1_part), dproj, TN).astype(BF16), 0)
-    o2 = s_out.hop(before=(s_in.left, s_in.right))
     s_in.hop(before=step4)
+    o2 = s_out.hop(during=(s_in.left, s_in.right))
     r1 = lax.rsqrt(jnp.mean(x * x, axis=-1, keepdims=True) + EPSILON)
     back1, d_gain_in = norm_backward(x, r1, gain_in, after(dh1, s_in.left, s_in.right))
     d_gains = jnp.concatenate(
@@ -604,18 +604,19 @@
     )
     d_gains = lax.psum(d_gains, "tensor")
     s_in.hop(before=o2, during=(d_gains,))
-    o3 = s_out.hop()
+    o3 = s_out.hop(during=(s_in.left, s_in.right))
+    d_gains = scatter_sum_small(d_gains, "dp", n_dp)
+    s_gu.arrived = after(s_gu.arrived[0], s_in.left, s_in.right), s_gu.arrived[1]
+    d_gu = s_gu.finish(2)
+    s_in.hop(before=(*o3, d_gains), during=(d_gu,))
+    d_gains = d_gains[0]
     d_tokens = after((dx2 + back1).astype(BF16), s_in.left, s_in.right)
-    d_gains = scatter_sum_small(after(d_gains, s_in.left, s_in.right), "dp", n_dp)[0]
-    s_in.hop(before=o3, during=(d_tokens,))
-    o4 = s_out.hop()
-    d_gu = after(s_gu.arrived[0], s_in.left, s_in.right)
-    s_gu.arrived = d_gu, s_gu.arrived[1]
-    d_gu = s_gu.finish(2)
-    d_down = after(s_down.result(), s_in.left, s_in.right)
+    o4 = s_out.hop(during=(s_in.left, s_in.right))
+    s_down.arrived = after(s_down.arrived[0], s_in.left, s_in.right), s_down.arrived[1]
+    d_down = s_down.result()
     d_out = after(s_out.result(), s_in.left, s_in.right)
     output = (x2 + after(ffn, s_in.left, s_in.right)).astype(BF16)
-    s_in.hop(before=o4, during=(d_gu, d_down, d_out, output))
+    s_in.hop(before=o4, during=(d_down, d_tokens))
     d_in = s_in.finish(4)
     return (
         output,

time: 690 us -> 679 us (0.984)
    ppermute x3, waiting for transfers between devices: 16 us -> 5.09 us  [scatter_sum_small(): lax.ppermute(other, axis, [(i, i ^ count) for i in range(whole)])]
    unnamed x147 -> x149, local copies, waits for them, and re-layouts: 22 us -> 22.7 us
  transfers between devices with their start and end apart: 83 -> 83, of which waited for: 35 -> 39; matrix products, arithmetic and copies ran while one was open for 30% -> 29% of each run, Pallas kernels for 16% -> 16%
where the time goes in v5:
time: 679 us; the launch traced here: 670 us
  waiting for transfers between devices  212 us (31%)
  matrix products  136 us (20%)
  Pallas kernels  113 us (17%)
  starting transfers between devices  78.3 us (12%)
  other arithmetic  66 us (10%)
  local copies, waits for them, and re-layouts  37.6 us (6%)
  between operations  15.2 us (2%)
  blocking collectives  11.1 us (2%)
    ppermute x36, waiting for transfers between devices, send_ahead(): return lax.ppermute(x, self.axis, self.ahead)  140 us
    dot_general x12, matrix products, mm(): return lax.dot_general(a, b, dims, preferred_element_type=F32)  136 us
    pallas_call x20, Pallas kernels, store(): pl.pallas_call(pair_kernel, grid_spec=pltpu.PrefetchScalarGridSpec(num_sc...  62.5 us
    ppermute x36, starting transfers between devices, send_ahead(): return lax.ppermute(x, self.axis, self.ahead)  46.2 us
    ppermute x36, waiting for transfers between devices, send_behind(): return lax.ppermute(x, self.axis, self.behind)  41.9 us
    ppermute x36, starting transfers between devices, send_behind(): return lax.ppermute(x, self.axis, self.behind)  30 us
    add x8, other arithmetic, hop(): self.left, self.right = (left + self.part(shift), right + self.part(-shift))  25.4 us
    unnamed x149, local copies, waits for them, and re-layouts  22.7 us
  transfers between devices with their start and end apart: 83, of which 39 were waited for; matrix products, arithmetic and copies ran while one was open for 29% of the time, Pallas kernels for 16%

profile of v5, /device:TPU:0, one launch (start us, length us, event | category | flops | bytes accessed | tf_op | source)
XLA Modules:
  0.0 669.7 jit_solution(13876238164453270963)
XLA Ops:
  19.0 22.7 %collective-permute-done.1.right = bf16[544,256]{1,0:T(8,128)(2,1)S(1)} collective-permute-done((bf16[544,256]{1,0:T(8,128)(2,1)S(1)}, bf16[544,256]{1,0:T(8,128)(2,1)S(1)}, u32[]{:S(2)}, u32[]{:S(2)}) %collective-permute-start.1) | collective-permute-done | bytes 278560 | tf_op jit(solution)/shard_map/ppermute | solution.py:241
  60.7 9.6 %collective-permute-done.6.left = bf16[256,2048]{1,0:T(8,128)(2,1)} collective-permute-done((bf16[256,2048]{1,0:T(8,128)(2,1)}, bf16[256,2048]{1,0:T(8,128)(2,1)}, u32[]{:S(2)}, u32[]{:S(2)}) %collective-permute-start.6) | collective-permute-done | bytes 1048608 | tf_op jit(solution)/shard_map/ppermute | solution.py:238
  87.6 16.9 %collective-permute-done.8.left = bf16[544,256]{1,0:T(8,128)(2,1)} collective-permute-done((bf16[544,256]{1,0:T(8,128)(2,1)}, bf16[544,256]{1,0:T(8,128)(2,1)}, u32[]{:S(2)}, u32[]{:S(2)}) %collective-permute-start.8) | collective-permute-done | bytes 278560 | tf_op jit(solution)/shard_map/ppermute | solution.py:238
  143.8 10.4 %convolution_convert_fusion.7.q_ref.a_ref.v_ref.z_ref = bf16[1024,2048]{1,0:T(8,128)(2,1)} fusion(bf16[1024,2048]{1,0:T(8,128)(2,1)S(1)} %fusion.2, bf16[2048,2048]{1,0:T(8,128)(2,1)S(1)} %copy-done), kind=kOutput, calls=%fused_computation.18 | convolution fusion | flops 8592031744 | bytes 16777216 | tf_op jit(solution)/shard_map/dot_general | solution.py:21
  155.1 14.0 %mixer_forward.1 = (bf16[1024,512]{1,0:T(8,128)(2,1)}, f32[1024,512]{1,0:T(8,128)}, f32[8,128,512]{2,1,0:T(8,128)}) custom-call(s32[1024]{0:T(1024)} %bitcast.71, bf16[1024,2048]{1,0:T(8,128)(2,1)} %convolution_convert_fusion.7.q_ref.a_ref.v_ref.z_ref, bf16[1024,2048]{1,0:T(8,128)(2,1)} %convolution_convert_fusion.7.q_ref.a_ref.v_ref.z_ref, ...), custom_call_target="tpu_custom_call" | custom-call | flops 30000001024 | bytes 10000000 | tf_op jit(solution)/shard_map/mixer_forward/pallas_call | solution.py:166
  169.1 5.6 convolution_convert_fusion.6
  186.8 8.3 %collective-permute-done.22.left = bf16[256,1408]{1,0:T(8,128)(2,1)} collective-permute-done((bf16[256,1408]{1,0:T(8,128)(2,1)S(1)}, bf16[256,1408]{1,0:T(8,128)(2,1)}, u32[]{:S(2)}, u32[]{:S(2)}) %collective-permute-start.22) | collective-permute-done | bytes 720928 | tf_op jit(solution)/shard_map/ppermute | solution.py:238
  205.4 14.8 %reduce-scatter.5.cloned.1.call-done = bf16[256,2048]{1,0:T(8,128)(2,1)} async-done(((bf16[1024,2048]{1,0:T(8,128)(2,1)}), bf16[256,2048]{1,0:T(8,128)(2,1)}) %reduce-scatter.5.cloned.1.call-update) | async-done | bytes 1048592 | tf_op jit(solution)/shard_map/reduce_scatter | solution.py:496
  235.8 8.5 %collective-permute-done.30.left = bf16[256,1408]{1,0:T(8,128)(2,1)S(1)} collective-permute-done((bf16[256,1408]{1,0:T(8,128)(2,1)}, bf16[256,1408]{1,0:T(8,128)(2,1)S(1)}, u32[]{:S(2)}, u32[]{:S(2)}) %collective-permute-start.30) | collective-permute-done | bytes 720928 | tf_op jit(solution)/shard_map/ppermute | solution.py:238
  260.5 4.2 collective-permute-done.28.left
  271.9 17.2 %fusion.29 = f32[1024,2816]{1,0:T(8,128)S(1)} fusion(bf16[1024,2048]{1,0:T(8,128)(2,1)} %all-gather.7.cloned.1.call-done, bf16[2048,2816]{1,0:T(8,128)(2,1)} %gather_pair.36), kind=kOutput, calls=%fused_computation.109 | convolution fusion | flops 11811160064 | bytes 27262976 | tf_op jit(solution)/shard_map/dot_general | solution.py:21
  296.2 8.0 %convolution_convert_fusion.2 = bf16[1408,2048]{1,0:T(8,128)(2,1)S(1)} fusion(bf16[1024,1408]{1,0:T(8,128)(2,1)S(1)} %multiply_convert_fusion.2, bf16[1024,2048]{1,0:T(8,128)(2,1)} %all-gather.9.cloned.1.call-done), kind=kOutput, calls=%fused_computation.7 | convolution fusion | flops 5908463616 | bytes 12845056 | tf_op jit(solution)/shard_map/dot_general | solution.py:21
  330.6 14.1 %multiply_convert_fusion.1 = (bf16[1024,1408]{1,0:T(8,128)(2,1)S(1)}, bf16[1024,1408]{1,0:T(8,128)(2,1)S(1)}) fusion(f32[1024,2816]{1,0:T(8,128)} %copy-done.13, bf16[1024,2048]{1,0:T(8,128)(2,1)} %all-gather.9.cloned.1.call-done, bf16[1408,2048]{1,0:T(8,128)(2,1)} %gather_pair.39), kind=kOutput, calls=%fused_computation.10 | convolution fusion | flops 5924323328 | bytes 27262976 | tf_op jit(solution)/shard_map/dot_general | solution.py:21
  353.6 18.2 %convolution_convert_fusion.own = bf16[2048,2816]{1,0:T(8,128)(2,1)} fusion(bf16[1024,2048]{1,0:T(8,128)(2,1)} %all-gather.7.cloned.1.call-done, bf16[1024,1408]{1,0:T(8,128)(2,1)} %copy-done.20, bf16[1024,1408]{1,0:T(8,128)(2,1)S(1)} %get-tuple-element.317), kind=kOutput, calls=%fused_computation | convolution fusion | flops 11828461568 | bytes 21495808 | tf_op jit(solution)/shard_map/dot_general | solution.py:21
  378.6 15.3 %convolution_convert_fusion.3 = bf16[1024,2048]{1,0:T(8,128)(2,1)} fusion(bf16[1024,2816]{1,0:T(8,128)(2,1)} %pad_maximum_fusion, bf16[2048,2816]{1,0:T(8,128)(2,1)S(1)} %bitcast.53), kind=kOutput, calls=%fused_computation.14 | convolution fusion | flops 11813257216 | bytes 21495808 | tf_op jit(solution)/shard_map/dot_general | solution.py:21
  398.6 28.3 %collective-permute-done.48 = bf16[256,2816]{1,0:T(8,128)(2,1)S(1)} collective-permute-done((bf16[256,2816]{1,0:T(8,128)(2,1)S(1)}, bf16[256,2816]{1,0:T(8,128)(2,1)S(1)}, u32[]{:S(2)}, u32[]{:S(2)}) %collective-permute-start.48) | collective-permute-done | bytes 1441824 | tf_op jit(solution)/shard_map/ppermute | solution.py:238
  432.2 5.8 reduce-scatter.7.cloned.1.call-done
  445.2 10.9 %convolution_convert_fusion.5 = bf16[1024,2048]{1,0:T(8,128)(2,1)} fusion(bf16[1024,1408]{1,0:T(8,128)(2,1)} %copy-done.19, bf16[1408,2048]{1,0:T(8,128)(2,1)} %gather_pair.39), kind=kOutput, calls=%fused_computation.16 | convolution fusion | flops 5907677184 | bytes 12845056 | tf_op jit(solution)/shard_map/dot_general | solution.py:21
  456.0 20.7 %collective-permute-done.50 = bf16[256,2816]{1,0:T(8,128)(2,1)S(1)} collective-permute-done((bf16[256,2816]{1,0:T(8,128)(2,1)}, bf16[256,2816]{1,0:T(8,128)(2,1)S(1)}, u32[]{:S(2)}, u32[]{:S(2)}) %collective-permute-start.50) | collective-permute-done | bytes 1441824 | tf_op jit(solution)/shard_map/ppermute | solution.py:238
  477.8 4.5 dynamic-slice_add_fusion
  484.4 6.0 convolution_convert_fusion.8
  494.1 19.1 %mixer_backward.1 = (bf16[1024,2048]{1,0:T(8,128)(2,1)}, f32[1,128]{1,0:T(1,128)}) custom-call(s32[1024]{0:T(1024)} %bitcast.72, bf16[1024,2048]{1,0:T(8,128)(2,1)} %convolution_convert_fusion.7.q_ref.a_ref.v_ref.z_ref, bf16[1024,2048]{1,0:T(8,128)(2,1)} %convolution_convert_fusion.7.q_ref.a_ref.v_ref.z_ref, ...), custom_call_target="tpu_custom_call" | custom-call | flops 60000002048 | bytes 14000000 | tf_op jit(solution)/shard_map/mixer_backward/pallas_call | solution.py:193
  516.0 13.9 %convolution_convert_fusion.4 = bf16[1024,2048]{1,0:T(8,128)(2,1)} fusion(bf16[1024,2048]{1,0:T(8,128)(2,1)} %get-tuple-element.266, bf16[2048,2048]{1,0:T(8,128)(2,1)} %gather_pair.27), kind=kOutput, calls=%fused_computation.15 | convolution fusion | flops 8592031744 | bytes 16777216 | tf_op jit(solution)/shard_map/dot_general | solution.py:21
  533.2 12.6 %convolution_convert_fusion.1.own = bf16[2048,2048]{1,0:T(8,128)(2,1)S(1)} fusion(bf16[1024,2048]{1,0:T(8,128)(2,1)} %copy-done.18, bf16[1024,2048]{1,0:T(8,128)(2,1)} %get-tuple-element.266), kind=kOutput, calls=%fused_computation.6 | convolution fusion | flops 8594128896 | bytes 16777216 | tf_op jit(solution)/shard_map/dot_general | solution.py:21
  557.5 6.7 collective-permute-done.58
  580.3 11.1 %psum.7 = f32[8,528]{1,0:T(8,128)S(1)} all-reduce(f32[8,528]{1,0:T(8,128)S(1)} %pad_maximum_fusion.1), channel_id=1, replica_groups=mesh['dp'=8,'tensor'=4] {'tensor'}, use_global_device_ids=true, to_apply=%region_10.11 | all-reduce | flops 4224 | bytes 33792 | tf_op jit(solution)/shard_map/psum | solution.py:605
  592.6 5.1 collective-permute-done.66
  601.6 4.4 dynamic-slice_add_fusion.8
  610.1 4.7 finish.2
  622.9 8.4 %collective-permute-done.69 = bf16[256,2048]{1,0:T(8,128)(2,1)} collective-permute-done((bf16[256,2048]{1,0:T(8,128)(2,1)}, bf16[256,2048]{1,0:T(8,128)(2,1)}, u32[]{:S(2)}, u32[]{:S(2)}) %collective-permute-start.69) | collective-permute-done | bytes 1048608 | tf_op jit(solution)/shard_map/ppermute | solution.py:238
  644.9 13.5 %collective-permute-done.73.left = bf16[256,2048]{1,0:T(8,128)(2,1)} collective-permute-done((bf16[256,2048]{1,0:T(8,128)(2,1)S(1)}, bf16[256,2048]{1,0:T(8,128)(2,1)}, u32[]{:S(2)}, u32[]{:S(2)}) %collective-permute-start.73) | collective-permute-done | bytes 1048608 | tf_op jit(solution)/shard_map/ppermute | solution.py:238
  658.4 4.2 finish.3
  (406 shorter events, 286.9 us)
Async XLA Ops:
  7.2 129.7 %all-gather.5.cloned.1.call-start = ((), (), s32[]{:S(2)}) async-start(), calls=%async_computation.4 | async-start | bytes 5242880 | tf_op jit(solution)/shard_map/all_gather | solution.py:492
  8.0 212.2 %reduce-scatter.5.cloned.1.call-start = ((), (), s32[]{:S(2)}) async-start(), calls=%async_computation.5 | async-start | bytes 5242880 | tf_op jit(solution)/shard_map/reduce_scatter | solution.py:496
  9.5 33.6 %collective-permute-start.3 = (bf16[256,2048]{1,0:T(8,128)(2,1)S(1)}, bf16[256,2048]{1,0:T(8,128)(2,1)}, u32[]{:S(2)}, u32[]{:S(2)}) collective-permute-start(bf16[256,2048]{1,0:T(8,128)(2,1)S(1)} %bitcast.56), channel_id=1, source_target_pairs={{8,0},{16,8},{24,16},{28,24},{20,28},{12,20},{4,12},{0,4},{9,1},{1... | collective-permute-start | bytes 3145736 | tf_op jit(solution)/shard_map/ppermute | solution.py:241
  12.5 30.6 %collective-permute-start.2 = (bf16[256,2048]{1,0:T(8,128)(2,1)S(1)}, bf16[256,2048]{1,0:T(8,128)(2,1)}, u32[]{:S(2)}, u32[]{:S(2)}) collective-permute-start(bf16[256,2048]{1,0:T(8,128)(2,1)S(1)} %bitcast.57), channel_id=1, source_target_pairs={{0,8},{8,16},{16,24},{24,28},{28,20},{20,12},{12,4},{4,0},{1,9},{9... | collective-permute-start | bytes 3145736 | tf_op jit(solution)/shard_map/ppermute | solution.py:238
  12.8 29.0 %collective-permute-start.1 = (bf16[544,256]{1,0:T(8,128)(2,1)S(1)}, bf16[544,256]{1,0:T(8,128)(2,1)S(1)}, u32[]{:S(2)}, u32[]{:S(2)}) collective-permute-start(bf16[544,256]{1,0:T(8,128)(2,1)S(1)} %constant_dynamic-update-slice_fusion.block), channel_id=1, source_target_pairs={{8,0},{16,8},{24,16},{28,24},{20,28},{12,20},{4,12},{0,4},{9,1},{1... | collective-permute-start | bytes 835592 | tf_op jit(solution)/shard_map/ppermute | solution.py:241
  14.7 28.4 %collective-permute-start = (bf16[544,256]{1,0:T(8,128)(2,1)S(1)}, bf16[544,256]{1,0:T(8,128)(2,1)S(1)}, u32[]{:S(2)}, u32[]{:S(2)}) collective-permute-start(bf16[544,256]{1,0:T(8,128)(2,1)S(1)} %constant_dynamic-update-slice_fusion.block), channel_id=1, source_target_pairs={{0,8},{8,16},{16,24},{24,28},{28,20},{20,12},{12,4},{4,0},{1,9},{9... | collective-permute-start | bytes 835592 | tf_op jit(solution)/shard_map/ppermute | solution.py:238
  44.3 30.1 %collective-permute-start.7 = (bf16[256,2048]{1,0:T(8,128)(2,1)}, bf16[256,2048]{1,0:T(8,128)(2,1)S(1)}, u32[]{:S(2)}, u32[]{:S(2)}) collective-permute-start(bf16[256,2048]{1,0:T(8,128)(2,1)} %collective-permute-done.3.right), channel_id=1, source_target_pairs={{8,0},{16,8},{24,16},{28,24},{20,28},{12,20},{4,12},{0,4},{9,1},{1... | collective-permute-start | bytes 3145736 | tf_op jit(solution)/shard_map/ppermute | solution.py:241
  45.9 28.1 %collective-permute-start.4 = (bf16[544,256]{1,0:T(8,128)(2,1)}, bf16[544,256]{1,0:T(8,128)(2,1)}, u32[]{:S(2)}, u32[]{:S(2)}) collective-permute-start(bf16[544,256]{1,0:T(8,128)(2,1)} %copy-done.46), channel_id=1, source_target_pairs={{0,8},{8,16},{16,24},{24,28},{28,20},{20,12},{12,4},{4,0},{1,9},{9... | collective-permute-start | bytes 835592 | tf_op jit(solution)/shard_map/ppermute | solution.py:238
  46.3 28.1 %collective-permute-start.5 = (bf16[544,256]{1,0:T(8,128)(2,1)}, bf16[544,256]{1,0:T(8,128)(2,1)}, u32[]{:S(2)}, u32[]{:S(2)}) collective-permute-start(bf16[544,256]{1,0:T(8,128)(2,1)} %copy-done.45), channel_id=1, source_target_pairs={{8,0},{16,8},{24,16},{28,24},{20,28},{12,20},{4,12},{0,4},{9,1},{1... | collective-permute-start | bytes 835592 | tf_op jit(solution)/shard_map/ppermute | solution.py:241
  75.4 32.4 %collective-permute-start.10 = (bf16[256,2048]{1,0:T(8,128)(2,1)}, bf16[256,2048]{1,0:T(8,128)(2,1)S(1)}, u32[]{:S(2)}, u32[]{:S(2)}) collective-permute-start(bf16[256,2048]{1,0:T(8,128)(2,1)} %collective-permute-done.6.left), channel_id=1, source_target_pairs={{0,8},{8,16},{16,24},{24,28},{28,20},{20,12},{12,4},{4,0},{1,9},{9... | collective-permute-start | bytes 3145736 | tf_op jit(solution)/shard_map/ppermute | solution.py:238
  76.9 31.7 %collective-permute-start.11 = (bf16[256,2048]{1,0:T(8,128)(2,1)}, bf16[256,2048]{1,0:T(8,128)(2,1)S(1)}, u32[]{:S(2)}, u32[]{:S(2)}) collective-permute-start(bf16[256,2048]{1,0:T(8,128)(2,1)} %copy-done.29), channel_id=1, source_target_pairs={{8,0},{16,8},{24,16},{28,24},{20,28},{12,20},{4,12},{0,4},{9,1},{1... | collective-permute-start | bytes 3145736 | tf_op jit(solution)/shard_map/ppermute | solution.py:241
  77.4 27.2 %collective-permute-start.8 = (bf16[544,256]{1,0:T(8,128)(2,1)}, bf16[544,256]{1,0:T(8,128)(2,1)}, u32[]{:S(2)}, u32[]{:S(2)}) collective-permute-start(bf16[544,256]{1,0:T(8,128)(2,1)} %collective-permute-done.4.left), channel_id=1, source_target_pairs={{0,8},{8,16},{16,24},{24,28},{28,20},{20,12},{12,4},{4,0},{1,9},{9... | collective-permute-start | bytes 835592 | tf_op jit(solution)/shard_map/ppermute | solution.py:238
  129.9 44.8 %collective-permute-start.17 = (bf16[256,1408]{1,0:T(8,128)(2,1)}, bf16[256,1408]{1,0:T(8,128)(2,1)}, u32[]{:S(2)}, u32[]{:S(2)}) collective-permute-start(bf16[256,1408]{1,0:T(8,128)(2,1)} %get-tuple-element.181), channel_id=1, source_target_pairs={{8,0},{16,8},{24,16},{28,24},{20,28},{12,20},{4,12},{0,4},{9,1},{1... | collective-permute-start | bytes 2162696 | tf_op jit(solution)/shard_map/ppermute | solution.py:241
  130.4 44.4 %collective-permute-start.18 = (bf16[256,1408]{1,0:T(8,128)(2,1)}, bf16[256,1408]{1,0:T(8,128)(2,1)}, u32[]{:S(2)}, u32[]{:S(2)}) collective-permute-start(bf16[256,1408]{1,0:T(8,128)(2,1)} %get-tuple-element.183), channel_id=1, source_target_pairs={{0,8},{8,16},{16,24},{24,28},{28,20},{20,12},{12,4},{4,0},{1,9},{9... | collective-permute-start | bytes 2162696 | tf_op jit(solution)/shard_map/ppermute | solution.py:238
  132.0 42.8 %collective-permute-start.19 = (bf16[256,1408]{1,0:T(8,128)(2,1)}, bf16[256,1408]{1,0:T(8,128)(2,1)}, u32[]{:S(2)}, u32[]{:S(2)}) collective-permute-start(bf16[256,1408]{1,0:T(8,128)(2,1)} %get-tuple-element.183), channel_id=1, source_target_pairs={{8,0},{16,8},{24,16},{28,24},{20,28},{12,20},{4,12},{0,4},{9,1},{1... | collective-permute-start | bytes 2162696 | tf_op jit(solution)/shard_map/ppermute | solution.py:241
  132.4 42.4 %collective-permute-start.20 = (bf16[1408,256]{1,0:T(8,128)(2,1)S(1)}, bf16[1408,256]{1,0:T(8,128)(2,1)}, u32[]{:S(2)}, u32[]{:S(2)}) collective-permute-start(bf16[1408,256]{1,0:T(8,128)(2,1)S(1)} %copy-done.30), channel_id=1, source_target_pairs={{0,8},{8,16},{16,24},{24,28},{28,20},{20,12},{12,4},{4,0},{1,9},{9... | collective-permute-start | bytes 2162696 | tf_op jit(solution)/shard_map/ppermute | solution.py:238
  175.1 91.1 %all-gather.7.cloned.1.call-start = ((), (), s32[]{:S(2)}) async-start(), calls=%async_computation.6 | async-start | bytes 5242880 | tf_op jit(solution)/shard_map/all_gather | solution.py:492
  181.1 40.6 %collective-permute-start.26 = (bf16[256,1408]{1,0:T(8,128)(2,1)}, bf16[256,1408]{1,0:T(8,128)(2,1)}, u32[]{:S(2)}, u32[]{:S(2)}) collective-permute-start(bf16[256,1408]{1,0:T(8,128)(2,1)} %collective-permute-done.18.left), channel_id=1, source_target_pairs={{0,8},{8,16},{16,24},{24,28},{28,20},{20,12},{12,4},{4,0},{1,9},{9... | collective-permute-start | bytes 2162696 | tf_op jit(solution)/shard_map/ppermute | solution.py:238
  182.7 39.0 %collective-permute-start.27 = (bf16[256,1408]{1,0:T(8,128)(2,1)}, bf16[256,1408]{1,0:T(8,128)(2,1)S(1)}, u32[]{:S(2)}, u32[]{:S(2)}) collective-permute-start(bf16[256,1408]{1,0:T(8,128)(2,1)} %collective-permute-done.19.right), channel_id=1, source_target_pairs={{8,0},{16,8},{24,16},{28,24},{20,28},{12,20},{4,12},{0,4},{9,1},{1... | collective-permute-start | bytes 2162696 | tf_op jit(solution)/shard_map/ppermute | solution.py:241
  225.5 70.6 %all-gather.9.cloned.1.call-start = ((), (), s32[]{:S(2)}) async-start(), calls=%async_computation.7 | async-start | bytes 5242880 | tf_op jit(solution)/shard_map/all_gather | solution.py:492
  226.1 211.8 %reduce-scatter.7.cloned.1.call-start = ((), (), s32[]{:S(2)}) async-start(), calls=%async_computation.8 | async-start | bytes 5242880 | tf_op jit(solution)/shard_map/reduce_scatter | solution.py:496
  258.5 30.6 %collective-permute-start.34 = (bf16[1408,256]{1,0:T(8,128)(2,1)}, bf16[1408,256]{1,0:T(8,128)(2,1)}, u32[]{:S(2)}, u32[]{:S(2)}) collective-permute-start(bf16[1408,256]{1,0:T(8,128)(2,1)} %collective-permute-done.20.left), channel_id=1, source_target_pairs={{0,8},{8,16},{16,24},{24,28},{28,20},{20,12},{12,4},{4,0},{1,9},{9... | collective-permute-start | bytes 2162696 | tf_op jit(solution)/shard_map/ppermute | solution.py:238
  260.0 29.1 %collective-permute-start.35 = (bf16[1408,256]{1,0:T(8,128)(2,1)}, bf16[1408,256]{1,0:T(8,128)(2,1)}, u32[]{:S(2)}, u32[]{:S(2)}) collective-permute-start(bf16[1408,256]{1,0:T(8,128)(2,1)} %collective-permute-done.21.right), channel_id=1, source_target_pairs={{8,0},{16,8},{24,16},{28,24},{20,28},{12,20},{4,12},{0,4},{9,1},{1... | collective-permute-start | bytes 2162696 | tf_op jit(solution)/shard_map/ppermute | solution.py:241
  393.9 90.4 %all-gather.11.cloned.1.call-start = ((), (), s32[]{:S(2)}) async-start(), calls=%async_computation.9 | async-start | bytes 5242880 | tf_op jit(solution)/shard_map/all_gather | solution.py:492
  396.1 30.8 %collective-permute-start.48 = (bf16[256,2816]{1,0:T(8,128)(2,1)S(1)}, bf16[256,2816]{1,0:T(8,128)(2,1)S(1)}, u32[]{:S(2)}, u32[]{:S(2)}) collective-permute-start(bf16[256,2816]{1,0:T(8,128)(2,1)S(1)} %get-tuple-element.246), channel_id=1, source_target_pairs={{0,8},{8,16},{16,24},{24,28},{28,20},{20,12},{12,4},{4,0},{1,9},{9... | collective-permute-start | bytes 4325384 | tf_op jit(solution)/shard_map/ppermute | solution.py:238
  397.7 30.8 %collective-permute-start.49 = (bf16[256,2816]{1,0:T(8,128)(2,1)S(1)}, bf16[256,2816]{1,0:T(8,128)(2,1)S(1)}, u32[]{:S(2)}, u32[]{:S(2)}) collective-permute-start(bf16[256,2816]{1,0:T(8,128)(2,1)S(1)} %get-tuple-element.247), channel_id=1, source_target_pairs={{8,0},{16,8},{24,16},{28,24},{20,28},{12,20},{4,12},{0,4},{9,1},{1... | collective-permute-start | bytes 4325384 | tf_op jit(solution)/shard_map/ppermute | solution.py:241
  443.0 135.1 %reduce-scatter.11.cloned.1.call-start = ((), (), s32[]{:S(2)}) async-start(), calls=%async_computation.11 | async-start | bytes 5242880 | tf_op jit(solution)/shard_map/reduce_scatter | solution.py:496
  443.1 33.6 %collective-permute-start.50 = (bf16[256,2816]{1,0:T(8,128)(2,1)}, bf16[256,2816]{1,0:T(8,128)(2,1)S(1)}, u32[]{:S(2)}, u32[]{:S(2)}) collective-permute-start(bf16[256,2816]{1,0:T(8,128)(2,1)} %get-tuple-element.252), channel_id=1, source_target_pairs={{0,8},{8,16},{16,24},{24,28},{28,20},{20,12},{12,4},{4,0},{1,9},{9... | collective-permute-start | bytes 4325384 | tf_op jit(solution)/shard_map/ppermute | solution.py:238
  444.6 33.2 %collective-permute-start.51 = (bf16[256,2816]{1,0:T(8,128)(2,1)S(1)}, bf16[256,2816]{1,0:T(8,128)(2,1)}, u32[]{:S(2)}, u32[]{:S(2)}) collective-permute-start(bf16[256,2816]{1,0:T(8,128)(2,1)S(1)} %get-tuple-element.253), channel_id=1, source_target_pairs={{8,0},{16,8},{24,16},{28,24},{20,28},{12,20},{4,12},{0,4},{9,1},{1... | collective-permute-start | bytes 4325384 | tf_op jit(solution)/shard_map/ppermute | solution.py:241
  482.3 32.5 %collective-permute-start.52 = (bf16[256,2816]{1,0:T(8,128)(2,1)}, bf16[256,2816]{1,0:T(8,128)(2,1)}, u32[]{:S(2)}, u32[]{:S(2)}) collective-permute-start(bf16[256,2816]{1,0:T(8,128)(2,1)} %get-tuple-element.262), channel_id=1, source_target_pairs={{0,8},{8,16},{16,24},{24,28},{28,20},{20,12},{12,4},{4,0},{1,9},{9... | collective-permute-start | bytes 4325384 | tf_op jit(solution)/shard_map/ppermute | solution.py:238
  483.8 32.2 %collective-permute-start.53 = (bf16[256,2816]{1,0:T(8,128)(2,1)}, bf16[256,2816]{1,0:T(8,128)(2,1)}, u32[]{:S(2)}, u32[]{:S(2)}) collective-permute-start(bf16[256,2816]{1,0:T(8,128)(2,1)} %get-tuple-element.263), channel_id=1, source_target_pairs={{8,0},{16,8},{24,16},{28,24},{20,28},{12,20},{4,12},{0,4},{9,1},{1... | collective-permute-start | bytes 4325384 | tf_op jit(solution)/shard_map/ppermute | solution.py:241
  530.0 90.3 %reduce-scatter.9.cloned.1.call-start = ((), (), s32[]{:S(2)}) async-start(), calls=%async_computation.10 | async-start | bytes 5242880 | tf_op jit(solution)/shard_map/reduce_scatter | solution.py:496
  (122 other events, 1456.2 us)
Sparse Core Ops, SparseCore 0:
  9.6 37.1 all-gather.4
  175.2 44.9 reduce-scatter.4
  225.6 34.4 all-gather.6
  261.6 34.4 all-gather.8
  394.0 43.8 reduce-scatter.6
  443.2 34.4 all-gather.10
  530.1 42.9 reduce-scatter.10
  575.7 44.5 reduce-scatter.8

commit v6 on v5

--- a/solution.py
+++ b/solution.py
@@ -8,7 +8,7 @@
 from jax.sharding import PartitionSpec as P
 
 HD = 128
-CHUNK = 128
+CHUNK = 256
 GROUP_EPSILON = 0.01
 F32 = jnp.float32
 BF16 = jnp.bfloat16

time: 679 us -> 680 us (level)
  waiting for transfers between devices: 212 us -> 219 us
  transfers between devices with their start and end apart: 83 -> 83, of which waited for: 39 -> 40; matrix products, arithmetic and copies ran while one was open for 29% -> 29% of each run, Pallas kernels for 16% -> 15%
where the time goes in v6:
time: 680 us; the launch traced here: 671 us
  waiting for transfers between devices  219 us (32%)
  matrix products  136 us (20%)
  Pallas kernels  107 us (16%)
  starting transfers between devices  78.5 us (12%)
  other arithmetic  66.1 us (10%)
  local copies, waits for them, and re-layouts  37.4 us (6%)
  between operations  15.5 us (2%)
  blocking collectives  11.1 us (2%)
    ppermute x36, waiting for transfers between devices, send_ahead(): return lax.ppermute(x, self.axis, self.ahead)  146 us
    dot_general x12, matrix products, mm(): return lax.dot_general(a, b, dims, preferred_element_type=F32)  136 us
    pallas_call x20, Pallas kernels, store(): pl.pallas_call(pair_kernel, grid_spec=pltpu.PrefetchScalarGridSpec(num_sc...  62.4 us
    ppermute x36, starting transfers between devices, send_ahead(): return lax.ppermute(x, self.axis, self.ahead)  46.9 us
    ppermute x36, waiting for transfers between devices, send_behind(): return lax.ppermute(x, self.axis, self.behind)  42.9 us
    ppermute x36, starting transfers between devices, send_behind(): return lax.ppermute(x, self.axis, self.behind)  29.3 us
    add x8, other arithmetic, hop(): self.left, self.right = (left + self.part(shift), right + self.part(-shift))  25.4 us
    reduce_scatter x4, waiting for transfers between devices, tensor_scatter_sum(): lax.psum_scatter(x, 'tensor', scatter_dimension=0, tiled=True).astype(F32)  22.6 us
  transfers between devices with their start and end apart: 83, of which 40 were waited for; matrix products, arithmetic and copies ran while one was open for 29% of the time, Pallas kernels for 15%

profile of v6, /device:TPU:0, one launch (start us, length us, event | category | flops | bytes accessed | tf_op | source)
XLA Modules:
  0.0 670.9 jit_solution(6156645973187361089)
XLA Ops:
  19.0 22.7 %collective-permute-done.1.right = bf16[544,256]{1,0:T(8,128)(2,1)S(1)} collective-permute-done((bf16[544,256]{1,0:T(8,128)(2,1)S(1)}, bf16[544,256]{1,0:T(8,128)(2,1)S(1)}, u32[]{:S(2)}, u32[]{:S(2)}) %collective-permute-start.1) | collective-permute-done | bytes 278560 | tf_op jit(solution)/shard_map/ppermute | solution.py:241
  60.7 9.6 %collective-permute-done.6.left = bf16[256,2048]{1,0:T(8,128)(2,1)} collective-permute-done((bf16[256,2048]{1,0:T(8,128)(2,1)}, bf16[256,2048]{1,0:T(8,128)(2,1)}, u32[]{:S(2)}, u32[]{:S(2)}) %collective-permute-start.6) | collective-permute-done | bytes 1048608 | tf_op jit(solution)/shard_map/ppermute | solution.py:238
  87.6 16.9 %collective-permute-done.8.left = bf16[544,256]{1,0:T(8,128)(2,1)} collective-permute-done((bf16[544,256]{1,0:T(8,128)(2,1)}, bf16[544,256]{1,0:T(8,128)(2,1)}, u32[]{:S(2)}, u32[]{:S(2)}) %collective-permute-start.8) | collective-permute-done | bytes 278560 | tf_op jit(solution)/shard_map/ppermute | solution.py:238
  143.7 10.4 %convolution_convert_fusion.7.q_ref.a_ref.v_ref.z_ref = bf16[1024,2048]{1,0:T(8,128)(2,1)} fusion(bf16[1024,2048]{1,0:T(8,128)(2,1)S(1)} %fusion.2, bf16[2048,2048]{1,0:T(8,128)(2,1)S(1)} %copy-done), kind=kOutput, calls=%fused_computation.18 | convolution fusion | flops 8592031744 | bytes 16777216 | tf_op jit(solution)/shard_map/dot_general | solution.py:21
  155.0 11.6 %mixer_forward.1 = (bf16[1024,512]{1,0:T(8,128)(2,1)}, f32[1024,512]{1,0:T(8,128)}, f32[4,128,512]{2,1,0:T(8,128)}) custom-call(s32[1024]{0:T(1024)} %bitcast.71, bf16[1024,2048]{1,0:T(8,128)(2,1)} %convolution_convert_fusion.7.q_ref.a_ref.v_ref.z_ref, bf16[1024,2048]{1,0:T(8,128)(2,1)} %convolution_convert_fusion.7.q_ref.a_ref.v_ref.z_ref, ...), custom_call_target="tpu_custom_call" | custom-call | flops 30000001024 | bytes 10000000 | tf_op jit(solution)/shard_map/mixer_forward/pallas_call | solution.py:166
  166.6 5.6 convolution_convert_fusion.6
  186.8 8.4 %collective-permute-done.22.left = bf16[256,1408]{1,0:T(8,128)(2,1)} collective-permute-done((bf16[256,1408]{1,0:T(8,128)(2,1)S(1)}, bf16[256,1408]{1,0:T(8,128)(2,1)}, u32[]{:S(2)}, u32[]{:S(2)}) %collective-permute-start.22) | collective-permute-done | bytes 720928 | tf_op jit(solution)/shard_map/ppermute | solution.py:238
  205.7 15.4 %reduce-scatter.5.cloned.1.call-done = bf16[256,2048]{1,0:T(8,128)(2,1)} async-done(((bf16[1024,2048]{1,0:T(8,128)(2,1)}), bf16[256,2048]{1,0:T(8,128)(2,1)}) %reduce-scatter.5.cloned.1.call-update) | async-done | bytes 1048592 | tf_op jit(solution)/shard_map/reduce_scatter | solution.py:496
  236.7 8.5 %collective-permute-done.30.left = bf16[256,1408]{1,0:T(8,128)(2,1)S(1)} collective-permute-done((bf16[256,1408]{1,0:T(8,128)(2,1)}, bf16[256,1408]{1,0:T(8,128)(2,1)S(1)}, u32[]{:S(2)}, u32[]{:S(2)}) %collective-permute-start.30) | collective-permute-done | bytes 720928 | tf_op jit(solution)/shard_map/ppermute | solution.py:238
  272.7 17.2 %fusion.29 = f32[1024,2816]{1,0:T(8,128)S(1)} fusion(bf16[1024,2048]{1,0:T(8,128)(2,1)} %all-gather.7.cloned.1.call-done, bf16[2048,2816]{1,0:T(8,128)(2,1)} %gather_pair.36), kind=kOutput, calls=%fused_computation.109 | convolution fusion | flops 11811160064 | bytes 27262976 | tf_op jit(solution)/shard_map/dot_general | solution.py:21
  297.0 8.0 %convolution_convert_fusion.2 = bf16[1408,2048]{1,0:T(8,128)(2,1)S(1)} fusion(bf16[1024,1408]{1,0:T(8,128)(2,1)S(1)} %multiply_convert_fusion.2, bf16[1024,2048]{1,0:T(8,128)(2,1)} %all-gather.9.cloned.1.call-done), kind=kOutput, calls=%fused_computation.7 | convolution fusion | flops 5908463616 | bytes 12845056 | tf_op jit(solution)/shard_map/dot_general | solution.py:21
  331.3 14.1 %multiply_convert_fusion.1 = (bf16[1024,1408]{1,0:T(8,128)(2,1)S(1)}, bf16[1024,1408]{1,0:T(8,128)(2,1)S(1)}) fusion(f32[1024,2816]{1,0:T(8,128)} %copy-done.13, bf16[1024,2048]{1,0:T(8,128)(2,1)} %all-gather.9.cloned.1.call-done, bf16[1408,2048]{1,0:T(8,128)(2,1)} %gather_pair.39), kind=kOutput, calls=%fused_computation.10 | convolution fusion | flops 5924323328 | bytes 27262976 | tf_op jit(solution)/shard_map/dot_general | solution.py:21
  354.1 18.2 %convolution_convert_fusion.own = bf16[2048,2816]{1,0:T(8,128)(2,1)} fusion(bf16[1024,2048]{1,0:T(8,128)(2,1)} %all-gather.7.cloned.1.call-done, bf16[1024,1408]{1,0:T(8,128)(2,1)} %copy-done.20, bf16[1024,1408]{1,0:T(8,128)(2,1)S(1)} %get-tuple-element.317), kind=kOutput, calls=%fused_computation | convolution fusion | flops 11828461568 | bytes 21495808 | tf_op jit(solution)/shard_map/dot_general | solution.py:21
  379.2 15.3 %convolution_convert_fusion.3 = bf16[1024,2048]{1,0:T(8,128)(2,1)} fusion(bf16[1024,2816]{1,0:T(8,128)(2,1)} %pad_maximum_fusion, bf16[2048,2816]{1,0:T(8,128)(2,1)S(1)} %bitcast.53), kind=kOutput, calls=%fused_computation.14 | convolution fusion | flops 11813257216 | bytes 21495808 | tf_op jit(solution)/shard_map/dot_general | solution.py:21
  398.8 28.9 %collective-permute-done.48 = bf16[256,2816]{1,0:T(8,128)(2,1)S(1)} collective-permute-done((bf16[256,2816]{1,0:T(8,128)(2,1)S(1)}, bf16[256,2816]{1,0:T(8,128)(2,1)S(1)}, u32[]{:S(2)}, u32[]{:S(2)}) %collective-permute-start.48) | collective-permute-done | bytes 1441824 | tf_op jit(solution)/shard_map/ppermute | solution.py:238
  432.5 6.3 reduce-scatter.7.cloned.1.call-done
  446.1 10.9 %convolution_convert_fusion.5 = bf16[1024,2048]{1,0:T(8,128)(2,1)} fusion(bf16[1024,1408]{1,0:T(8,128)(2,1)} %copy-done.19, bf16[1408,2048]{1,0:T(8,128)(2,1)} %gather_pair.39), kind=kOutput, calls=%fused_computation.16 | convolution fusion | flops 5907677184 | bytes 12845056 | tf_op jit(solution)/shard_map/dot_general | solution.py:21
  456.9 20.6 %collective-permute-done.50 = bf16[256,2816]{1,0:T(8,128)(2,1)S(1)} collective-permute-done((bf16[256,2816]{1,0:T(8,128)(2,1)}, bf16[256,2816]{1,0:T(8,128)(2,1)S(1)}, u32[]{:S(2)}, u32[]{:S(2)}) %collective-permute-start.50) | collective-permute-done | bytes 1441824 | tf_op jit(solution)/shard_map/ppermute | solution.py:238
  478.7 4.5 dynamic-slice_add_fusion
  485.4 6.0 convolution_convert_fusion.8
  495.2 15.6 %mixer_backward.1 = (bf16[1024,2048]{1,0:T(8,128)(2,1)}, f32[1,128]{1,0:T(1,128)}) custom-call(s32[1024]{0:T(1024)} %bitcast.72, bf16[1024,2048]{1,0:T(8,128)(2,1)} %convolution_convert_fusion.7.q_ref.a_ref.v_ref.z_ref, bf16[1024,2048]{1,0:T(8,128)(2,1)} %convolution_convert_fusion.7.q_ref.a_ref.v_ref.z_ref, ...), custom_call_target="tpu_custom_call" | custom-call | flops 60000002048 | bytes 14000000 | tf_op jit(solution)/shard_map/mixer_backward/pallas_call | solution.py:193
  510.8 4.9 collective-permute-done.52.left
  517.1 13.9 %convolution_convert_fusion.4 = bf16[1024,2048]{1,0:T(8,128)(2,1)} fusion(bf16[1024,2048]{1,0:T(8,128)(2,1)} %get-tuple-element.266, bf16[2048,2048]{1,0:T(8,128)(2,1)} %gather_pair.27), kind=kOutput, calls=%fused_computation.15 | convolution fusion | flops 8592031744 | bytes 16777216 | tf_op jit(solution)/shard_map/dot_general | solution.py:21
  534.4 12.5 %convolution_convert_fusion.1.own = bf16[2048,2048]{1,0:T(8,128)(2,1)S(1)} fusion(bf16[1024,2048]{1,0:T(8,128)(2,1)} %copy-done.18, bf16[1024,2048]{1,0:T(8,128)(2,1)} %get-tuple-element.266), kind=kOutput, calls=%fused_computation.6 | convolution fusion | flops 8594128896 | bytes 16777216 | tf_op jit(solution)/shard_map/dot_general | solution.py:21
  558.5 6.7 %collective-permute-done.58 = bf16[256,256]{1,0:T(8,128)(2,1)S(1)} collective-permute-done((bf16[256,256]{1,0:T(8,128)(2,1)S(1)}, bf16[256,256]{1,0:T(8,128)(2,1)S(1)}, u32[]{:S(2)}, u32[]{:S(2)}) %collective-permute-start.58) | collective-permute-done | bytes 131104 | tf_op jit(solution)/shard_map/ppermute | solution.py:238
  581.5 11.1 %psum.7 = f32[8,528]{1,0:T(8,128)S(1)} all-reduce(f32[8,528]{1,0:T(8,128)S(1)} %pad_maximum_fusion.1), channel_id=1, replica_groups=mesh['dp'=8,'tensor'=4] {'tensor'}, use_global_device_ids=true, to_apply=%region_10.11 | all-reduce | flops 4224 | bytes 33792 | tf_op jit(solution)/shard_map/psum | solution.py:605
  594.0 4.9 collective-permute-done.66
  602.9 4.4 dynamic-slice_add_fusion.8
  611.7 4.7 finish.2
  624.0 8.5 %collective-permute-done.69 = bf16[256,2048]{1,0:T(8,128)(2,1)} collective-permute-done((bf16[256,2048]{1,0:T(8,128)(2,1)}, bf16[256,2048]{1,0:T(8,128)(2,1)}, u32[]{:S(2)}, u32[]{:S(2)}) %collective-permute-start.69) | collective-permute-done | bytes 1048608 | tf_op jit(solution)/shard_map/ppermute | solution.py:238
  646.1 13.1 %collective-permute-done.73.left = bf16[256,2048]{1,0:T(8,128)(2,1)} collective-permute-done((bf16[256,2048]{1,0:T(8,128)(2,1)S(1)}, bf16[256,2048]{1,0:T(8,128)(2,1)}, u32[]{:S(2)}, u32[]{:S(2)}) %collective-permute-start.73) | collective-permute-done | bytes 1048608 | tf_op jit(solution)/shard_map/ppermute | solution.py:238
  659.4 4.2 finish.3
  (406 shorter events, 291.8 us)
Async XLA Ops:
  7.2 129.7 %all-gather.5.cloned.1.call-start = ((), (), s32[]{:S(2)}) async-start(), calls=%async_computation.4 | async-start | bytes 5242880 | tf_op jit(solution)/shard_map/all_gather | solution.py:492
  8.0 213.1 %reduce-scatter.5.cloned.1.call-start = ((), (), s32[]{:S(2)}) async-start(), calls=%async_computation.5 | async-start | bytes 5242880 | tf_op jit(solution)/shard_map/reduce_scatter | solution.py:496
  9.5 33.6 %collective-permute-start.3 = (bf16[256,2048]{1,0:T(8,128)(2,1)S(1)}, bf16[256,2048]{1,0:T(8,128)(2,1)}, u32[]{:S(2)}, u32[]{:S(2)}) collective-permute-start(bf16[256,2048]{1,0:T(8,128)(2,1)S(1)} %bitcast.56), channel_id=1, source_target_pairs={{8,0},{16,8},{24,16},{28,24},{20,28},{12,20},{4,12},{0,4},{9,1},{1... | collective-permute-start | bytes 3145736 | tf_op jit(solution)/shard_map/ppermute | solution.py:241
  12.5 30.6 %collective-permute-start.2 = (bf16[256,2048]{1,0:T(8,128)(2,1)S(1)}, bf16[256,2048]{1,0:T(8,128)(2,1)}, u32[]{:S(2)}, u32[]{:S(2)}) collective-permute-start(bf16[256,2048]{1,0:T(8,128)(2,1)S(1)} %bitcast.57), channel_id=1, source_target_pairs={{0,8},{8,16},{16,24},{24,28},{28,20},{20,12},{12,4},{4,0},{1,9},{9... | collective-permute-start | bytes 3145736 | tf_op jit(solution)/shard_map/ppermute | solution.py:238
  12.8 29.0 %collective-permute-start.1 = (bf16[544,256]{1,0:T(8,128)(2,1)S(1)}, bf16[544,256]{1,0:T(8,128)(2,1)S(1)}, u32[]{:S(2)}, u32[]{:S(2)}) collective-permute-start(bf16[544,256]{1,0:T(8,128)(2,1)S(1)} %constant_dynamic-update-slice_fusion.block), channel_id=1, source_target_pairs={{8,0},{16,8},{24,16},{28,24},{20,28},{12,20},{4,12},{0,4},{9,1},{1... | collective-permute-start | bytes 835592 | tf_op jit(solution)/shard_map/ppermute | solution.py:241
  14.7 28.4 %collective-permute-start = (bf16[544,256]{1,0:T(8,128)(2,1)S(1)}, bf16[544,256]{1,0:T(8,128)(2,1)S(1)}, u32[]{:S(2)}, u32[]{:S(2)}) collective-permute-start(bf16[544,256]{1,0:T(8,128)(2,1)S(1)} %constant_dynamic-update-slice_fusion.block), channel_id=1, source_target_pairs={{0,8},{8,16},{16,24},{24,28},{28,20},{20,12},{12,4},{4,0},{1,9},{9... | collective-permute-start | bytes 835592 | tf_op jit(solution)/shard_map/ppermute | solution.py:238
  44.3 30.1 %collective-permute-start.7 = (bf16[256,2048]{1,0:T(8,128)(2,1)}, bf16[256,2048]{1,0:T(8,128)(2,1)S(1)}, u32[]{:S(2)}, u32[]{:S(2)}) collective-permute-start(bf16[256,2048]{1,0:T(8,128)(2,1)} %collective-permute-done.3.right), channel_id=1, source_target_pairs={{8,0},{16,8},{24,16},{28,24},{20,28},{12,20},{4,12},{0,4},{9,1},{1... | collective-permute-start | bytes 3145736 | tf_op jit(solution)/shard_map/ppermute | solution.py:241
  45.9 28.1 %collective-permute-start.4 = (bf16[544,256]{1,0:T(8,128)(2,1)}, bf16[544,256]{1,0:T(8,128)(2,1)}, u32[]{:S(2)}, u32[]{:S(2)}) collective-permute-start(bf16[544,256]{1,0:T(8,128)(2,1)} %copy-done.46), channel_id=1, source_target_pairs={{0,8},{8,16},{16,24},{24,28},{28,20},{20,12},{12,4},{4,0},{1,9},{9... | collective-permute-start | bytes 835592 | tf_op jit(solution)/shard_map/ppermute | solution.py:238
  46.3 28.1 %collective-permute-start.5 = (bf16[544,256]{1,0:T(8,128)(2,1)}, bf16[544,256]{1,0:T(8,128)(2,1)}, u32[]{:S(2)}, u32[]{:S(2)}) collective-permute-start(bf16[544,256]{1,0:T(8,128)(2,1)} %copy-done.45), channel_id=1, source_target_pairs={{8,0},{16,8},{24,16},{28,24},{20,28},{12,20},{4,12},{0,4},{9,1},{1... | collective-permute-start | bytes 835592 | tf_op jit(solution)/shard_map/ppermute | solution.py:241
  75.4 32.4 %collective-permute-start.10 = (bf16[256,2048]{1,0:T(8,128)(2,1)}, bf16[256,2048]{1,0:T(8,128)(2,1)S(1)}, u32[]{:S(2)}, u32[]{:S(2)}) collective-permute-start(bf16[256,2048]{1,0:T(8,128)(2,1)} %collective-permute-done.6.left), channel_id=1, source_target_pairs={{0,8},{8,16},{16,24},{24,28},{28,20},{20,12},{12,4},{4,0},{1,9},{9... | collective-permute-start | bytes 3145736 | tf_op jit(solution)/shard_map/ppermute | solution.py:238
  76.9 31.7 %collective-permute-start.11 = (bf16[256,2048]{1,0:T(8,128)(2,1)}, bf16[256,2048]{1,0:T(8,128)(2,1)S(1)}, u32[]{:S(2)}, u32[]{:S(2)}) collective-permute-start(bf16[256,2048]{1,0:T(8,128)(2,1)} %copy-done.29), channel_id=1, source_target_pairs={{8,0},{16,8},{24,16},{28,24},{20,28},{12,20},{4,12},{0,4},{9,1},{1... | collective-permute-start | bytes 3145736 | tf_op jit(solution)/shard_map/ppermute | solution.py:241
  77.4 27.2 %collective-permute-start.8 = (bf16[544,256]{1,0:T(8,128)(2,1)}, bf16[544,256]{1,0:T(8,128)(2,1)}, u32[]{:S(2)}, u32[]{:S(2)}) collective-permute-start(bf16[544,256]{1,0:T(8,128)(2,1)} %collective-permute-done.4.left), channel_id=1, source_target_pairs={{0,8},{8,16},{16,24},{24,28},{28,20},{20,12},{12,4},{4,0},{1,9},{9... | collective-permute-start | bytes 835592 | tf_op jit(solution)/shard_map/ppermute | solution.py:238
  129.9 42.3 %collective-permute-start.17 = (bf16[256,1408]{1,0:T(8,128)(2,1)}, bf16[256,1408]{1,0:T(8,128)(2,1)}, u32[]{:S(2)}, u32[]{:S(2)}) collective-permute-start(bf16[256,1408]{1,0:T(8,128)(2,1)} %get-tuple-element.181), channel_id=1, source_target_pairs={{8,0},{16,8},{24,16},{28,24},{20,28},{12,20},{4,12},{0,4},{9,1},{1... | collective-permute-start | bytes 2162696 | tf_op jit(solution)/shard_map/ppermute | solution.py:241
  130.3 41.9 %collective-permute-start.18 = (bf16[256,1408]{1,0:T(8,128)(2,1)}, bf16[256,1408]{1,0:T(8,128)(2,1)}, u32[]{:S(2)}, u32[]{:S(2)}) collective-permute-start(bf16[256,1408]{1,0:T(8,128)(2,1)} %get-tuple-element.183), channel_id=1, source_target_pairs={{0,8},{8,16},{16,24},{24,28},{28,20},{20,12},{12,4},{4,0},{1,9},{9... | collective-permute-start | bytes 2162696 | tf_op jit(solution)/shard_map/ppermute | solution.py:238
  131.9 40.3 %collective-permute-start.19 = (bf16[256,1408]{1,0:T(8,128)(2,1)}, bf16[256,1408]{1,0:T(8,128)(2,1)}, u32[]{:S(2)}, u32[]{:S(2)}) collective-permute-start(bf16[256,1408]{1,0:T(8,128)(2,1)} %get-tuple-element.183), channel_id=1, source_target_pairs={{8,0},{16,8},{24,16},{28,24},{20,28},{12,20},{4,12},{0,4},{9,1},{1... | collective-permute-start | bytes 2162696 | tf_op jit(solution)/shard_map/ppermute | solution.py:241
  132.4 42.3 %collective-permute-start.20 = (bf16[1408,256]{1,0:T(8,128)(2,1)S(1)}, bf16[1408,256]{1,0:T(8,128)(2,1)}, u32[]{:S(2)}, u32[]{:S(2)}) collective-permute-start(bf16[1408,256]{1,0:T(8,128)(2,1)S(1)} %copy-done.30), channel_id=1, source_target_pairs={{0,8},{8,16},{16,24},{24,28},{28,20},{20,12},{12,4},{4,0},{1,9},{9... | collective-permute-start | bytes 2162696 | tf_op jit(solution)/shard_map/ppermute | solution.py:238
  175.9 91.2 %all-gather.7.cloned.1.call-start = ((), (), s32[]{:S(2)}) async-start(), calls=%async_computation.6 | async-start | bytes 5242880 | tf_op jit(solution)/shard_map/all_gather | solution.py:492
  181.3 41.3 %collective-permute-start.26 = (bf16[256,1408]{1,0:T(8,128)(2,1)}, bf16[256,1408]{1,0:T(8,128)(2,1)}, u32[]{:S(2)}, u32[]{:S(2)}) collective-permute-start(bf16[256,1408]{1,0:T(8,128)(2,1)} %collective-permute-done.18.left), channel_id=1, source_target_pairs={{0,8},{8,16},{16,24},{24,28},{28,20},{20,12},{12,4},{4,0},{1,9},{9... | collective-permute-start | bytes 2162696 | tf_op jit(solution)/shard_map/ppermute | solution.py:238
  183.0 39.5 %collective-permute-start.27 = (bf16[256,1408]{1,0:T(8,128)(2,1)}, bf16[256,1408]{1,0:T(8,128)(2,1)S(1)}, u32[]{:S(2)}, u32[]{:S(2)}) collective-permute-start(bf16[256,1408]{1,0:T(8,128)(2,1)} %collective-permute-done.19.right), channel_id=1, source_target_pairs={{8,0},{16,8},{24,16},{28,24},{20,28},{12,20},{4,12},{0,4},{9,1},{1... | collective-permute-start | bytes 2162696 | tf_op jit(solution)/shard_map/ppermute | solution.py:241
  226.4 70.6 %all-gather.9.cloned.1.call-start = ((), (), s32[]{:S(2)}) async-start(), calls=%async_computation.7 | async-start | bytes 5242880 | tf_op jit(solution)/shard_map/all_gather | solution.py:492
  227.0 211.8 %reduce-scatter.7.cloned.1.call-start = ((), (), s32[]{:S(2)}) async-start(), calls=%async_computation.8 | async-start | bytes 5242880 | tf_op jit(solution)/shard_map/reduce_scatter | solution.py:496
  259.4 30.6 %collective-permute-start.34 = (bf16[1408,256]{1,0:T(8,128)(2,1)}, bf16[1408,256]{1,0:T(8,128)(2,1)}, u32[]{:S(2)}, u32[]{:S(2)}) collective-permute-start(bf16[1408,256]{1,0:T(8,128)(2,1)} %collective-permute-done.20.left), channel_id=1, source_target_pairs={{0,8},{8,16},{16,24},{24,28},{28,20},{20,12},{12,4},{4,0},{1,9},{9... | collective-permute-start | bytes 2162696 | tf_op jit(solution)/shard_map/ppermute | solution.py:238
  260.9 29.1 %collective-permute-start.35 = (bf16[1408,256]{1,0:T(8,128)(2,1)}, bf16[1408,256]{1,0:T(8,128)(2,1)}, u32[]{:S(2)}, u32[]{:S(2)}) collective-permute-start(bf16[1408,256]{1,0:T(8,128)(2,1)} %collective-permute-done.21.right), channel_id=1, source_target_pairs={{8,0},{16,8},{24,16},{28,24},{20,28},{12,20},{4,12},{0,4},{9,1},{1... | collective-permute-start | bytes 2162696 | tf_op jit(solution)/shard_map/ppermute | solution.py:241
  394.6 90.8 %all-gather.11.cloned.1.call-start = ((), (), s32[]{:S(2)}) async-start(), calls=%async_computation.9 | async-start | bytes 5242880 | tf_op jit(solution)/shard_map/all_gather | solution.py:492
  396.8 30.9 %collective-permute-start.48 = (bf16[256,2816]{1,0:T(8,128)(2,1)S(1)}, bf16[256,2816]{1,0:T(8,128)(2,1)S(1)}, u32[]{:S(2)}, u32[]{:S(2)}) collective-permute-start(bf16[256,2816]{1,0:T(8,128)(2,1)S(1)} %get-tuple-element.246), channel_id=1, source_target_pairs={{0,8},{8,16},{16,24},{24,28},{28,20},{20,12},{12,4},{4,0},{1,9},{9... | collective-permute-start | bytes 4325384 | tf_op jit(solution)/shard_map/ppermute | solution.py:238
  398.3 30.5 %collective-permute-start.49 = (bf16[256,2816]{1,0:T(8,128)(2,1)S(1)}, bf16[256,2816]{1,0:T(8,128)(2,1)S(1)}, u32[]{:S(2)}, u32[]{:S(2)}) collective-permute-start(bf16[256,2816]{1,0:T(8,128)(2,1)S(1)} %get-tuple-element.247), channel_id=1, source_target_pairs={{8,0},{16,8},{24,16},{28,24},{20,28},{12,20},{4,12},{0,4},{9,1},{1... | collective-permute-start | bytes 4325384 | tf_op jit(solution)/shard_map/ppermute | solution.py:241
  443.9 135.4 %reduce-scatter.11.cloned.1.call-start = ((), (), s32[]{:S(2)}) async-start(), calls=%async_computation.11 | async-start | bytes 5242880 | tf_op jit(solution)/shard_map/reduce_scatter | solution.py:496
  444.0 33.6 %collective-permute-start.50 = (bf16[256,2816]{1,0:T(8,128)(2,1)}, bf16[256,2816]{1,0:T(8,128)(2,1)S(1)}, u32[]{:S(2)}, u32[]{:S(2)}) collective-permute-start(bf16[256,2816]{1,0:T(8,128)(2,1)} %get-tuple-element.252), channel_id=1, source_target_pairs={{0,8},{8,16},{16,24},{24,28},{28,20},{20,12},{12,4},{4,0},{1,9},{9... | collective-permute-start | bytes 4325384 | tf_op jit(solution)/shard_map/ppermute | solution.py:238
  445.5 33.1 %collective-permute-start.51 = (bf16[256,2816]{1,0:T(8,128)(2,1)S(1)}, bf16[256,2816]{1,0:T(8,128)(2,1)}, u32[]{:S(2)}, u32[]{:S(2)}) collective-permute-start(bf16[256,2816]{1,0:T(8,128)(2,1)S(1)} %get-tuple-element.253), channel_id=1, source_target_pairs={{8,0},{16,8},{24,16},{28,24},{20,28},{12,20},{4,12},{0,4},{9,1},{1... | collective-permute-start | bytes 4325384 | tf_op jit(solution)/shard_map/ppermute | solution.py:241
  483.2 32.4 %collective-permute-start.52 = (bf16[256,2816]{1,0:T(8,128)(2,1)}, bf16[256,2816]{1,0:T(8,128)(2,1)}, u32[]{:S(2)}, u32[]{:S(2)}) collective-permute-start(bf16[256,2816]{1,0:T(8,128)(2,1)} %get-tuple-element.262), channel_id=1, source_target_pairs={{0,8},{8,16},{16,24},{24,28},{28,20},{20,12},{12,4},{4,0},{1,9},{9... | collective-permute-start | bytes 4325384 | tf_op jit(solution)/shard_map/ppermute | solution.py:238
  484.7 32.4 %collective-permute-start.53 = (bf16[256,2816]{1,0:T(8,128)(2,1)}, bf16[256,2816]{1,0:T(8,128)(2,1)}, u32[]{:S(2)}, u32[]{:S(2)}) collective-permute-start(bf16[256,2816]{1,0:T(8,128)(2,1)} %get-tuple-element.263), channel_id=1, source_target_pairs={{8,0},{16,8},{24,16},{28,24},{20,28},{12,20},{4,12},{0,4},{9,1},{1... | collective-permute-start | bytes 4325384 | tf_op jit(solution)/shard_map/ppermute | solution.py:241
  531.0 90.4 %reduce-scatter.9.cloned.1.call-start = ((), (), s32[]{:S(2)}) async-start(), calls=%async_computation.10 | async-start | bytes 5242880 | tf_op jit(solution)/shard_map/reduce_scatter | solution.py:496
  (122 other events, 1458.9 us)
Sparse Core Ops, SparseCore 0:
  9.6 37.1 all-gather.4
  176.1 44.9 reduce-scatter.4
  226.5 34.4 all-gather.6
  262.5 34.4 all-gather.8
  394.7 44.0 reduce-scatter.6
  444.0 34.4 all-gather.10
  531.1 42.9 reduce-scatter.10
  576.8 44.5 reduce-scatter.8
